TPU v7x, 128 devices: a whole 4x4x4 slice. The times are simulated.
128 devices in a mesh: flow: 8 (over x, core), cross: 16 (over y, z).
Axes of the slice: x: 4, y: 4, z: 4, core: 2. Of those that a mesh axis runs over, the one named last changes fastest.
Arguments:
- matrix_start: float32 [32, 128, 512], P('flow', 'cross'), may hold values from -6 to 6
- storage: float32 [32, 128, 512], P('flow', 'cross'), may hold values from 0.1 to 1
- perm: float32 [32, 128, 512], P('flow', 'cross'), may hold values from 0.3 to 3
- frac_start: float32 [3072, 256], P(('flow', 'cross')), may hold values from -6 to 6
- frac_store: float32 [3072, 256], P(('flow', 'cross')), may hold values from 0.05 to 0.5
- frac_cond: float32 [3072, 256], P(('flow', 'cross')), may hold values from 2 to 20
- segment_ids: int32 [3072, 256], P(('flow', 'cross')), may hold values from 0 to 7, never falling along the last dimension, each value on 1 to 64 neighbouring positions
- block_counts: int32 [128], P(('flow', 'cross')), may hold values from 1 to 24, 1024 in all
- hit_tile: int32 [3072, 256, 1], P(('flow', 'cross')), may hold values from 0 to 127; in each aligned block of 6144 rows (0 to 6143, 6144 to 12287, ..., all dimensions but the last counted through in order) at most 72 rows name the same one
- hit_cell: int32 [3072, 256], P(('flow', 'cross')), may hold values from 0 to 16383
- hit_weight: float32 [3072, 256], P(('flow', 'cross')), may hold values from 1 to 8
Outputs:
- matrix_pressure: float32 [32, 128, 512], P('flow', 'cross')
- frac_pressure: float32 [3072, 256], P(('flow', 'cross'))
Inputs may be any that keep to these rules, and one draw needn't show every extreme that they name: `hit_tile`: in the 6144 rows of one owner, at most 72 fracture cells lie in one matrix tile, and in some owners exactly 72 do. Tile t is the one with flow index t // 16 and cross index t % 16. `block_counts`: the counts sum to 1024 and the largest is exactly 24. `segment_ids`: within a block the ids never fall, and each segment holds 1 to 64 cells.
All inputs are finite; a program needn't handle non-finite values.
Results may differ from a plain program's by a relative error of at most 0.0001.
Values sent between devices are 32-bit elements; how exact they have to be, the bound alone decides.
No kernel may reach another device: no remote copies, remote signals or barrier semaphores. Data moves between devices by JAX's collectives and lax.ppermute only.
A program may use at most 64 MiB of HBM per device.

v0:
```python
import jax
import jax.numpy as jnp
from jax import lax
from jax.sharding import PartitionSpec as P

SWEEPS = 4


def with_halo(block, sides, width):
    for axis, dim in sides:
        count = lax.axis_size(axis)
        forward = [(i, i + 1) for i in range(count - 1)]
        backward = [(target, source) for source, target in forward]
        low = lax.ppermute(
            lax.slice_in_dim(block, block.shape[dim] - width, None, axis=dim), axis, forward
        )
        high = lax.ppermute(lax.slice_in_dim(block, 0, width, axis=dim), axis, backward)
        block = jnp.concatenate([low, block, high], axis=dim)
    return block


def beside(padded):
    return [
        padded[:-2, 1:-1, 1:-1],
        padded[2:, 1:-1, 1:-1],
        padded[1:-1, :-2, 1:-1],
        padded[1:-1, 2:, 1:-1],
        padded[1:-1, 1:-1, :-2],
        padded[1:-1, 1:-1, 2:],
    ]


def transmit(centre, neighbours):
    return [2.0 * centre * neighbour / (centre + neighbour) for neighbour in neighbours]


def chain_links(frac_cond, segment_ids):
    linked = (segment_ids[:, :-1] == segment_ids[:, 1:]).astype(jnp.float32)
    zero_col = jnp.zeros_like(frac_cond[:, :1])
    link_right = jnp.concatenate([frac_cond[:, :-1] * linked, zero_col], axis=1)
    link_left = jnp.concatenate([zero_col, link_right[:, :-1]], axis=1)
    return (link_left, link_right)


def fracture_update(
    frac_now, frac_start, frac_store, link_left, link_right, weight_live, matrix_seen, live_mask
):
    zero_col = jnp.zeros_like(frac_now[:, :1])
    left_value = jnp.concatenate([zero_col, frac_now[:, :-1]], axis=1)
    right_value = jnp.concatenate([frac_now[:, 1:], zero_col], axis=1)
    numerator = (
        frac_store * frac_start
        + link_left * left_value
        + link_right * right_value
        + weight_live * matrix_seen
    )
    denominator = frac_store + link_left + link_right + weight_live
    return jnp.where(live_mask, numerator / denominator, frac_start)


def pad_depth(field):
    return jnp.pad(field, ((0, 0), (0, 0), (1, 1)))


def on_device(
    matrix_start,
    storage,
    perm,
    frac_start,
    frac_store,
    frac_cond,
    segment_ids,
    block_counts,
    hit_tile,
    hit_cell,
    hit_weight,
):
    n_flow = lax.axis_size("flow")
    n_cross = lax.axis_size("cross")
    devices = n_flow * n_cross
    blocks_here, cells_block = frac_start.shape
    row_count = blocks_here * cells_block
    capacity = 3 * row_count // (2 * devices)
    tile_shape = matrix_start.shape
    tile_cells = matrix_start.size
    rock_pad = pad_depth(with_halo(perm, (("flow", 0), ("cross", 1)), 1))
    conduct = transmit(perm, beside(rock_pad))
    cond_total = sum(conduct)
    live_mask = (jnp.arange(blocks_here, dtype=jnp.int32) < block_counts[0])[:, None]
    weight_live = jnp.where(live_mask, hit_weight, jnp.zeros_like(hit_weight))
    target = hit_tile.reshape(row_count)
    order_rows = jnp.argsort(target, stable=True)
    sorted_target = target[order_rows]
    per_target = jnp.zeros((devices,), jnp.int32).at[target].add(jnp.ones((row_count,), jnp.int32))
    first_slot = jnp.cumsum(per_target) - per_target
    group_start = first_slot[sorted_target]
    slot_sorted = sorted_target * capacity + jnp.arange(row_count, dtype=jnp.int32) - group_start
    row_of_slot = (
        jnp.full((devices * capacity,), row_count, jnp.int32).at[slot_sorted].set(order_rows)
    )
    slot_of_row = jnp.zeros((row_count,), jnp.int32).at[order_rows].set(slot_sorted)

    def pack_rows(values):
        padded_rows = jnp.concatenate([values.reshape(row_count), jnp.zeros((1,), jnp.float32)])
        return padded_rows[row_of_slot].reshape(devices, capacity)

    def deliver(payload):
        return lax.all_to_all(payload, ("flow", "cross"), split_axis=1, concat_axis=1, tiled=True)

    hit_lists = deliver(
        jnp.stack([pack_rows(hit_cell.astype(jnp.float32)), pack_rows(weight_live)])
    )
    recv_cell = hit_lists[0].astype(jnp.int32).reshape(-1)
    weight_sum = (
        jnp.zeros((tile_cells,), jnp.float32)
        .at[recv_cell]
        .add(hit_lists[1].reshape(-1))
        .reshape(tile_shape)
    )
    matrix_denom = storage + cond_total + weight_sum
    matrix_source = storage * matrix_start
    link_left, link_right = chain_links(frac_cond, segment_ids)
    matrix_now, frac_now = (matrix_start, frac_start)
    for sweep_no in range(SWEEPS):
        padded = pad_depth(with_halo(matrix_now, (("flow", 0), ("cross", 1)), 1))
        views = beside(padded)
        inflow = sum((face * view for face, view in zip(conduct, views)))
        outgoing = pack_rows(weight_live * frac_now)
        returning = matrix_now.reshape(-1)[recv_cell].reshape(devices, capacity)
        carried = deliver(jnp.stack([outgoing, returning]))
        transfer = (
            jnp.zeros((tile_cells,), jnp.float32)
            .at[recv_cell]
            .add(carried[0].reshape(-1))
            .reshape(tile_shape)
        )
        matrix_seen = carried[1].reshape(-1)[slot_of_row].reshape(blocks_here, cells_block)
        matrix_next = (matrix_source + inflow + transfer) / matrix_denom
        frac_now = fracture_update(
            frac_now,
            frac_start,
            frac_store,
            link_left,
            link_right,
            weight_live,
            matrix_seen,
            live_mask,
        )
        matrix_now = matrix_next
    return (matrix_now, frac_now)


def solution(mesh):
    in_specs = (
        P("flow", "cross", None),
        P("flow", "cross", None),
        P("flow", "cross", None),
        P(("flow", "cross"), None),
        P(("flow", "cross"), None),
        P(("flow", "cross"), None),
        P(("flow", "cross"), None),
        P(("flow", "cross")),
        P(("flow", "cross"), None, None),
        P(("flow", "cross"), None),
        P(("flow", "cross"), None),
    )
    out_specs = (P("flow", "cross", None), P(("flow", "cross"), None))
    return jax.shard_map(
        on_device, mesh=mesh, in_specs=in_specs, out_specs=out_specs, check_vma=False
    )
```

profile of v0, /device:TPU:1, one launch (start us, length us, event | category | flops | bytes accessed | tf_op | source)
XLA Modules:
  0.0 1223.3 jit_solution(11660480689613541074)
XLA Ops:
  1.4 6.7 sort.17
  8.1 34.3 %gather_fusion = s32[6144]{0:T(1024)S(1)} fusion(s32[6144]{0:T(1024)S(1)} %bitcast.38, s32[6144]{0:T(1024)S(1)} %get-tuple-element.56), kind=kCustom, calls=%fused_computation | custom fusion | bytes 73728 | tf_op jit(solution)/shard_map/gather | solution.py:93
  42.5 42.9 %scatter_custom_fusion = s32[128]{0:T(128)S(1)} fusion(s32[6144]{0:T(1024)S(1)} %bitcast.64, s32[6144]{0:T(1024)S(1)} %broadcast.147, s32[]{:T(128)} %constant.15.clone.1), kind=kCustom, calls=%fused_computation.220 | custom fusion | flops 6144 | bytes 516 | tf_op jit(solution)/shard_map/scatter-add | solution.py:94
  85.8 36.8 %gather_fusion.1 = s32[6144]{0:T(1024)S(1)} fusion(s32[128]{0:T(128)S(1)} %sub.15, s32[6144]{0:T(1024)S(1)} %broadcast_clamp_fusion.1), kind=kCustom, calls=%fused_computation.1 | custom fusion | bytes 73728 | tf_op jit(solution)/shard_map/gather | solution.py:96
  122.6 23.0 %scatter_custom_fusion.1 = s32[9216]{0:T(1024)S(1)} fusion(s32[6144]{0:T(1024)S(1)} %bitcast.65, s32[6144]{0:T(1024)S(1)} %get-tuple-element.3, s32[]{:T(128)} %constant.14.clone.1), kind=kCustom, calls=%fused_computation.197 | custom fusion | bytes 36868 | tf_op jit(solution)/shard_map/scatter | solution.py:99
  146.5 51.2 %gather_fusion.3 = f32[9216]{0:T(1024)S(1)} fusion(f32[6145]{0:T(1024)S(1)} %get-tuple-element.58, s32[9216]{0:T(1024)S(1)} %fusion.56), kind=kCustom, calls=%fused_computation.3 | custom fusion | bytes 110592 | tf_op jit(solution)/shard_map/gather | solution.py:105
  198.5 51.2 %gather_fusion.2 = f32[9216]{0:T(1024)S(1)} fusion(f32[6145]{0:T(1024)S(1)} %pad_maximum_fusion.10, s32[9216]{0:T(1024)S(1)} %fusion.56), kind=kCustom, calls=%fused_computation.2 | custom fusion | bytes 110592 | tf_op jit(solution)/shard_map/gather | solution.py:105
  250.5 11.5 all-to-all-start
  262.1 3.5 collective-permute-start
  265.6 1.9 collective-permute-start.2
  267.6 3.6 collective-permute-start.1
  271.2 1.9 collective-permute-start.3
  273.2 23.0 %scatter_custom_fusion.4 = s32[6144]{0:T(1024)S(1)} fusion(s32[6144]{0:T(1024)S(1)} %get-tuple-element.55, s32[6144]{0:T(1024)S(1)} %add_subtract_fusion, s32[]{:T(128)} %constant.15.clone.1), kind=kCustom, calls=%fused_computation.217 | custom fusion | bytes 24580 | tf_op jit(solution)/shard_map/scatter | solution.py:101
  296.4 51.2 %gather_fusion.4 = f32[9216]{0:T(1024)S(1)} fusion(f32[6145]{0:T(1024)S(1)} %get-tuple-element.57, s32[9216]{0:T(1024)S(1)} %fusion.56), kind=kCustom, calls=%fused_computation.4 | custom fusion | bytes 110592 | tf_op jit(solution)/shard_map/gather | solution.py:105
  347.7 3.2 collective-permute-start.4
  352.4 4.0 collective-permute-start.5
  357.9 2.9 collective-permute-done.7
  361.4 51.2 %gather_fusion.5 = f32[9216]{0:T(1024)S(1)} fusion(f32[16384]{0:T(1024)S(1)} %bitcast.40, s32[9216]{0:T(1024)S(1)} %broadcast_clamp_fusion), kind=kCustom, calls=%fused_computation.5 | custom fusion | bytes 110592 | tf_op jit(solution)/shard_map/gather | solution.py:129
  413.4 14.9 %all-to-all-start.1 = ((f32[2,128,72]{2,0,1:T(2,128)}), f32[2,128,72]{2,0,1:T(2,128)S(1)}, u32[]{:S(2)}, u32[]{:S(2)}) async-start(f32[2,128,72]{2,0,1:T(2,128)} %copy.17), calls=%async_computation.1 | async-start | bytes 262144 | tf_op jit(solution)/shard_map/all_to_all | solution.py:108
  428.6 48.7 %scatter_custom_fusion.3 = f32[16384]{0:T(1024)S(1)} fusion(s32[9216]{0:T(1024)S(1)} %bitcast.52, f32[9216]{0:T(1024)S(1)} %reshape.368, f32[]{:T(128)} %constant.12.clone.1), kind=kCustom, calls=%fused_computation.178 | custom fusion | flops 9216 | bytes 65540 | tf_op jit(solution)/shard_map/scatter-add | solution.py:117
  477.9 48.7 %scatter_custom_fusion.2 = f32[16384]{0:T(1024)S(1)} fusion(s32[9216]{0:T(1024)S(1)} %bitcast.53, f32[9216]{0:T(1024)S(1)} %reshape.360, f32[]{:T(128)} %constant.12.clone.1), kind=kCustom, calls=%fused_computation.180 | custom fusion | flops 9216 | bytes 65540 | tf_op jit(solution)/shard_map/scatter-add | solution.py:134
  527.6 51.2 %gather_fusion.8 = f32[9216]{0:T(1024)S(1)} fusion(f32[16384]{0:T(1024)S(1)} %bitcast.42, s32[9216]{0:T(1024)S(1)} %broadcast_clamp_fusion), kind=kCustom, calls=%fused_computation.8 | custom fusion | bytes 110592 | tf_op jit(solution)/shard_map/gather | solution.py:129
  579.0 34.3 %gather_fusion.6 = f32[6144]{0:T(1024)S(1)} fusion(f32[9216]{0:T(1024)S(1)} %reshape_squeeze.29, s32[6144]{0:T(1024)S(1)} %fusion.67), kind=kCustom, calls=%fused_computation.6 | custom fusion | bytes 73728 | tf_op jit(solution)/shard_map/gather | solution.py:137
  614.2 51.2 %gather_fusion.7 = f32[9216]{0:T(1024)S(1)} fusion(f32[6145]{0:T(1024)S(1)} %pad_maximum_fusion.7, s32[9216]{0:T(1024)S(1)} %fusion.56), kind=kCustom, calls=%fused_computation.7 | custom fusion | bytes 110592 | tf_op jit(solution)/shard_map/gather | solution.py:105
  665.4 3.4 collective-permute-start.8
  668.8 1.9 collective-permute-start.9
  671.5 23.1 %all-to-all-start.2 = ((f32[2,128,72]{2,0,1:T(2,128)}), f32[2,128,72]{2,0,1:T(2,128)S(1)}, u32[]{:S(2)}, u32[]{:S(2)}) async-start(f32[2,128,72]{2,0,1:T(2,128)} %copy.18), calls=%async_computation.2 | async-start | bytes 262144 | tf_op jit(solution)/shard_map/all_to_all | solution.py:108
  694.6 3.4 collective-permute-start.10
  699.4 3.4 collective-permute-done.11
  705.1 34.3 %gather_fusion.9 = f32[6144]{0:T(1024)S(1)} fusion(f32[9216]{0:T(1024)S(1)} %reshape_squeeze.31, s32[6144]{0:T(1024)S(1)} %fusion.67), kind=kCustom, calls=%fused_computation.9 | custom fusion | bytes 73728 | tf_op jit(solution)/shard_map/gather | solution.py:137
  739.5 51.2 %gather_fusion.10 = f32[9216]{0:T(1024)S(1)} fusion(f32[6145]{0:T(1024)S(1)} %pad_maximum_fusion.6, s32[9216]{0:T(1024)S(1)} %fusion.56), kind=kCustom, calls=%fused_computation.10 | custom fusion | bytes 110592 | tf_op jit(solution)/shard_map/gather | solution.py:105
  790.9 48.7 %scatter_custom_fusion.5 = f32[16384]{0:T(1024)S(1)} fusion(s32[9216]{0:T(1024)S(1)} %bitcast.54, f32[9216]{0:T(1024)S(1)} %reshape.384, f32[]{:T(128)} %constant.12.clone.1), kind=kCustom, calls=%fused_computation.176 | custom fusion | flops 9216 | bytes 65540 | tf_op jit(solution)/shard_map/scatter-add | solution.py:134
  839.8 51.2 %gather_fusion.11 = f32[9216]{0:T(1024)S(1)} fusion(f32[16384]{0:T(1024)S(1)} %bitcast.43, s32[9216]{0:T(1024)S(1)} %broadcast_clamp_fusion), kind=kCustom, calls=%fused_computation.11 | custom fusion | bytes 110592 | tf_op jit(solution)/shard_map/gather | solution.py:129
  891.0 2.8 collective-permute-start.12
  896.6 14.8 %all-to-all-start.3 = ((f32[2,128,72]{2,0,1:T(2,128)}), f32[2,128,72]{2,0,1:T(2,128)S(1)}, u32[]{:S(2)}, u32[]{:S(2)}) async-start(f32[2,128,72]{2,0,1:T(2,128)} %copy.19), calls=%async_computation.3 | async-start | bytes 262144 | tf_op jit(solution)/shard_map/all_to_all | solution.py:108
  911.4 3.4 collective-permute-start.14
  916.5 3.1 collective-permute-done.15
  921.9 34.3 %gather_fusion.12 = f32[6144]{0:T(1024)S(1)} fusion(f32[9216]{0:T(1024)S(1)} %reshape_squeeze.33, s32[6144]{0:T(1024)S(1)} %fusion.67), kind=kCustom, calls=%fused_computation.12 | custom fusion | bytes 73728 | tf_op jit(solution)/shard_map/gather | solution.py:137
  956.3 51.2 %gather_fusion.13 = f32[9216]{0:T(1024)S(1)} fusion(f32[6145]{0:T(1024)S(1)} %pad_maximum_fusion.5, s32[9216]{0:T(1024)S(1)} %fusion.56), kind=kCustom, calls=%fused_computation.13 | custom fusion | bytes 110592 | tf_op jit(solution)/shard_map/gather | solution.py:105
  1007.7 48.7 %scatter_custom_fusion.6 = f32[16384]{0:T(1024)S(1)} fusion(s32[9216]{0:T(1024)S(1)} %bitcast.55, f32[9216]{0:T(1024)S(1)} %reshape.392, f32[]{:T(128)} %constant.12.clone.1), kind=kCustom, calls=%fused_computation.174 | custom fusion | flops 9216 | bytes 65540 | tf_op jit(solution)/shard_map/scatter-add | solution.py:134
  1056.6 51.2 %gather_fusion.14 = f32[9216]{0:T(1024)S(1)} fusion(f32[16384]{0:T(1024)S(1)} %bitcast.41, s32[9216]{0:T(1024)S(1)} %broadcast_clamp_fusion), kind=kCustom, calls=%fused_computation.14 | custom fusion | bytes 110592 | tf_op jit(solution)/shard_map/gather | solution.py:129
  1107.9 2.8 collective-permute-start.16
  1110.7 1.9 collective-permute-start.17
  1113.4 14.8 %all-to-all-start.4 = ((f32[2,128,72]{2,0,1:T(2,128)}), f32[2,128,72]{2,0,1:T(2,128)S(1)}, u32[]{:S(2)}, u32[]{:S(2)}) async-start(f32[2,128,72]{2,0,1:T(2,128)} %copy.20), calls=%async_computation.4 | async-start | bytes 262144 | tf_op jit(solution)/shard_map/all_to_all | solution.py:108
  1128.3 3.4 collective-permute-start.18
  1133.1 3.4 collective-permute-done.19
  1138.7 34.3 %gather_fusion.15 = f32[6144]{0:T(1024)S(1)} fusion(f32[9216]{0:T(1024)S(1)} %reshape_squeeze.35, s32[6144]{0:T(1024)S(1)} %fusion.67), kind=kCustom, calls=%fused_computation.15 | custom fusion | bytes 73728 | tf_op jit(solution)/shard_map/gather | solution.py:137
  1173.1 48.7 %scatter_custom_fusion.7 = f32[16384]{0:T(1024)S(1)} fusion(s32[9216]{0:T(1024)S(1)} %bitcast.56, f32[9216]{0:T(1024)S(1)} %reshape.400, f32[]{:T(128)} %constant.12.clone.1), kind=kCustom, calls=%fused_computation.172 | custom fusion | flops 9216 | bytes 65540 | tf_op jit(solution)/shard_map/scatter-add | solution.py:134
  (160 shorter events, 28.6 us)
Async XLA Ops:
  0.6 0.7 copy-start
  145.6 0.7 copy-start.2
  145.7 0.7 copy-start.5
  197.7 0.7 copy-start.8
  250.5 11.5 copy-start.1
  250.5 110.5 %all-to-all-start = ((f32[2,128,72]{2,0,1:T(2,128)}), f32[2,128,72]{2,0,1:T(2,128)S(1)}, u32[]{:S(2)}, u32[]{:S(2)}) async-start(f32[2,128,72]{2,0,1:T(2,128)} %copy.16), calls=%async_computation | async-start | bytes 262144 | tf_op jit(solution)/shard_map/all_to_all | solution.py:108
  262.0 5.5 copy-start.4
  262.1 85.6 %collective-permute-start = (f32[1,8,512]{2,1,0:T(8,128)S(1)}, f32[1,8,512]{2,1,0:T(8,128)S(1)}, u32[]{:S(2)}, u32[]{:S(2)}) collective-permute-start(f32[1,8,512]{2,1,0:T(8,128)S(1)} %get-tuple-element.42), channel_id=1, source_target_pairs={{0,16},{16,32},{32,48},{48,64},{64,80},{80,96},{96,112},{1,17},{17... | collective-permute-start | bytes 49160 | tf_op jit(solution)/shard_map/ppermute | solution.py:14
  265.6 82.1 %collective-permute-start.2 = (f32[1,8,512]{2,1,0:T(8,128)S(1)}, f32[1,8,512]{2,1,0:T(8,128)S(1)}, u32[]{:S(2)}, u32[]{:S(2)}) collective-permute-start(f32[1,8,512]{2,1,0:T(8,128)S(1)} %get-tuple-element.41), channel_id=1, source_target_pairs={{16,0},{32,16},{48,32},{64,48},{80,64},{96,80},{112,96},{17,1},{33... | collective-permute-start | bytes 49160 | tf_op jit(solution)/shard_map/ppermute | solution.py:17
  267.6 84.7 %collective-permute-start.1 = (f32[1,8,512]{2,1,0:T(8,128)S(1)}, f32[1,8,512]{2,1,0:T(8,128)S(1)}, u32[]{:S(2)}, u32[]{:S(2)}) collective-permute-start(f32[1,8,512]{2,1,0:T(8,128)S(1)} %get-tuple-element.44), channel_id=1, source_target_pairs={{0,16},{16,32},{32,48},{48,64},{64,80},{80,96},{96,112},{1,17},{17... | collective-permute-start | bytes 49160 | tf_op jit(solution)/shard_map/ppermute | solution.py:14
  271.2 81.1 %collective-permute-start.3 = (f32[1,8,512]{2,1,0:T(8,128)S(1)}, f32[1,8,512]{2,1,0:T(8,128)S(1)}, u32[]{:S(2)}, u32[]{:S(2)}) collective-permute-start(f32[1,8,512]{2,1,0:T(8,128)S(1)} %get-tuple-element.43), channel_id=1, source_target_pairs={{16,0},{32,16},{48,32},{64,48},{80,64},{96,80},{112,96},{17,1},{33... | collective-permute-start | bytes 49160 | tf_op jit(solution)/shard_map/ppermute | solution.py:17
  273.1 23.1 %copy-start.9 = (f32[24,256]{1,0:T(8,128)S(1)}, f32[24,256]{1,0:T(8,128)}, u32[]{:S(2)}) copy-start(f32[24,256]{1,0:T(8,128)} %param.16) | copy-start | bytes 73732
  273.2 23.0 %copy-start.7 = (s32[24,256]{1,0:T(8,128)S(1)}, s32[24,256]{1,0:T(8,128)}, u32[]{:S(2)}) copy-start(s32[24,256]{1,0:T(8,128)} %param.17) | copy-start | bytes 73732
  347.7 9.9 collective-permute-start.4
  351.0 6.7 collective-permute-start.6
  352.4 5.5 collective-permute-start.5
  356.4 4.4 collective-permute-start.7
  413.4 63.9 %all-to-all-start.1 = ((f32[2,128,72]{2,0,1:T(2,128)}), f32[2,128,72]{2,0,1:T(2,128)S(1)}, u32[]{:S(2)}, u32[]{:S(2)}) async-start(f32[2,128,72]{2,0,1:T(2,128)} %copy.17), calls=%async_computation.1 | async-start | bytes 262144 | tf_op jit(solution)/shard_map/all_to_all | solution.py:108
  526.6 0.8 copy-start.3
  613.3 0.7 copy-start.6
  665.4 29.1 %collective-permute-start.8 = (f32[1,8,512]{2,1,0:T(8,128)S(1)}, f32[1,8,512]{2,1,0:T(8,128)S(1)}, u32[]{:S(2)}, u32[]{:S(2)}) collective-permute-start(f32[1,8,512]{2,1,0:T(8,128)S(1)} %get-tuple-element.39), channel_id=1, source_target_pairs={{0,16},{16,32},{32,48},{48,64},{64,80},{80,96},{96,112},{1,17},{17... | collective-permute-start | bytes 49160 | tf_op jit(solution)/shard_map/ppermute | solution.py:14
  668.8 25.8 %collective-permute-start.9 = (f32[1,8,512]{2,1,0:T(8,128)S(1)}, f32[1,8,512]{2,1,0:T(8,128)S(1)}, u32[]{:S(2)}, u32[]{:S(2)}) collective-permute-start(f32[1,8,512]{2,1,0:T(8,128)S(1)} %get-tuple-element.40), channel_id=1, source_target_pairs={{16,0},{32,16},{48,32},{64,48},{80,64},{96,80},{112,96},{17,1},{33... | collective-permute-start | bytes 49160 | tf_op jit(solution)/shard_map/ppermute | solution.py:17
  671.5 33.1 %all-to-all-start.2 = ((f32[2,128,72]{2,0,1:T(2,128)}), f32[2,128,72]{2,0,1:T(2,128)S(1)}, u32[]{:S(2)}, u32[]{:S(2)}) async-start(f32[2,128,72]{2,0,1:T(2,128)} %copy.18), calls=%async_computation.2 | async-start | bytes 262144 | tf_op jit(solution)/shard_map/all_to_all | solution.py:108
  694.6 4.8 collective-permute-start.10
  698.0 4.7 collective-permute-start.11
  891.0 20.4 %collective-permute-start.12 = (f32[1,8,512]{2,1,0:T(8,128)S(1)}, f32[1,8,512]{2,1,0:T(8,128)S(1)}, u32[]{:S(2)}, u32[]{:S(2)}) collective-permute-start(f32[1,8,512]{2,1,0:T(8,128)S(1)} %get-tuple-element.37), channel_id=1, source_target_pairs={{0,16},{16,32},{32,48},{48,64},{64,80},{80,96},{96,112},{1,17},{17... | collective-permute-start | bytes 49160 | tf_op jit(solution)/shard_map/ppermute | solution.py:14
  893.9 17.6 %collective-permute-start.13 = (f32[1,8,512]{2,1,0:T(8,128)S(1)}, f32[1,8,512]{2,1,0:T(8,128)S(1)}, u32[]{:S(2)}, u32[]{:S(2)}) collective-permute-start(f32[1,8,512]{2,1,0:T(8,128)S(1)} %get-tuple-element.38), channel_id=1, source_target_pairs={{16,0},{32,16},{48,32},{64,48},{80,64},{96,80},{112,96},{17,1},{33... | collective-permute-start | bytes 49160 | tf_op jit(solution)/shard_map/ppermute | solution.py:17
  896.6 24.9 %all-to-all-start.3 = ((f32[2,128,72]{2,0,1:T(2,128)}), f32[2,128,72]{2,0,1:T(2,128)S(1)}, u32[]{:S(2)}, u32[]{:S(2)}) async-start(f32[2,128,72]{2,0,1:T(2,128)} %copy.19), calls=%async_computation.3 | async-start | bytes 262144 | tf_op jit(solution)/shard_map/all_to_all | solution.py:108
  911.4 5.0 collective-permute-start.14
  914.9 4.7 collective-permute-start.15
  1107.9 20.4 %collective-permute-start.16 = (f32[1,8,512]{2,1,0:T(8,128)S(1)}, f32[1,8,512]{2,1,0:T(8,128)S(1)}, u32[]{:S(2)}, u32[]{:S(2)}) collective-permute-start(f32[1,8,512]{2,1,0:T(8,128)S(1)} %get-tuple-element.35), channel_id=1, source_target_pairs={{0,16},{16,32},{32,48},{48,64},{64,80},{80,96},{96,112},{1,17},{17... | collective-permute-start | bytes 49160 | tf_op jit(solution)/shard_map/ppermute | solution.py:14
  1110.7 17.6 %collective-permute-start.17 = (f32[1,8,512]{2,1,0:T(8,128)S(1)}, f32[1,8,512]{2,1,0:T(8,128)S(1)}, u32[]{:S(2)}, u32[]{:S(2)}) collective-permute-start(f32[1,8,512]{2,1,0:T(8,128)S(1)} %get-tuple-element.36), channel_id=1, source_target_pairs={{16,0},{32,16},{48,32},{64,48},{80,64},{96,80},{112,96},{17,1},{33... | collective-permute-start | bytes 49160 | tf_op jit(solution)/shard_map/ppermute | solution.py:17
  1113.4 24.9 %all-to-all-start.4 = ((f32[2,128,72]{2,0,1:T(2,128)}), f32[2,128,72]{2,0,1:T(2,128)S(1)}, u32[]{:S(2)}, u32[]{:S(2)}) async-start(f32[2,128,72]{2,0,1:T(2,128)} %copy.20), calls=%async_computation.4 | async-start | bytes 262144 | tf_op jit(solution)/shard_map/all_to_all | solution.py:108
  1128.3 4.8 collective-permute-start.18
  1131.7 4.7 collective-permute-start.19
where the time goes:
time: 1230 us; the launch traced here: 1220 us
  local copies, waits for them, and re-layouts  777 us (63%)
  other arithmetic  297 us (24%)
  starting transfers between devices  129 us (10%)
  waiting for transfers between devices  17.6 us (1%)
    gather x6, local copies, waits for them, and re-layouts, pack_rows(): return padded_rows[row_of_slot].reshape(devices, capacity)  307 us
    gather x4, local copies, waits for them, and re-layouts, on_device(): returning = matrix_now.reshape(-1)[recv_cell].reshape(devices, capacity)  205 us
    scatter-add x4, other arithmetic, on_device(): transfer = jnp.zeros((tile_cells,), jnp.float32).at[recv_cell].add(carrie...  195 us
    gather x4, local copies, waits for them, and re-layouts, on_device(): carried[1].reshape(-1)[slot_of_row].reshape(blocks_here, cells_block)  137 us
    all_to_all x5, starting transfers between devices, deliver(): lax.all_to_all(payload, ('flow', 'cross'), split_axis=1, concat_axis=1, t...  79.1 us
    scatter-add x1, other arithmetic, on_device(): weight_sum = jnp.zeros((tile_cells,), jnp.float32).at[recv_cell].add(hit_...  48.7 us
    scatter-add x1, other arithmetic, on_device(): jnp.zeros((devices,), jnp.int32).at[target]  42.9 us
    gather x1, local copies, waits for them, and re-layouts, on_device(): group_start = first_slot[sorted_target]  36.8 us
  transfers between devices with their start and end apart: 25, of which 7 were waited for; matrix products, arithmetic and copies ran while one was open for 10% of the time, Pallas kernels for 0%

commit v1 on v0

v1 whole, which is shorter than its diff:
```python
import functools

import jax
import jax.numpy as jnp
from jax import lax
from jax.experimental import pallas as pl
from jax.experimental.pallas import tpu as pltpu
from jax.sharding import PartitionSpec as P

F32 = jnp.float32
BF16 = jnp.bfloat16
I32 = jnp.int32

LANES = 256
HALF_RANKS = 36
PAD_RANKS = 40
ROWS = 64
VMEM_LIMIT = 48 * 1024 * 1024

NN = (((1,), (0,)), ((), ()))
NT = (((1,), (1,)), ((), ()))


def call(body, out_shape, n_in, scratch=(), smem=(), cost=1000000):
    in_specs = [
        pl.BlockSpec(memory_space=pltpu.SMEM if i in smem else pltpu.VMEM) for i in range(n_in)
    ]
    out_specs = jax.tree.map(lambda _: pl.BlockSpec(memory_space=pltpu.VMEM), out_shape)
    return pl.pallas_call(
        body,
        out_shape=out_shape,
        in_specs=in_specs,
        out_specs=out_specs,
        scratch_shapes=list(scratch),
        compiler_params=pltpu.CompilerParams(vmem_limit_bytes=VMEM_LIMIT),
        cost_estimate=pl.CostEstimate(flops=cost, bytes_accessed=cost, transcendentals=0),
    )


def shape(*dims, dtype=F32):
    return jax.ShapeDtypeStruct(dims, dtype)


def halves(value):
    high = value.astype(BF16)
    low = (value - high.astype(F32)).astype(BF16)
    return high, low


def one_hot(index_row, count):
    place = lax.broadcasted_iota(I32, (count, LANES), 0)
    return place == index_row


def as_bf16(mask):
    return jnp.where(mask, 1.0, 0.0).astype(BF16)


def shift_right(x):
    return pltpu.roll(x, 1, 1)


def shift_left(x):
    return pltpu.roll(x, LANES - 1, 1)


def store_slots(out_ref, by_slot, group, groups):
    rows = by_slot.shape[0]
    if rows < 128:
        by_slot = jnp.concatenate([by_slot, jnp.zeros((128 - rows, LANES), F32)], axis=0)
    turned = by_slot.T
    for part in range(2):
        out_ref[pl.ds(group * 2 + part, 128, stride=2 * groups), :] = turned[
            part * 128 : part * 128 + 128
        ]


def load_slots(in_ref, group, groups):
    parts = [in_ref[pl.ds(group * 2 + part, 128, stride=2 * groups), :] for part in range(2)]
    return jnp.concatenate(parts, axis=0).T


def owner_first(
    count_ref,
    start_ref,
    store_ref,
    cond_ref,
    seg_ref,
    tile_ref,
    cell_ref,
    weight_ref,
    out_ref,
    coef_ref,
    slot_ref,
    key_hot,
    spread,
    values,
):
    blocks = start_ref.shape[0]
    size = (blocks, LANES)
    live = lax.broadcasted_iota(I32, size, 0) < count_ref[0]
    lane = lax.broadcasted_iota(I32, size, 1)
    start = start_ref[...]
    store = store_ref[...]
    weight = jnp.where(live, weight_ref[...], 0.0)
    seg = seg_ref[...]
    linked = (seg == shift_left(seg)) & (lane < LANES - 1)
    right = jnp.where(linked, cond_ref[...], 0.0)
    left = shift_right(right)
    inverse = 1.0 / (store + left + right + weight)
    own = jnp.where(live, store * start * inverse, start)
    left = jnp.where(live, left * inverse, 0.0)
    right = jnp.where(live, right * inverse, 0.0)
    pull = weight * inverse
    coef_ref[0] = own
    coef_ref[1] = left
    coef_ref[2] = right
    coef_ref[3] = pull
    coef_ref[4] = weight
    partial = own + left * shift_right(start) + right * shift_left(start)
    values[0] = cell_ref[...].astype(F32)
    values[1] = weight
    values[2] = weight * start
    values[3] = weight * partial
    values[4] = weight * pull
    slot_ref[0] = jnp.where(live, tile_ref[...], -1)
    upper = as_bf16(
        lax.broadcasted_iota(I32, (LANES, LANES), 0) <= lax.broadcasted_iota(I32, (LANES, LANES), 1)
    )

    def step(b, seen_before):
        target = slot_ref[0, pl.ds(b, 1), :]
        hot = one_hot(target, 128)
        running = lax.dot_general(as_bf16(hot), upper, NN, preferred_element_type=F32) + seen_before
        rank = jnp.sum(jnp.where(hot, running, 0.0), axis=0, keepdims=True).astype(I32) - 1
        rank = jnp.maximum(rank, 0)
        key = jnp.where(target >= 0, target + (rank & 1) * 128, -1)
        rank_half = rank >> 1
        slot_ref[0, pl.ds(b, 1), :] = key
        slot_ref[1, pl.ds(b, 1), :] = rank_half
        key_hot[b] = as_bf16(one_hot(key, LANES))
        rank_hot = one_hot(rank_half, PAD_RANKS)
        rows = []
        for v in range(5):
            high, low = halves(values[v, pl.ds(b, 1), :])
            rows += [high.astype(F32), low.astype(F32)]
        spread[b] = jnp.concatenate(
            [jnp.where(rank_hot, row, 0.0) for row in rows], axis=0
        ).astype(BF16)
        return running[:, LANES - 1 :]

    lax.fori_loop(0, blocks, step, jnp.zeros((128, 1), F32))
    total = jnp.zeros((10 * PAD_RANKS, LANES), F32)
    for b in range(blocks):
        total += lax.dot_general(spread[b], key_hot[b], NT, preferred_element_type=F32)
    sums = [
        total[2 * v * PAD_RANKS : (2 * v + 1) * PAD_RANKS]
        + total[(2 * v + 1) * PAD_RANKS : (2 * v + 2) * PAD_RANKS]
        for v in range(5)
    ]
    store_slots(out_ref, jnp.concatenate(sums[:3], axis=0), 0, 2)
    store_slots(out_ref, jnp.concatenate(sums[3:], axis=0), 1, 2)


def unpack(recv_ref, slot_ref, key_hot, seen, blocks):
    turned = load_slots(recv_ref, 0, 1)
    turned = turned[: 2 * PAD_RANKS]
    high, low = halves(turned)
    table = jnp.concatenate([high.astype(F32), low.astype(F32)], axis=0).astype(BF16)

    def step(b, carry):
        hot = as_bf16(one_hot(slot_ref[0, pl.ds(b, 1), :], LANES))
        if key_hot is not None:
            key_hot[b] = hot
        found = lax.dot_general(table, hot, NN, preferred_element_type=F32)
        found = found[: 2 * PAD_RANKS] + found[2 * PAD_RANKS :]
        rank_hot = one_hot(slot_ref[1, pl.ds(b, 1), :], PAD_RANKS)
        for v in range(2):
            mine = jnp.where(rank_hot, found[v * PAD_RANKS : (v + 1) * PAD_RANKS], 0.0)
            seen[v, pl.ds(b, 1), :] = jnp.sum(mine, axis=0, keepdims=True)
        return carry

    lax.fori_loop(0, blocks, step, 0)


def owner_middle(
    recv_ref, start_ref, coef_ref, slot_ref, out_ref, partial_ref, key_hot, spread, seen, values
):
    blocks = start_ref.shape[0]
    unpack(recv_ref, slot_ref, key_hot, seen, blocks)
    own, left, right, pull, weight = [coef_ref[i] for i in range(5)]
    now = start_ref[...]
    for v in range(2):
        now = own + left * shift_right(now) + right * shift_left(now) + pull * seen[v]
    partial = own + left * shift_right(now) + right * shift_left(now)
    partial_ref[...] = partial
    values[0] = weight * now
    values[1] = weight * partial

    def step(b, carry):
        rank_hot = one_hot(slot_ref[1, pl.ds(b, 1), :], PAD_RANKS)
        rows = []
        for v in range(2):
            high, low = halves(values[v, pl.ds(b, 1), :])
            rows += [high.astype(F32), low.astype(F32)]
        spread[b] = jnp.concatenate(
            [jnp.where(rank_hot, row, 0.0) for row in rows], axis=0
        ).astype(BF16)
        return carry

    lax.fori_loop(0, blocks, step, 0)
    total = jnp.zeros((4 * PAD_RANKS, LANES), F32)
    for b in range(blocks):
        total += lax.dot_general(spread[b], key_hot[b], NT, preferred_element_type=F32)
    sums = [
        total[2 * v * PAD_RANKS : (2 * v + 1) * PAD_RANKS]
        + total[(2 * v + 1) * PAD_RANKS : (2 * v + 2) * PAD_RANKS]
        for v in range(2)
    ]
    store_slots(out_ref, jnp.concatenate(sums, axis=0), 0, 1)


def owner_last(recv_ref, coef_ref, slot_ref, partial_ref, out_ref, seen):
    blocks = partial_ref.shape[0]
    unpack(recv_ref, slot_ref, None, seen, blocks)
    own, left, right, pull = [coef_ref[i] for i in range(4)]
    now = partial_ref[...] + pull * seen[0]
    out_ref[...] = own + left * shift_right(now) + right * shift_left(now) + pull * seen[1]


def fold(field):
    return jnp.concatenate([field[:, :LANES], field[:, LANES:]], axis=0)


def unfold(rows):
    half = ROWS // 2
    return jnp.concatenate([rows[:half], rows[half:]], axis=1)


def gather_cells(fields, cell_ref, cell_hot, found_ref):
    parts = []
    for field in fields:
        high, low = halves(fold(field))
        parts += [high, low]
    table = jnp.concatenate([p.astype(F32) for p in parts], axis=0).astype(BF16)

    def step(r, carry):
        row_hot = one_hot(cell_ref[0, pl.ds(r, 1), :], ROWS)
        found = lax.dot_general(table, cell_hot[r], NN, preferred_element_type=F32)
        for v in range(len(fields)):
            both = found[2 * v * ROWS : (2 * v + 1) * ROWS] + found[(2 * v + 1) * ROWS : (2 * v + 2) * ROWS]
            found_ref[pl.ds(v * PAD_RANKS + r, 1), :] = jnp.sum(
                jnp.where(row_hot, both, 0.0), axis=0, keepdims=True
            )
        return carry

    lax.fori_loop(0, HALF_RANKS, step, 0)


def scatter_cells(values_ref, count, cell_ref, cell_hot, spread):
    def step(r, carry):
        row_hot = one_hot(cell_ref[0, pl.ds(r, 1), :], ROWS)
        cell_hot[r] = as_bf16(one_hot(cell_ref[1, pl.ds(r, 1), :], LANES))
        rows = []
        for v in range(count):
            high, low = halves(values_ref[v, pl.ds(r, 1), :])
            rows += [high.astype(F32), low.astype(F32)]
        spread[r] = jnp.concatenate(
            [jnp.where(row_hot, row, 0.0) for row in rows], axis=0
        ).astype(BF16)
        return carry

    lax.fori_loop(0, HALF_RANKS, step, 0)
    total = jnp.zeros((2 * count * ROWS, LANES), F32)
    for r in range(HALF_RANKS):
        total += lax.dot_general(spread[r], cell_hot[r], NT, preferred_element_type=F32)
    return [
        unfold(total[2 * v * ROWS : (2 * v + 1) * ROWS] + total[(2 * v + 1) * ROWS : (2 * v + 2) * ROWS])
        for v in range(count)
    ]


def neighbours(field, x_low, x_high, y_low, y_high, ny):
    rows, nz = field.shape
    nx = rows // ny
    west = jnp.concatenate([x_low, field[: rows - ny]], axis=0)
    east = jnp.concatenate([field[ny:], x_high], axis=0)
    place = lax.broadcasted_iota(I32, (rows, nz), 0) % ny
    wide_low = jnp.concatenate(
        [jnp.broadcast_to(y_low[i : i + 1], (ny, nz)) for i in range(nx)], axis=0
    )
    wide_high = jnp.concatenate(
        [jnp.broadcast_to(y_high[i : i + 1], (ny, nz)) for i in range(nx)], axis=0
    )
    south = jnp.where(place == 0, wide_low, pltpu.roll(field, 1, 0))
    north = jnp.where(place == ny - 1, wide_high, pltpu.roll(field, rows - 1, 0))
    below = pltpu.roll(field, 1, 1)
    above = pltpu.roll(field, nz - 1, 1)
    return west, east, south, north, below, above


def rock(edge_ref, perm_ref, start_ref, storage_ref, xl, xh, yl, yh, faces_ref, base_ref):
    rows, nz = perm_ref.shape
    ny = 8
    perm = perm_ref[...]
    start = start_ref[...]
    beside = neighbours(perm, xl[0], xh[0], yl[0], yh[0], ny)
    values = neighbours(start, xl[1], xh[1], yl[1], yh[1], ny)
    row = lax.broadcasted_iota(I32, (rows, nz), 0)
    lane = lax.broadcasted_iota(I32, (rows, nz), 1)
    closed = [
        (row < ny) & (edge_ref[0] == 0),
        (row >= rows - ny) & (edge_ref[1] == 0),
        (row % ny == 0) & (edge_ref[2] == 0),
        (row % ny == ny - 1) & (edge_ref[3] == 0),
        lane == 0,
        lane == nz - 1,
    ]
    storage = storage_ref[...]
    base = storage * start
    inflow = jnp.zeros_like(start)
    total = storage
    for i in range(6):
        face = jnp.where(closed[i], 0.0, 2.0 * perm * beside[i] / (perm + beside[i]))
        faces_ref[i] = face
        total += face
        inflow += face * values[i]
    base_ref[0] = total
    base_ref[1] = base
    base_ref[2] = base + inflow


def tile_first(recv_ref, start_ref, base_ref, out_ref, next_ref, sums_ref, cells_ref,
               cell_hot, spread, values, found):
    first = load_slots(recv_ref, 0, 2)
    second = load_slots(recv_ref, 1, 2)
    cell = first[:PAD_RANKS].astype(I32)
    deep = cell & 511
    cells_ref[0] = ((deep >> 8) << 5) + (cell >> 9)
    cells_ref[1] = deep & (LANES - 1)
    values[0] = first[PAD_RANKS : 2 * PAD_RANKS]
    values[1] = first[2 * PAD_RANKS : 3 * PAD_RANKS]
    values[2] = second[:PAD_RANKS]
    values[3] = second[PAD_RANKS : 2 * PAD_RANKS]
    weight, pushed, partial, pull = scatter_cells(values, 4, cells_ref, cell_hot, spread)
    start = start_ref[...]
    inverse = 1.0 / (base_ref[0] + weight)
    now = (base_ref[2] + pushed) * inverse
    next_ref[...] = now
    sums_ref[0] = inverse
    sums_ref[1] = base_ref[1] + partial + start * pull
    sums_ref[2] = pull
    found[...] = jnp.zeros_like(found)
    gather_cells([start, now], cells_ref, cell_hot, found)
    store_slots(out_ref, found[...], 0, 1)


def flow_in(field, faces_ref, xl, xh, yl, yh):
    around = neighbours(field, xl[...], xh[...], yl[...], yh[...], 8)
    total = faces_ref[0] * around[0]
    for i in range(1, 6):
        total += faces_ref[i] * around[i]
    return total


def tile_second(now_ref, sums_ref, faces_ref, xl, xh, yl, yh, next_ref):
    inflow = flow_in(now_ref[...], faces_ref, xl, xh, yl, yh)
    next_ref[...] = (sums_ref[1] + inflow) * sums_ref[0]


def tile_third(recv_ref, now_ref, sums_ref, base_ref, faces_ref, cells_ref, xl, xh, yl, yh,
               out_ref, next_ref, last_ref, cell_hot, spread, values, found):
    turned = load_slots(recv_ref, 0, 1)
    values[0] = turned[:PAD_RANKS]
    values[1] = turned[PAD_RANKS : 2 * PAD_RANKS]
    pushed, partial = scatter_cells(values, 2, cells_ref, cell_hot, spread)
    now = now_ref[...]
    inflow = flow_in(now, faces_ref, xl, xh, yl, yh)
    later = (base_ref[1] + inflow + pushed) * sums_ref[0]
    next_ref[...] = later
    last_ref[...] = base_ref[1] + partial + now * sums_ref[2]
    found[...] = jnp.zeros_like(found)
    gather_cells([now, later], cells_ref, cell_hot, found)
    store_slots(out_ref, found[...], 0, 1)


def tile_last(now_ref, last_ref, sums_ref, faces_ref, xl, xh, yl, yh, out_ref):
    inflow = flow_in(now_ref[...], faces_ref, xl, xh, yl, yh)
    out_ref[...] = (last_ref[...] + inflow) * sums_ref[0]


def ring(block, axis, step):
    count = lax.axis_size(axis)
    return lax.ppermute(block, axis, [(i, (i + step) % count) for i in range(count)])


def halo(field):
    return (
        ring(field[..., -1, :, :], "flow", 1),
        ring(field[..., 0, :, :], "flow", -1),
        ring(field[..., :, -1, :], "cross", 1),
        ring(field[..., :, 0, :], "cross", -1),
    )


def deliver(payload):
    return lax.all_to_all(payload, ("flow", "cross"), split_axis=0, concat_axis=0, tiled=True)


def on_device(
    matrix_start,
    storage,
    perm,
    frac_start,
    frac_store,
    frac_cond,
    segment_ids,
    block_counts,
    hit_tile,
    hit_cell,
    hit_weight,
):
    n_flow = lax.axis_size("flow")
    n_cross = lax.axis_size("cross")
    i_flow = lax.axis_index("flow")
    i_cross = lax.axis_index("cross")
    blocks = frac_start.shape[0]
    nx, ny, nz = matrix_start.shape
    rows = nx * ny
    flat = lambda a: a.reshape(rows, nz)
    cube = lambda a: a.reshape(nx, ny, nz)

    hits, coef, slots = call(
        owner_first,
        (shape(512, 128), shape(5, blocks, LANES), shape(2, blocks, LANES, dtype=I32)),
        8,
        scratch=[
            pltpu.VMEM((blocks, LANES, LANES), BF16),
            pltpu.VMEM((blocks, 10 * PAD_RANKS, LANES), BF16),
            pltpu.VMEM((5, blocks, LANES), F32),
        ],
        smem=(0,),
    )(
        block_counts,
        frac_start,
        frac_store,
        frac_cond,
        segment_ids,
        hit_tile.reshape(blocks, LANES),
        hit_cell,
        hit_weight,
    )
    hits = deliver(hits)
    around = halo(jnp.stack([perm, matrix_start]))
    edges = jnp.stack(
        [i_flow, n_flow - 1 - i_flow, i_cross, n_cross - 1 - i_cross]
    ).astype(I32)
    start = flat(matrix_start)
    faces, base = call(
        rock, (shape(6, rows, nz), shape(3, rows, nz)), 8, smem=(0,)
    )(edges, flat(perm), start, flat(storage), *around)

    tile_scratch = lambda count: [
        pltpu.VMEM((HALF_RANKS, LANES, LANES), BF16),
        pltpu.VMEM((HALF_RANKS, 2 * count * ROWS, LANES), BF16),
        pltpu.VMEM((count, PAD_RANKS, LANES), F32),
        pltpu.VMEM((2 * PAD_RANKS, LANES), F32),
    ]
    seen, first, sums, cells = call(
        tile_first,
        (
            shape(256, 128),
            shape(rows, nz),
            shape(3, rows, nz),
            shape(2, PAD_RANKS, LANES, dtype=I32),
        ),
        3,
        scratch=tile_scratch(4),
    )(hits, start, base)
    seen = deliver(seen)
    second = call(tile_second, shape(rows, nz), 7)(first, sums, faces, *halo(cube(first)))

    pushed, partial = call(
        owner_middle,
        (shape(256, 128), shape(blocks, LANES)),
        4,
        scratch=[
            pltpu.VMEM((blocks, LANES, LANES), BF16),
            pltpu.VMEM((blocks, 4 * PAD_RANKS, LANES), BF16),
            pltpu.VMEM((2, blocks, LANES), F32),
            pltpu.VMEM((2, blocks, LANES), F32),
        ],
    )(seen, frac_start, coef, slots)
    pushed = deliver(pushed)

    seen, third, last = call(
        tile_third,
        (shape(256, 128), shape(rows, nz), shape(rows, nz)),
        10,
        scratch=tile_scratch(2),
    )(pushed, second, sums, base, faces, cells, *halo(cube(second)))
    seen = deliver(seen)
    fourth = call(tile_last, shape(rows, nz), 8)(third, last, sums, faces, *halo(cube(third)))
    frac = call(
        owner_last,
        shape(blocks, LANES),
        4,
        scratch=[pltpu.VMEM((2, blocks, LANES), F32)],
    )(seen, coef, slots, partial)
    return cube(fourth), frac


def solution(mesh):
    grid = P("flow", "cross", None)
    owner = P(("flow", "cross"), None)
    in_specs = (grid,) * 3 + (owner,) * 4 + (P(("flow", "cross")), P(("flow", "cross"), None, None), owner, owner)
    return jax.shard_map(
        on_device, mesh=mesh, in_specs=in_specs, out_specs=(grid, owner), check_vma=False
    )
```

time: 1230 us -> 129 us (0.10)
  local copies, waits for them, and re-layouts: 777 us -> 3.93 us
  other arithmetic: 297 us -> 0.14 us
  starting transfers between devices: 129 us -> 57.3 us
  Pallas kernels: 0 us -> 47.8 us
    gather x16 -> x0, local copies, waits for them, and re-layouts: 720 us -> none  [the longest x6 307 us: pack_rows(): return padded_rows[row_of_slot].reshape(devices, capacity)]
    scatter-add x6 -> x0, other arithmetic: 286 us -> none  [the longest x4 195 us: on_device(): transfer = jnp.zeros((tile_cells,), jnp.float32).at[recv_cell].add(carrie...]
    all_to_all x5 -> x4, starting transfers between devices: 79.1 us -> 27.2 us  [deliver(): lax.all_to_all(payload, ('flow', 'cross'), split_axis=0, concat_axis=0, t...]
    pallas_call x0 -> x8, Pallas kernels: none -> 47.8 us  [the longest x1 13.3 us: on_device(): call(tile_first, (shape(256, 128), shape(rows, nz), shape(3, rows, nz), s...]
    scatter x2 -> x0, local copies, waits for them, and re-layouts: 46 us -> none  [the longest x1 23 us: on_device(): jnp.zeros((row_count,), jnp.int32).at[order_rows].set(slot_sorted)]
    ppermute x20 -> x16, starting transfers between devices: 49.9 us -> 30.1 us  [ring(): lax.ppermute(block, axis, [(i, (i + step) % count) for i in range(count)])]
  transfers between devices with their start and end apart: 25 -> 20, of which waited for: 7 -> 8; matrix products, arithmetic and copies ran while one was open for 10% -> 0% of each run, Pallas kernels for 0% -> 7%
where the time goes in v1:
time: 129 us
  starting transfers between devices  57.3 us (44%)
  Pallas kernels  47.8 us (37%)
  waiting for transfers between devices  18 us (14%)
  local copies, waits for them, and re-layouts  3.93 us (3%)
  between operations  1.57 us (1%)
    ppermute x16, starting transfers between devices, ring(): lax.ppermute(block, axis, [(i, (i + step) % count) for i in range(count)])  30.1 us
    all_to_all x4, starting transfers between devices, deliver(): lax.all_to_all(payload, ('flow', 'cross'), split_axis=0, concat_axis=0, t...  27.2 us
    pallas_call x1, Pallas kernels, on_device(): call(tile_first, (shape(256, 128), shape(rows, nz), shape(3, rows, nz), s...  13.3 us
    pallas_call x1, Pallas kernels, on_device(): call(tile_third, (shape(256, 128), shape(rows, nz), shape(rows, nz)), 10,...  11.5 us
    all_to_all x4, waiting for transfers between devices, deliver(): lax.all_to_all(payload, ('flow', 'cross'), split_axis=0, concat_axis=0, t...  11.4 us
    pallas_call x1, Pallas kernels, on_device(): call(owner_first, (shape(512, 128), shape(5, blocks, LANES), shape(2, blo...  8.7 us
    pallas_call x1, Pallas kernels, on_device(): call(owner_middle, (shape(256, 128), shape(blocks, LANES)), 4, scratch=[p...  7.36 us
    ppermute x16, waiting for transfers between devices, ring(): lax.ppermute(block, axis, [(i, (i + step) % count) for i in range(count)])  6.62 us
  transfers between devices with their start and end apart: 20, of which 8 were waited for; matrix products, arithmetic and copies ran while one was open for 0% of the time, Pallas kernels for 7%

profile of v1, /device:TPU:1, one launch (start us, length us, event | category | flops | bytes accessed | tf_op | source)
XLA Modules:
  0.0 128.7 jit_solution(9708697215536062133)
XLA Ops:
  1.3 0.8 copy.49
  2.1 0.7 copy-done.5
  2.8 0.7 copy-done.6
  3.5 0.7 copy-done.7
  4.3 0.7 copy-done.8
  5.0 8.7 %shard_map.122 = (f32[512,128]{1,0:T(8,128)}, f32[5,24,256]{2,1,0:T(8,128)S(1)}, s32[2,24,256]{2,1,0:T(8,128)S(1)}) custom-call(s32[1]{0:T(128)S(6)} %copy.56.count_ref, f32[24,256]{1,0:T(8,128)S(1)} %copy-done.2, f32[24,256]{1,0:T(8,128)S(1)} %copy-done.4, f32[24,256]{1,0:T(8,128)S(1)} %copy-done.5, s32[24,256]{1,0:T(8,128)S(1)} %copy-done.6, ...), custom_call_target="tpu_custom_call" | custom-call | flops 1000000 | bytes 1000000 | tf_op jit(solution)/shard_map/pallas_call | solution.py:433
  13.7 11.5 %all-to-all-start = ((f32[128,4,128]{2,1,0:T(4,128)}), f32[128,4,128]{2,1,0:T(4,128)S(1)}, u32[]{:S(2)}, u32[]{:S(2)}) async-start(f32[128,4,128]{2,1,0:T(4,128)} %bitcast), calls=%async_computation | async-start | bytes 524288 | tf_op jit(solution)/shard_map/all_to_all | solution.py:407
  25.2 0.1 copy_bitcast_fusion
  25.4 5.6 %collective-permute-start.3 = (f32[2,4,512]{2,1,0:T(4,128)S(1)}, f32[2,4,512]{2,1,0:T(4,128)S(1)}, u32[]{:S(2)}, u32[]{:S(2)}) collective-permute-start(f32[2,4,512]{2,1,0:T(4,128)S(1)} %get-tuple-element.30), channel_id=1, source_target_pairs={{0,15},{1,0},{2,1},{3,2},{4,3},{5,4},{6,5},{7,6},{8,7},{9,8},{10,9... | collective-permute-start | bytes 49160 | tf_op jit(solution)/shard_map/ppermute | solution.py:394
  31.0 0.1 fusion.1
  31.1 1.7 %collective-permute-start = (f32[2,8,512]{2,0,1:T(2,128)S(1)}, f32[2,8,512]{2,0,1:T(2,128)S(1)}, u32[]{:S(2)}, u32[]{:S(2)}) collective-permute-start(f32[2,8,512]{2,0,1:T(2,128)S(1)} %bitcast.67), channel_id=1, source_target_pairs={{0,16},{16,32},{32,48},{48,64},{64,80},{80,96},{96,112},{112,0},{1... | collective-permute-start | bytes 98312 | tf_op jit(solution)/shard_map/ppermute | solution.py:394
  32.8 0.0 collective-permute-start.1
  32.9 0.1 pad_add_fusion.edge_ref
  32.9 0.9 collective-permute-done
  33.9 2.6 %collective-permute-done.1 = f32[2,8,512]{2,0,1:T(2,128)S(1)} collective-permute-done((f32[2,8,512]{2,0,1:T(2,128)S(1)}, f32[2,8,512]{2,0,1:T(2,128)S(1)}, u32[]{:S(2)}, u32[]{:S(2)}) %collective-permute-start.1) | collective-permute-done | bytes 32800 | tf_op jit(solution)/shard_map/ppermute | solution.py:394
  36.5 0.0 collective-permute-done.3.yh
  36.5 0.4 collective-permute-done.2.yl
  36.9 0.7 shard_map.123
  37.6 13.3 %shard_map.124 = (f32[256,128]{1,0:T(8,128)}, f32[32,512]{1,0:T(8,128)S(1)}, f32[3,32,512]{2,1,0:T(8,128)S(1)}, s32[2,40,256]{2,1,0:T(8,128)S(1)}) custom-call(f32[512,128]{1,0:T(8,128)S(1)} %bitcast.54, f32[32,512]{1,0:T(8,128)S(1)} %bitcast.56, f32[3,32,512]{2,1,0:T(8,128)S(1)} %get-tuple-element.17.base_ref), custom_call_target="tpu_custom_call" | custom-call | flops 1000000 | bytes 1000000 | tf_op jit(solution)/shard_map/pallas_call | solution.py:469
  51.0 1.8 %collective-permute-start.5 = (f32[8,512]{1,0:T(8,128)S(1)}, f32[8,512]{1,0:T(8,128)S(1)}, u32[]{:S(2)}, u32[]{:S(2)}) collective-permute-start(f32[8,512]{1,0:T(8,128)S(1)} %get-tuple-element.44), channel_id=1, source_target_pairs={{0,112},{16,0},{32,16},{48,32},{64,48},{80,64},{96,80},{112,96},{1... | collective-permute-start | bytes 49160 | tf_op jit(solution)/shard_map/ppermute | solution.py:394
  52.7 1.1 collective-permute-start.4
  53.9 0.1 collective-permute-start.6
  54.0 4.8 %collective-permute-start.7 = (f32[4,512]{1,0:T(4,128)S(1)}, f32[4,512]{1,0:T(4,128)S(1)}, u32[]{:S(2)}, u32[]{:S(2)}) collective-permute-start(f32[4,512]{1,0:T(4,128)S(1)} %bitcast.69), channel_id=1, source_target_pairs={{0,15},{1,0},{2,1},{3,2},{4,3},{5,4},{6,5},{7,6},{8,7},{9,8},{10,9... | collective-permute-start | bytes 24584 | tf_op jit(solution)/shard_map/ppermute | solution.py:394
  58.7 4.8 %all-to-all-start.1 = ((f32[128,2,128]{2,1,0:T(2,128)}), f32[128,2,128]{2,1,0:T(2,128)S(1)}, u32[]{:S(2)}, u32[]{:S(2)}) async-start(f32[128,2,128]{2,1,0:T(2,128)} %bitcast.13), calls=%async_computation.1 | async-start | bytes 262144 | tf_op jit(solution)/shard_map/all_to_all | solution.py:407
  63.6 0.0 collective-permute-done.6.yl
  63.6 0.0 collective-permute-done.7.yh
  63.6 0.0 collective-permute-done.4.xl
  63.6 0.1 shard_map.126.now_ref
  63.7 1.1 collective-permute-start.9
  64.8 0.7 collective-permute-start.8
  65.5 8.1 %all-to-all-done.1 = f32[128,2,128]{2,1,0:T(2,128)S(1)} async-done(((f32[128,2,128]{2,1,0:T(2,128)}), f32[128,2,128]{2,1,0:T(2,128)S(1)}, u32[]{:S(2)}, u32[]{:S(2)}) %all-to-all-start.1) | async-done | bytes 131104 | tf_op jit(solution)/shard_map/all_to_all | solution.py:407
  73.6 7.4 %shard_map.125 = (f32[256,128]{1,0:T(8,128)}, f32[24,256]{1,0:T(8,128)S(1)}) custom-call(f32[256,128]{1,0:T(8,128)S(1)} %bitcast.58, f32[24,256]{1,0:T(8,128)S(1)} %copy-done.2, f32[5,24,256]{2,1,0:T(8,128)S(1)} %get-tuple-element.19.coef_ref, s32[2,24,256]{2,1,0:T(8,128)S(1)} %get-tuple-element.20.slot_ref), custom_call_target="tpu_custom_call" | custom-call | flops 1000000 | bytes 1000000 | tf_op jit(solution)/shard_map/pallas_call | solution.py:483
  80.9 4.2 %all-to-all-start.2 = ((f32[128,2,128]{2,1,0:T(2,128)}), f32[128,2,128]{2,1,0:T(2,128)S(1)}, u32[]{:S(2)}, u32[]{:S(2)}) async-start(f32[128,2,128]{2,1,0:T(2,128)} %bitcast.15), calls=%async_computation.2 | async-start | bytes 262144 | tf_op jit(solution)/shard_map/all_to_all | solution.py:407
  85.2 1.6 %collective-permute-start.10 = (f32[4,512]{1,0:T(4,128)S(1)}, f32[4,512]{1,0:T(4,128)S(1)}, u32[]{:S(2)}, u32[]{:S(2)}) collective-permute-start(f32[4,512]{1,0:T(4,128)S(1)} %bitcast.73), channel_id=1, source_target_pairs={{0,1},{1,2},{2,3},{3,4},{4,5},{5,6},{6,7},{7,8},{8,9},{9,10},{10,1... | collective-permute-start | bytes 24584 | tf_op jit(solution)/shard_map/ppermute | solution.py:394
  86.7 4.1 %collective-permute-start.11 = (f32[4,512]{1,0:T(4,128)S(1)}, f32[4,512]{1,0:T(4,128)S(1)}, u32[]{:S(2)}, u32[]{:S(2)}) collective-permute-start(f32[4,512]{1,0:T(4,128)S(1)} %bitcast.70), channel_id=1, source_target_pairs={{0,15},{1,0},{2,1},{3,2},{4,3},{5,4},{6,5},{7,6},{8,7},{9,8},{10,9... | collective-permute-start | bytes 24584 | tf_op jit(solution)/shard_map/ppermute | solution.py:394
  90.9 1.4 %collective-permute-done.10.yl = f32[4,512]{1,0:T(4,128)S(1)} collective-permute-done((f32[4,512]{1,0:T(4,128)S(1)}, f32[4,512]{1,0:T(4,128)S(1)}, u32[]{:S(2)}, u32[]{:S(2)}) %collective-permute-start.10) | collective-permute-done | bytes 8224 | tf_op jit(solution)/shard_map/ppermute | solution.py:394
  92.3 0.0 collective-permute-done.11.yh
  92.3 2.9 %all-to-all-done.2 = f32[128,2,128]{2,1,0:T(2,128)S(1)} async-done(((f32[128,2,128]{2,1,0:T(2,128)}), f32[128,2,128]{2,1,0:T(2,128)S(1)}, u32[]{:S(2)}, u32[]{:S(2)}) %all-to-all-start.2) | async-done | bytes 131104 | tf_op jit(solution)/shard_map/all_to_all | solution.py:407
  95.1 11.5 %shard_map.127 = (f32[256,128]{1,0:T(8,128)}, f32[32,512]{1,0:T(8,128)S(1)}, f32[32,512]{1,0:T(8,128)S(1)}) custom-call(f32[256,128]{1,0:T(8,128)S(1)} %bitcast.57, f32[32,512]{1,0:T(8,128)S(1)} %shard_map.126.now_ref, f32[3,32,512]{2,1,0:T(8,128)S(1)} %get-tuple-element.23.sums_ref, f32[3,32,512]{2,1,0:T(8,128)S(1)} %get-tuple-element.17.base_ref, ...), custom_call_target="tpu_custom_call" | custom-call | flops 1000000 | bytes 1000000 | tf_op jit(solution)/shard_map/pallas_call | solution.py:496
  106.6 6.7 %all-to-all-start.3 = ((f32[128,2,128]{2,1,0:T(2,128)}), f32[128,2,128]{2,1,0:T(2,128)S(1)}, u32[]{:S(2)}, u32[]{:S(2)}) async-start(f32[128,2,128]{2,1,0:T(2,128)} %bitcast.27), calls=%async_computation.3 | async-start | bytes 262144 | tf_op jit(solution)/shard_map/all_to_all | solution.py:407
  113.3 1.1 collective-permute-start.13
  114.4 0.7 collective-permute-start.12
  115.1 1.6 %collective-permute-start.14 = (f32[4,512]{1,0:T(4,128)S(1)}, f32[4,512]{1,0:T(4,128)S(1)}, u32[]{:S(2)}, u32[]{:S(2)}) collective-permute-start(f32[4,512]{1,0:T(4,128)S(1)} %bitcast.74), channel_id=1, source_target_pairs={{0,1},{1,2},{2,3},{3,4},{4,5},{5,6},{6,7},{7,8},{8,9},{9,10},{10,1... | collective-permute-start | bytes 24584 | tf_op jit(solution)/shard_map/ppermute | solution.py:394
  116.7 4.1 %collective-permute-start.15 = (f32[4,512]{1,0:T(4,128)S(1)}, f32[4,512]{1,0:T(4,128)S(1)}, u32[]{:S(2)}, u32[]{:S(2)}) collective-permute-start(f32[4,512]{1,0:T(4,128)S(1)} %bitcast.71), channel_id=1, source_target_pairs={{0,15},{1,0},{2,1},{3,2},{4,3},{5,4},{6,5},{7,6},{8,7},{9,8},{10,9... | collective-permute-start | bytes 24584 | tf_op jit(solution)/shard_map/ppermute | solution.py:394
  120.8 1.3 %collective-permute-done.14.yl = f32[4,512]{1,0:T(4,128)S(1)} collective-permute-done((f32[4,512]{1,0:T(4,128)S(1)}, f32[4,512]{1,0:T(4,128)S(1)}, u32[]{:S(2)}, u32[]{:S(2)}) %collective-permute-start.14) | collective-permute-done | bytes 8224 | tf_op jit(solution)/shard_map/ppermute | solution.py:394
  122.1 0.7 shard_map.128
  122.9 0.4 all-to-all-done.3
  123.3 5.4 %shard_map.129 = f32[24,256]{1,0:T(8,128)} custom-call(f32[256,128]{1,0:T(8,128)S(1)} %bitcast.59, f32[5,24,256]{2,1,0:T(8,128)S(1)} %get-tuple-element.19.coef_ref, s32[2,24,256]{2,1,0:T(8,128)S(1)} %get-tuple-element.20.slot_ref, f32[24,256]{1,0:T(8,128)S(1)} %get-tuple-element.29.partial_ref), custom_call_target="tpu_custom_call" | custom-call | flops 1000000 | bytes 1000000 | tf_op jit(solution)/shard_map/pallas_call | solution.py:504
  (39 shorter events, 0.2 us)
Async XLA Ops:
  1.3 0.8 copy-start.2
  1.3 0.8 copy-start.4
  2.1 0.7 copy-start.5
  2.8 0.7 copy-start.6
  3.5 0.7 copy-start.7
  4.3 0.7 copy-start.8
  13.7 11.5 %copy-start = (f32[4,8,512]{2,1,0:T(8,128)S(1)}, f32[4,8,512]{2,1,0:T(8,128)}, u32[]{:S(2)}) copy-start(f32[4,8,512]{2,1,0:T(8,128)} %param.11) | copy-start | bytes 196612
  13.7 11.5 %copy-start.1 = (f32[4,8,512]{2,1,0:T(8,128)S(1)}, f32[4,8,512]{2,1,0:T(8,128)}, u32[]{:S(2)}) copy-start(f32[4,8,512]{2,1,0:T(8,128)} %param.13) | copy-start | bytes 196612
  13.7 23.9 %all-to-all-start = ((f32[128,4,128]{2,1,0:T(4,128)}), f32[128,4,128]{2,1,0:T(4,128)S(1)}, u32[]{:S(2)}, u32[]{:S(2)}) async-start(f32[128,4,128]{2,1,0:T(4,128)} %bitcast), calls=%async_computation | async-start | bytes 524288 | tf_op jit(solution)/shard_map/all_to_all | solution.py:407
  25.4 11.1 %collective-permute-start.3 = (f32[2,4,512]{2,1,0:T(4,128)S(1)}, f32[2,4,512]{2,1,0:T(4,128)S(1)}, u32[]{:S(2)}, u32[]{:S(2)}) collective-permute-start(f32[2,4,512]{2,1,0:T(4,128)S(1)} %get-tuple-element.30), channel_id=1, source_target_pairs={{0,15},{1,0},{2,1},{3,2},{4,3},{5,4},{6,5},{7,6},{8,7},{9,8},{10,9... | collective-permute-start | bytes 49160 | tf_op jit(solution)/shard_map/ppermute | solution.py:394
  31.0 5.9 %collective-permute-start.2 = (f32[2,4,512]{2,1,0:T(4,128)S(1)}, f32[2,4,512]{2,1,0:T(4,128)S(1)}, u32[]{:S(2)}, u32[]{:S(2)}) collective-permute-start(f32[2,4,512]{2,1,0:T(4,128)S(1)} %get-tuple-element.31), channel_id=1, source_target_pairs={{0,1},{1,2},{2,3},{3,4},{4,5},{5,6},{6,7},{7,8},{8,9},{9,10},{10,1... | collective-permute-start | bytes 49160 | tf_op jit(solution)/shard_map/ppermute | solution.py:394
  31.1 2.8 %collective-permute-start = (f32[2,8,512]{2,0,1:T(2,128)S(1)}, f32[2,8,512]{2,0,1:T(2,128)S(1)}, u32[]{:S(2)}, u32[]{:S(2)}) collective-permute-start(f32[2,8,512]{2,0,1:T(2,128)S(1)} %bitcast.67), channel_id=1, source_target_pairs={{0,16},{16,32},{32,48},{48,64},{64,80},{80,96},{96,112},{112,0},{1... | collective-permute-start | bytes 98312 | tf_op jit(solution)/shard_map/ppermute | solution.py:394
  32.8 3.6 %collective-permute-start.1 = (f32[2,8,512]{2,0,1:T(2,128)S(1)}, f32[2,8,512]{2,0,1:T(2,128)S(1)}, u32[]{:S(2)}, u32[]{:S(2)}) collective-permute-start(f32[2,8,512]{2,0,1:T(2,128)S(1)} %bitcast.68), channel_id=1, source_target_pairs={{0,112},{16,0},{32,16},{48,32},{64,48},{80,64},{96,80},{112,96},{1... | collective-permute-start | bytes 98312 | tf_op jit(solution)/shard_map/ppermute | solution.py:394
  32.9 4.0 %copy-start.3 = (f32[4,8,512]{2,1,0:T(8,128)S(1)}, f32[4,8,512]{2,1,0:T(8,128)}, u32[]{:S(2)}) copy-start(f32[4,8,512]{2,1,0:T(8,128)} %param.12) | copy-start | bytes 196612
  51.0 12.6 %collective-permute-start.5 = (f32[8,512]{1,0:T(8,128)S(1)}, f32[8,512]{1,0:T(8,128)S(1)}, u32[]{:S(2)}, u32[]{:S(2)}) collective-permute-start(f32[8,512]{1,0:T(8,128)S(1)} %get-tuple-element.44), channel_id=1, source_target_pairs={{0,112},{16,0},{32,16},{48,32},{64,48},{80,64},{96,80},{112,96},{1... | collective-permute-start | bytes 49160 | tf_op jit(solution)/shard_map/ppermute | solution.py:394
  52.7 10.8 %collective-permute-start.4 = (f32[8,512]{1,0:T(8,128)S(1)}, f32[8,512]{1,0:T(8,128)S(1)}, u32[]{:S(2)}, u32[]{:S(2)}) collective-permute-start(f32[8,512]{1,0:T(8,128)S(1)} %get-tuple-element.45), channel_id=1, source_target_pairs={{0,16},{16,32},{32,48},{48,64},{64,80},{80,96},{96,112},{112,0},{1... | collective-permute-start | bytes 49160 | tf_op jit(solution)/shard_map/ppermute | solution.py:394
  53.9 9.7 %collective-permute-start.6 = (f32[4,512]{1,0:T(4,128)S(1)}, f32[4,512]{1,0:T(4,128)S(1)}, u32[]{:S(2)}, u32[]{:S(2)}) collective-permute-start(f32[4,512]{1,0:T(4,128)S(1)} %bitcast.72), channel_id=1, source_target_pairs={{0,1},{1,2},{2,3},{3,4},{4,5},{5,6},{6,7},{7,8},{8,9},{9,10},{10,1... | collective-permute-start | bytes 24584 | tf_op jit(solution)/shard_map/ppermute | solution.py:394
  54.0 9.6 %collective-permute-start.7 = (f32[4,512]{1,0:T(4,128)S(1)}, f32[4,512]{1,0:T(4,128)S(1)}, u32[]{:S(2)}, u32[]{:S(2)}) collective-permute-start(f32[4,512]{1,0:T(4,128)S(1)} %bitcast.69), channel_id=1, source_target_pairs={{0,15},{1,0},{2,1},{3,2},{4,3},{5,4},{6,5},{7,6},{8,7},{9,8},{10,9... | collective-permute-start | bytes 24584 | tf_op jit(solution)/shard_map/ppermute | solution.py:394
  58.7 14.8 %all-to-all-start.1 = ((f32[128,2,128]{2,1,0:T(2,128)}), f32[128,2,128]{2,1,0:T(2,128)S(1)}, u32[]{:S(2)}, u32[]{:S(2)}) async-start(f32[128,2,128]{2,1,0:T(2,128)} %bitcast.13), calls=%async_computation.1 | async-start | bytes 262144 | tf_op jit(solution)/shard_map/all_to_all | solution.py:407
  63.7 28.5 %collective-permute-start.9 = (f32[8,512]{1,0:T(8,128)S(1)}, f32[8,512]{1,0:T(8,128)S(1)}, u32[]{:S(2)}, u32[]{:S(2)}) collective-permute-start(f32[8,512]{1,0:T(8,128)S(1)} %get-tuple-element.40), channel_id=1, source_target_pairs={{0,112},{16,0},{32,16},{48,32},{64,48},{80,64},{96,80},{112,96},{1... | collective-permute-start | bytes 49160 | tf_op jit(solution)/shard_map/ppermute | solution.py:394
  64.8 27.5 %collective-permute-start.8 = (f32[8,512]{1,0:T(8,128)S(1)}, f32[8,512]{1,0:T(8,128)S(1)}, u32[]{:S(2)}, u32[]{:S(2)}) collective-permute-start(f32[8,512]{1,0:T(8,128)S(1)} %get-tuple-element.41), channel_id=1, source_target_pairs={{0,16},{16,32},{32,48},{48,64},{64,80},{80,96},{96,112},{112,0},{1... | collective-permute-start | bytes 49160 | tf_op jit(solution)/shard_map/ppermute | solution.py:394
  80.9 14.2 %all-to-all-start.2 = ((f32[128,2,128]{2,1,0:T(2,128)}), f32[128,2,128]{2,1,0:T(2,128)S(1)}, u32[]{:S(2)}, u32[]{:S(2)}) async-start(f32[128,2,128]{2,1,0:T(2,128)} %bitcast.15), calls=%async_computation.2 | async-start | bytes 262144 | tf_op jit(solution)/shard_map/all_to_all | solution.py:407
  85.2 7.1 %collective-permute-start.10 = (f32[4,512]{1,0:T(4,128)S(1)}, f32[4,512]{1,0:T(4,128)S(1)}, u32[]{:S(2)}, u32[]{:S(2)}) collective-permute-start(f32[4,512]{1,0:T(4,128)S(1)} %bitcast.73), channel_id=1, source_target_pairs={{0,1},{1,2},{2,3},{3,4},{4,5},{5,6},{6,7},{7,8},{8,9},{9,10},{10,1... | collective-permute-start | bytes 24584 | tf_op jit(solution)/shard_map/ppermute | solution.py:394
  86.7 5.5 %collective-permute-start.11 = (f32[4,512]{1,0:T(4,128)S(1)}, f32[4,512]{1,0:T(4,128)S(1)}, u32[]{:S(2)}, u32[]{:S(2)}) collective-permute-start(f32[4,512]{1,0:T(4,128)S(1)} %bitcast.70), channel_id=1, source_target_pairs={{0,15},{1,0},{2,1},{3,2},{4,3},{5,4},{6,5},{7,6},{8,7},{9,8},{10,9... | collective-permute-start | bytes 24584 | tf_op jit(solution)/shard_map/ppermute | solution.py:394
  106.6 16.7 %all-to-all-start.3 = ((f32[128,2,128]{2,1,0:T(2,128)}), f32[128,2,128]{2,1,0:T(2,128)S(1)}, u32[]{:S(2)}, u32[]{:S(2)}) async-start(f32[128,2,128]{2,1,0:T(2,128)} %bitcast.27), calls=%async_computation.3 | async-start | bytes 262144 | tf_op jit(solution)/shard_map/all_to_all | solution.py:407
  113.3 8.8 %collective-permute-start.13 = (f32[8,512]{1,0:T(8,128)S(1)}, f32[8,512]{1,0:T(8,128)S(1)}, u32[]{:S(2)}, u32[]{:S(2)}) collective-permute-start(f32[8,512]{1,0:T(8,128)S(1)} %get-tuple-element.36), channel_id=1, source_target_pairs={{0,112},{16,0},{32,16},{48,32},{64,48},{80,64},{96,80},{112,96},{1... | collective-permute-start | bytes 49160 | tf_op jit(solution)/shard_map/ppermute | solution.py:394
  114.4 7.7 %collective-permute-start.12 = (f32[8,512]{1,0:T(8,128)S(1)}, f32[8,512]{1,0:T(8,128)S(1)}, u32[]{:S(2)}, u32[]{:S(2)}) collective-permute-start(f32[8,512]{1,0:T(8,128)S(1)} %get-tuple-element.37), channel_id=1, source_target_pairs={{0,16},{16,32},{32,48},{48,64},{64,80},{80,96},{96,112},{112,0},{1... | collective-permute-start | bytes 49160 | tf_op jit(solution)/shard_map/ppermute | solution.py:394
  115.1 7.0 %collective-permute-start.14 = (f32[4,512]{1,0:T(4,128)S(1)}, f32[4,512]{1,0:T(4,128)S(1)}, u32[]{:S(2)}, u32[]{:S(2)}) collective-permute-start(f32[4,512]{1,0:T(4,128)S(1)} %bitcast.74), channel_id=1, source_target_pairs={{0,1},{1,2},{2,3},{3,4},{4,5},{5,6},{6,7},{7,8},{8,9},{9,10},{10,1... | collective-permute-start | bytes 24584 | tf_op jit(solution)/shard_map/ppermute | solution.py:394
  116.7 5.4 %collective-permute-start.15 = (f32[4,512]{1,0:T(4,128)S(1)}, f32[4,512]{1,0:T(4,128)S(1)}, u32[]{:S(2)}, u32[]{:S(2)}) collective-permute-start(f32[4,512]{1,0:T(4,128)S(1)} %bitcast.71), channel_id=1, source_target_pairs={{0,15},{1,0},{2,1},{3,2},{4,3},{5,4},{6,5},{7,6},{8,7},{9,8},{10,9... | collective-permute-start | bytes 24584 | tf_op jit(solution)/shard_map/ppermute | solution.py:394

commit v2 on v1

v2 whole, which is shorter than its diff:
```python
import jax
import jax.numpy as jnp
from jax import lax
from jax.experimental import pallas as pl
from jax.experimental.pallas import tpu as pltpu
from jax.sharding import PartitionSpec as P

F32 = jnp.float32
BF16 = jnp.bfloat16
I32 = jnp.int32
I16 = jnp.int16

LANES = 256
HALF_RANKS = 36
PAD_RANKS = 40
ROWS = 64
VMEM_LIMIT = 40 * 1024 * 1024

NN = (((1,), (0,)), ((), ()))
NT = (((1,), (1,)), ((), ()))


def call(body, out_shape, n_in, scratch=(), smem=(), remote=(), microseconds=1):
    def place(i):
        if i in smem:
            return pltpu.SMEM
        return pl.ANY if i in remote else pltpu.VMEM

    out_specs = jax.tree.map(lambda _: pl.BlockSpec(memory_space=pltpu.VMEM), out_shape)
    return pl.pallas_call(
        body,
        out_shape=out_shape,
        in_specs=[pl.BlockSpec(memory_space=place(i)) for i in range(n_in)],
        out_specs=out_specs,
        scratch_shapes=list(scratch),
        compiler_params=pltpu.CompilerParams(vmem_limit_bytes=VMEM_LIMIT),
        cost_estimate=pl.CostEstimate(
            flops=0, bytes_accessed=int(microseconds * 3_000_000), transcendentals=0
        ),
    )


def shape(*dims, dtype=F32):
    return jax.ShapeDtypeStruct(dims, dtype)


def halves(value):
    high = value.astype(BF16).astype(F32)
    return high, value - high


def hot_rows(index_row, count):
    place = lax.broadcasted_iota(I16, (16, LANES), 0)
    index = jnp.broadcast_to(index_row, (16, LANES)).astype(I16)
    one, none = jnp.ones((16, LANES), BF16), jnp.zeros((16, LANES), BF16)
    return jnp.concatenate(
        [jnp.where(place == index - jnp.int16(16 * j), one, none) for j in range(count // 16)], axis=0
    )


def same(index_row, count):
    return lax.broadcasted_iota(I32, (count, LANES), 0) == index_row


def shift_right(x):
    return pltpu.roll(x, 1, 1)


def shift_left(x):
    return pltpu.roll(x, LANES - 1, 1)


def store_slots(out_ref, by_slot, group, groups):
    rows = by_slot.shape[0]
    if rows < 128:
        by_slot = jnp.concatenate([by_slot, jnp.zeros((128 - rows, LANES), F32)], axis=0)
    turned = by_slot.T
    for part in range(2):
        out_ref[pl.ds(group * 2 + part, 128, stride=2 * groups), :] = turned[
            part * 128 : part * 128 + 128
        ]


def load_slots(in_ref, group, groups):
    parts = [in_ref[pl.ds(group * 2 + part, 128, stride=2 * groups), :] for part in range(2)]
    return jnp.concatenate(parts, axis=0).T


def spread_ranks(split, b, rank_half):
    mine = same(rank_half, PAD_RANKS)
    rows = [jnp.where(mine, split[v, b : b + 1, :], 0.0) for v in range(split.shape[0])]
    return jnp.concatenate(rows, axis=0).astype(BF16)


def joined(total, height, count):
    return [
        total[2 * v * height : (2 * v + 1) * height] + total[(2 * v + 1) * height : (2 * v + 2) * height]
        for v in range(count)
    ]


def put_split(split, v, value):
    high, low = halves(value)
    split[2 * v] = high
    split[2 * v + 1] = low


def owner_first(
    count_ref, start_hbm, store_hbm, cond_hbm, seg_hbm, tile_hbm, cell_hbm, weight_hbm,
    out_ref, coef_ref, slot_ref,
    start_ref, store_ref, cond_ref, seg_ref, tile_ref, cell_ref, weight_ref, arrived, split,
):
    pairs = [
        (tile_hbm, tile_ref), (seg_hbm, seg_ref), (cond_hbm, cond_ref), (weight_hbm, weight_ref),
        (store_hbm, store_ref), (start_hbm, start_ref), (cell_hbm, cell_ref),
    ]
    copies = [pltpu.make_async_copy(a, b, arrived.at[i]) for i, (a, b) in enumerate(pairs)]
    for copy in copies:
        copy.start()
    for copy in copies:
        copy.wait()
    blocks = start_ref.shape[0]
    size = (blocks, LANES)
    live = lax.broadcasted_iota(I32, size, 0) < count_ref[0]
    lane = lax.broadcasted_iota(I32, size, 1)
    start = start_ref[...]
    store = store_ref[...]
    weight = jnp.where(live, weight_ref[...], 0.0)
    seg = seg_ref[...]
    linked = (seg == shift_left(seg)) & (lane < LANES - 1)
    right = jnp.where(linked, cond_ref[...], 0.0)
    left = shift_right(right)
    inverse = 1.0 / (store + left + right + weight)
    own = jnp.where(live, store * start * inverse, start)
    left = jnp.where(live, left * inverse, 0.0)
    right = jnp.where(live, right * inverse, 0.0)
    pull = weight * inverse
    coef_ref[0] = own
    coef_ref[1] = left
    coef_ref[2] = right
    coef_ref[3] = pull
    coef_ref[4] = weight
    partial = own + left * shift_right(start) + right * shift_left(start)
    put_split(split, 0, cell_ref[...].astype(F32))
    put_split(split, 1, weight)
    put_split(split, 2, weight * start)
    put_split(split, 3, weight * partial)
    put_split(split, 4, weight * pull)
    tile = jnp.concatenate(
        [tile_ref[pl.ds(0, blocks, stride=2), :], tile_ref[pl.ds(1, blocks, stride=2), :]], axis=1
    )
    slot_ref[0] = jnp.where(live, tile, -1)
    upper = jnp.where(
        lax.broadcasted_iota(I32, (LANES, LANES), 0) <= lax.broadcasted_iota(I32, (LANES, LANES), 1),
        1.0, 0.0,
    ).astype(BF16)
    before = jnp.zeros((128, LANES), F32)
    total = jnp.zeros((10 * PAD_RANKS, LANES), F32)
    for b in range(blocks):
        target = slot_ref[0, b : b + 1, :]
        mine = same(target, 128)
        running = lax.dot_general(
            jnp.where(mine, 1.0, 0.0).astype(BF16), upper, NN, preferred_element_type=F32
        )
        rank = jnp.sum(jnp.where(mine, running + before, 0.0), axis=0, keepdims=True).astype(I32) - 1
        before += jnp.broadcast_to(running[:, LANES - 1 :], (128, LANES))
        rank = jnp.maximum(rank, 0)
        key = jnp.where(target >= 0, target + (rank & 1) * 128, -1)
        rank_half = rank >> 1
        slot_ref[0, b : b + 1, :] = key
        slot_ref[1, b : b + 1, :] = rank_half
        total += lax.dot_general(
            spread_ranks(split, b, rank_half), hot_rows(key, LANES), NT, preferred_element_type=F32
        )
    sums = joined(total, PAD_RANKS, 5)
    store_slots(out_ref, jnp.concatenate(sums[:3], axis=0), 0, 2)
    store_slots(out_ref, jnp.concatenate(sums[3:], axis=0), 1, 2)


def unpack(recv_ref, slot_ref, key_hot, seen, blocks):
    turned = load_slots(recv_ref, 0, 1)[: 2 * PAD_RANKS]
    table = jnp.concatenate(halves(turned), axis=0).astype(BF16)
    for b in range(blocks):
        hot = hot_rows(slot_ref[0, b : b + 1, :], LANES)
        if key_hot is not None:
            key_hot[b] = hot
        found = lax.dot_general(table, hot, NN, preferred_element_type=F32)
        found = found[: 2 * PAD_RANKS] + found[2 * PAD_RANKS :]
        mine = same(slot_ref[1, b : b + 1, :], PAD_RANKS)
        for v in range(2):
            part = jnp.where(mine, found[v * PAD_RANKS : (v + 1) * PAD_RANKS], 0.0)
            seen[v, b : b + 1, :] = jnp.sum(part, axis=0, keepdims=True)


def owner_middle(
    recv_ref, start_ref, coef_ref, slot_ref, out_ref, partial_ref, key_hot, seen, split
):
    blocks = start_ref.shape[0]
    unpack(recv_ref, slot_ref, key_hot, seen, blocks)
    own, left, right, pull, weight = [coef_ref[i] for i in range(5)]
    now = start_ref[...]
    for v in range(2):
        now = own + left * shift_right(now) + right * shift_left(now) + pull * seen[v]
    partial = own + left * shift_right(now) + right * shift_left(now)
    partial_ref[...] = partial
    put_split(split, 0, weight * now)
    put_split(split, 1, weight * partial)
    total = jnp.zeros((4 * PAD_RANKS, LANES), F32)
    for b in range(blocks):
        total += lax.dot_general(
            spread_ranks(split, b, slot_ref[1, b : b + 1, :]), key_hot[b], NT,
            preferred_element_type=F32,
        )
    store_slots(out_ref, jnp.concatenate(joined(total, PAD_RANKS, 2), axis=0), 0, 1)


def owner_last(recv_ref, coef_ref, slot_ref, partial_ref, out_ref, seen):
    blocks = partial_ref.shape[0]
    unpack(recv_ref, slot_ref, None, seen, blocks)
    own, left, right, pull = [coef_ref[i] for i in range(4)]
    now = partial_ref[...] + pull * seen[0]
    out_ref[...] = own + left * shift_right(now) + right * shift_left(now) + pull * seen[1]


def fold(field):
    return jnp.concatenate([field[:, :LANES], field[:, LANES:]], axis=0)


def unfold(rows):
    half = ROWS // 2
    return jnp.concatenate([rows[:half], rows[half:]], axis=1)


def gather_cells(fields, cell_ref, found_ref):
    parts = []
    for field in fields:
        parts += halves(fold(field))
    table = jnp.concatenate(parts, axis=0).astype(BF16)
    for r in range(HALF_RANKS):
        mine = same(cell_ref[0, r : r + 1, :], ROWS)
        hot = hot_rows(cell_ref[1, r : r + 1, :], LANES)
        found = lax.dot_general(table, hot, NN, preferred_element_type=F32)
        for v, both in enumerate(joined(found, ROWS, len(fields))):
            found_ref[v * PAD_RANKS + r : v * PAD_RANKS + r + 1, :] = jnp.sum(
                jnp.where(mine, both, 0.0), axis=0, keepdims=True
            )


def scatter_cells(split, count, cell_ref, sums_ref):
    place = lax.broadcasted_iota(I16, (16, LANES), 0)
    none = jnp.zeros((16, LANES), BF16)
    total = jnp.zeros((2 * count * ROWS, LANES), F32)
    for r in range(HALF_RANKS):
        row = jnp.broadcast_to(cell_ref[0, r : r + 1, :], (16, LANES)).astype(I16)
        mine = [place == row - jnp.int16(16 * j) for j in range(ROWS // 16)]
        rows = []
        for v in range(2 * count):
            value = jnp.broadcast_to(split[v, r : r + 1, :], (16, LANES)).astype(BF16)
            rows += [jnp.where(m, value, none) for m in mine]
        hot = hot_rows(cell_ref[1, r : r + 1, :], LANES)
        total += lax.dot_general(
            jnp.concatenate(rows, axis=0), hot, NT, preferred_element_type=F32
        )
    for v, both in enumerate(joined(total, ROWS, count)):
        sums_ref[v] = unfold(both)


def put_faces(field, refs):
    rows = field.shape[0]
    refs[0][...] = field[rows - 8 :]
    refs[1][...] = field[:8]
    refs[2][...] = jnp.concatenate([field[i + 7 : i + 8] for i in range(0, rows, 8)], axis=0)
    refs[3][...] = jnp.concatenate([field[i : i + 1] for i in range(0, rows, 8)], axis=0)


def rock_faces(perm_ref, start_ref, a, b, c, d):
    perm, start = perm_ref[...], start_ref[...]
    rows = perm.shape[0]
    for i, field in enumerate((perm, start)):
        a[i * 8 : i * 8 + 8, :] = field[rows - 8 :]
        b[i * 8 : i * 8 + 8, :] = field[:8]
    c[...] = jnp.concatenate(
        [f[i + 7 : i + 8] for f in (perm, start) for i in range(0, rows, 8)], axis=0
    )
    d[...] = jnp.concatenate(
        [f[i : i + 1] for f in (perm, start) for i in range(0, rows, 8)], axis=0
    )


def neighbours(field, x_low, x_high, y_low, y_high, ny):
    rows, nz = field.shape
    nx = rows // ny
    west = jnp.concatenate([x_low, field[: rows - ny]], axis=0)
    east = jnp.concatenate([field[ny:], x_high], axis=0)
    place = lax.broadcasted_iota(I32, (rows, nz), 0) % ny
    wide_low = jnp.concatenate(
        [jnp.broadcast_to(y_low[i : i + 1], (ny, nz)) for i in range(nx)], axis=0
    )
    wide_high = jnp.concatenate(
        [jnp.broadcast_to(y_high[i : i + 1], (ny, nz)) for i in range(nx)], axis=0
    )
    south = jnp.where(place == 0, wide_low, pltpu.roll(field, 1, 0))
    north = jnp.where(place == ny - 1, wide_high, pltpu.roll(field, rows - 1, 0))
    below = pltpu.roll(field, 1, 1)
    above = pltpu.roll(field, nz - 1, 1)
    return west, east, south, north, below, above


def tile_scatter(recv_ref, sums_ref, cells_ref, split):
    first = load_slots(recv_ref, 0, 2)
    second = load_slots(recv_ref, 1, 2)
    cell = first[:PAD_RANKS].astype(I32)
    deep = cell & 511
    cells_ref[0] = ((deep >> 8) << 5) + (cell >> 9)
    cells_ref[1] = deep & (LANES - 1)
    put_split(split, 0, first[PAD_RANKS : 2 * PAD_RANKS])
    put_split(split, 1, first[2 * PAD_RANKS : 3 * PAD_RANKS])
    put_split(split, 2, second[:PAD_RANKS])
    put_split(split, 3, second[PAD_RANKS : 2 * PAD_RANKS])
    scatter_cells(split, 4, cells_ref, sums_ref)


def tile_first(edge_ref, hits_ref, cells_ref, perm_ref, start_ref, storage_ref, xl, xh, yl, yh,
               out_ref, next_ref, sums_ref, faces_ref, a, b, c, d, found):
    rows, nz = perm_ref.shape
    ny = 8
    perm = perm_ref[...]
    start = start_ref[...]
    nx = rows // ny
    beside = neighbours(perm, xl[:8], xh[:8], yl[:nx], yh[:nx], ny)
    around = neighbours(start, xl[8:], xh[8:], yl[nx:], yh[nx:], ny)
    row = lax.broadcasted_iota(I32, (rows, nz), 0)
    lane = lax.broadcasted_iota(I32, (rows, nz), 1)
    closed = [
        (row < ny) & (edge_ref[0] == 0),
        (row >= rows - ny) & (edge_ref[1] == 0),
        (row % ny == 0) & (edge_ref[2] == 0),
        (row % ny == ny - 1) & (edge_ref[3] == 0),
        lane == 0,
        lane == nz - 1,
    ]
    storage = storage_ref[...]
    base = storage * start
    inflow = jnp.zeros_like(start)
    total = storage + hits_ref[0]
    for i in range(6):
        face = jnp.where(closed[i], 0.0, 2.0 * perm * beside[i] / (perm + beside[i]))
        faces_ref[i] = face
        total += face
        inflow += face * around[i]
    inverse = 1.0 / total
    now = (base + inflow + hits_ref[1]) * inverse
    next_ref[...] = now
    put_faces(now, (a, b, c, d))
    sums_ref[0] = inverse
    sums_ref[1] = base
    sums_ref[2] = base + hits_ref[2] + start * hits_ref[3]
    sums_ref[3] = hits_ref[3]
    found[...] = jnp.zeros_like(found)
    gather_cells([start, now], cells_ref, found)
    store_slots(out_ref, found[...], 0, 1)


def flow_in(field, faces_ref, xl, xh, yl, yh):
    around = neighbours(field, xl[...], xh[...], yl[...], yh[...], 8)
    total = faces_ref[0] * around[0]
    for i in range(1, 6):
        total += faces_ref[i] * around[i]
    return total


def tile_second(now_ref, sums_ref, faces_ref, xl, xh, yl, yh, after, next_ref, a, b, c, d):
    inflow = flow_in(now_ref[...], faces_ref, xl, xh, yl, yh)
    later = (sums_ref[2] + inflow) * sums_ref[0]
    next_ref[...] = later
    put_faces(later, (a, b, c, d))


def tile_scatter_again(recv_ref, cells_ref, sums_ref, split):
    turned = load_slots(recv_ref, 0, 1)
    put_split(split, 0, turned[:PAD_RANKS])
    put_split(split, 1, turned[PAD_RANKS : 2 * PAD_RANKS])
    scatter_cells(split, 2, cells_ref, sums_ref)


def tile_third(hits_ref, now_ref, sums_ref, faces_ref, cells_ref, xl, xh, yl, yh,
               out_ref, next_ref, last_ref, a, b, c, d, found):
    now = now_ref[...]
    inflow = flow_in(now, faces_ref, xl, xh, yl, yh)
    later = (sums_ref[1] + inflow + hits_ref[0]) * sums_ref[0]
    next_ref[...] = later
    put_faces(later, (a, b, c, d))
    last_ref[...] = sums_ref[1] + hits_ref[1] + now * sums_ref[3]
    found[...] = jnp.zeros_like(found)
    gather_cells([now, later], cells_ref, found)
    store_slots(out_ref, found[...], 0, 1)


def tile_last(now_ref, last_ref, sums_ref, faces_ref, xl, xh, yl, yh, after, out_ref):
    inflow = flow_in(now_ref[...], faces_ref, xl, xh, yl, yh)
    out_ref[...] = (last_ref[...] + inflow) * sums_ref[0]


def ring(block, axis, step):
    count = lax.axis_size(axis)
    return lax.ppermute(block, axis, [(i, (i + step) % count) for i in range(count)])


def swap(faces):
    return (
        ring(faces[0], "flow", 1),
        ring(faces[1], "flow", -1),
        ring(faces[2], "cross", 1),
        ring(faces[3], "cross", -1),
    )


def deliver(payload):
    return lax.all_to_all(payload, ("flow", "cross"), split_axis=0, concat_axis=0, tiled=True)


def on_device(
    matrix_start, storage, perm, frac_start, frac_store, frac_cond,
    segment_ids, block_counts, hit_tile, hit_cell, hit_weight,
):
    n_flow, n_cross = lax.axis_size("flow"), lax.axis_size("cross")
    i_flow, i_cross = lax.axis_index("flow"), lax.axis_index("cross")
    blocks = frac_start.shape[0]
    nx, ny, nz = matrix_start.shape
    rows = nx * ny
    start, storage, perm = [a.reshape(rows, nz) for a in (matrix_start, storage, perm)]
    field = shape(rows, nz)
    faces_of = lambda n: (shape(n * ny, nz), shape(n * ny, nz), shape(n * nx, nz), shape(n * nx, nz))
    owned = lambda dtype: pltpu.VMEM((blocks, LANES), dtype)
    edges = jnp.stack([i_flow, n_flow - 1 - i_flow, i_cross, n_cross - 1 - i_cross]).astype(I32)

    hits, coef, slots = call(
        owner_first,
        (shape(512, 128), shape(5, blocks, LANES), shape(2, blocks, LANES, dtype=I32)),
        8,
        scratch=[
            owned(F32), owned(F32), owned(F32), owned(I32),
            pltpu.VMEM((2 * blocks, 128), I32), owned(I32), owned(F32),
            pltpu.SemaphoreType.DMA((7,)),
            pltpu.VMEM((10, blocks, LANES), F32),
        ],
        smem=(0,),
        remote=range(1, 8),
        microseconds=6,
    )(
        block_counts, frac_start, frac_store, frac_cond, segment_ids,
        hit_tile.reshape(2 * blocks, 128), hit_cell, hit_weight,
    )
    hits = deliver(hits)
    around = swap(call(rock_faces, faces_of(2), 2)(perm, start))
    sums, cells = call(
        tile_scatter,
        (shape(4, rows, nz), shape(2, PAD_RANKS, LANES, dtype=I32)),
        1,
        scratch=[pltpu.VMEM((8, PAD_RANKS, LANES), F32)],
        microseconds=4,
    )(hits)
    found = pltpu.VMEM((2 * PAD_RANKS, LANES), F32)
    seen, first, sums, faces, *sides = call(
        tile_first,
        (shape(256, 128), field, shape(4, rows, nz), shape(6, rows, nz)) + faces_of(1),
        10,
        scratch=[found],
        smem=(0,),
        microseconds=4,
    )(edges, sums, cells, perm, start, storage, *around)
    seen = deliver(seen)
    around = swap(sides)

    pushed, partial = call(
        owner_middle,
        (shape(256, 128), shape(blocks, LANES)),
        4,
        scratch=[
            pltpu.VMEM((blocks, LANES, LANES), BF16),
            pltpu.VMEM((2, blocks, LANES), F32),
            pltpu.VMEM((4, blocks, LANES), F32),
        ],
        microseconds=5,
    )(seen, frac_start, coef, slots)
    pushed = deliver(pushed)
    second, *sides = call(tile_second, (field,) + faces_of(1), 8, remote=(7,))(
        first, sums, faces, *around, partial
    )
    around = swap(sides)

    hits = call(
        tile_scatter_again,
        shape(2, rows, nz),
        2,
        scratch=[pltpu.VMEM((4, PAD_RANKS, LANES), F32)],
        microseconds=3,
    )(pushed, cells)
    seen, third, last, *sides = call(
        tile_third,
        (shape(256, 128), field, field) + faces_of(1),
        9,
        scratch=[found],
        microseconds=4,
    )(hits, second, sums, faces, cells, *around)
    seen = deliver(seen)
    around = swap(sides)
    frac = call(
        owner_last,
        shape(blocks, LANES),
        4,
        scratch=[pltpu.VMEM((2, blocks, LANES), F32)],
        microseconds=4,
    )(seen, coef, slots, partial)
    fourth = call(tile_last, field, 9, remote=(8,))(third, last, sums, faces, *around, frac)
    return fourth.reshape(nx, ny, nz), frac


def solution(mesh):
    grid = P("flow", "cross", None)
    owner = P(("flow", "cross"), None)
    counts, tiles = P(("flow", "cross")), P(("flow", "cross"), None, None)
    in_specs = (grid,) * 3 + (owner,) * 4 + (counts, tiles, owner, owner)
    return jax.shard_map(
        on_device, mesh=mesh, in_specs=in_specs, out_specs=(grid, owner), check_vma=False
    )
```

time: 129 us -> 104 us (0.81)
  Pallas kernels: 47.8 us -> 19.3 us
  blocking collectives: 0 us -> 14.2 us
  waiting for transfers between devices: 18 us -> 8.06 us
  starting transfers between devices: 57.3 us -> 54.5 us
  local copies, waits for them, and re-layouts: 3.93 us -> 5.91 us
    pallas_call x5 -> x7, Pallas kernels: 26.4 us -> 9.57 us  [the longest x1 2.72 us: on_device(): call(tile_scatter, (shape(4, rows, nz), shape(2, PAD_RANKS, LANES, dtype=...]
    all_to_all x0 -> x1, blocking collectives: none -> 14.2 us  [deliver(): lax.all_to_all(payload, ('flow', 'cross'), split_axis=0, concat_axis=0, t...]
    ppermute x16, waiting for transfers between devices: 6.62 us -> 1.41 us  [ring(): lax.ppermute(block, axis, [(i, (i + step) % count) for i in range(count)])]
    pallas_call x1, Pallas kernels: 7.36 us -> 2.63 us  [on_device(): call(owner_middle, (shape(256, 128), shape(blocks, LANES)), 4, scratch=[p...]
    all_to_all x4 -> x3, waiting for transfers between devices: 11.4 us -> 6.64 us  [deliver(): lax.all_to_all(payload, ('flow', 'cross'), split_axis=0, concat_axis=0, t...]
    pallas_call x1, Pallas kernels: 5.39 us -> 1.48 us  [on_device(): call(owner_last, shape(blocks, LANES), 4, scratch=[pltpu.VMEM((2, blocks,...]
    pallas_call x1, Pallas kernels: 8.7 us -> 5.66 us  [on_device(): call(owner_first, (shape(512, 128), shape(5, blocks, LANES), shape(2, blo...]
    unnamed x27 -> x24, local copies, waits for them, and re-layouts: 3.77 us -> 5.91 us
  transfers between devices with their start and end apart: 20 -> 19, of which waited for: 8 -> 3; matrix products, arithmetic and copies ran while one was open for 0% -> 0% of each run, Pallas kernels for 7% -> 6%
where the time goes in v2:
time: 104 us
  starting transfers between devices  54.5 us (52%)
  Pallas kernels  19.3 us (19%)
  blocking collectives  14.2 us (14%)
  waiting for transfers between devices  8.06 us (8%)
  local copies, waits for them, and re-layouts  5.91 us (6%)
  between operations  1.5 us (1%)
    ppermute x16, starting transfers between devices, ring(): lax.ppermute(block, axis, [(i, (i + step) % count) for i in range(count)])  29.2 us
    all_to_all x3, starting transfers between devices, deliver(): lax.all_to_all(payload, ('flow', 'cross'), split_axis=0, concat_axis=0, t...  25.3 us
    all_to_all x1, blocking collectives, deliver(): lax.all_to_all(payload, ('flow', 'cross'), split_axis=0, concat_axis=0, t...  14.2 us
    all_to_all x3, waiting for transfers between devices, deliver(): lax.all_to_all(payload, ('flow', 'cross'), split_axis=0, concat_axis=0, t...  6.64 us
    unnamed x24, local copies, waits for them, and re-layouts  5.91 us
    pallas_call x1, Pallas kernels, on_device(): call(owner_first, (shape(512, 128), shape(5, blocks, LANES), shape(2, blo...  5.66 us
    pallas_call x1, Pallas kernels, on_device(): call(tile_scatter, (shape(4, rows, nz), shape(2, PAD_RANKS, LANES, dtype=...  2.72 us
    pallas_call x1, Pallas kernels, on_device(): call(owner_middle, (shape(256, 128), shape(blocks, LANES)), 4, scratch=[p...  2.63 us
  transfers between devices with their start and end apart: 19, of which 3 were waited for; matrix products, arithmetic and copies ran while one was open for 0% of the time, Pallas kernels for 6%

profile of v2, /device:TPU:1, one launch (start us, length us, event | category | flops | bytes accessed | tf_op | source)
XLA Modules:
  0.0 103.6 jit_solution(773412443923241206)
XLA Ops:
  1.3 0.0 copy-start.2
  1.3 0.7 copy-done.2
  2.0 0.7 copy-done.6
  2.8 0.7 copy-done.7
  3.5 0.7 copy-done.8
  4.2 0.7 copy-done.9
  5.0 0.7 copy-done.10
  5.7 0.7 copy-done.11
  6.4 5.7 %shard_map.122 = (f32[512,128]{1,0:T(8,128)}, f32[5,24,256]{2,1,0:T(8,128)S(1)}, s32[2,24,256]{2,1,0:T(8,128)S(1)}) custom-call(s32[1]{0:T(128)S(6)} %copy.13.count_ref, f32[24,256]{1,0:T(8,128)S(1)} %copy-done.2, f32[24,256]{1,0:T(8,128)S(1)} %copy-done.6, f32[24,256]{1,0:T(8,128)S(1)} %copy-done.7, s32[24,256]{1,0:T(8,128)S(1)} %copy-done.8, ...), custom_call_target="tpu_custom_call" | custom-call | bytes 18000000 | tf_op jit(solution)/shard_map/pallas_call | solution.py:437
  12.1 0.0 copy-start
  12.1 0.0 copy-start.1
  12.1 11.5 %all-to-all-start = ((f32[128,4,128]{2,1,0:T(4,128)}), f32[128,4,128]{2,1,0:T(4,128)S(1)}, u32[]{:S(2)}, u32[]{:S(2)}) async-start(f32[128,4,128]{2,1,0:T(4,128)} %bitcast.5), calls=%async_computation | async-start | bytes 524288 | tf_op jit(solution)/shard_map/all_to_all | solution.py:419
  23.7 1.6 %collective-permute-start.2 = (f32[8,512]{1,0:T(8,128)S(1)}, f32[8,512]{1,0:T(8,128)S(1)}, u32[]{:S(2)}, u32[]{:S(2)}) collective-permute-start(f32[8,512]{1,0:T(8,128)S(1)} %get-tuple-element.38), channel_id=1, source_target_pairs={{0,1},{1,2},{2,3},{3,4},{4,5},{5,6},{6,7},{7,8},{8,9},{9,10},{10,1... | collective-permute-start | bytes 49160 | tf_op jit(solution)/shard_map/ppermute | solution.py:406
  25.3 4.1 %collective-permute-start.3 = (f32[8,512]{1,0:T(8,128)S(1)}, f32[8,512]{1,0:T(8,128)S(1)}, u32[]{:S(2)}, u32[]{:S(2)}) collective-permute-start(f32[8,512]{1,0:T(8,128)S(1)} %get-tuple-element.39), channel_id=1, source_target_pairs={{0,15},{1,0},{2,1},{3,2},{4,3},{5,4},{6,5},{7,6},{8,7},{9,8},{10,9... | collective-permute-start | bytes 49160 | tf_op jit(solution)/shard_map/ppermute | solution.py:406
  29.4 1.7 %collective-permute-start = (f32[16,512]{1,0:T(8,128)S(1)}, f32[16,512]{1,0:T(8,128)S(1)}, u32[]{:S(2)}, u32[]{:S(2)}) collective-permute-start(f32[16,512]{1,0:T(8,128)S(1)} %get-tuple-element.36), channel_id=1, source_target_pairs={{0,16},{16,32},{32,48},{48,64},{64,80},{80,96},{96,112},{112,0},{1... | collective-permute-start | bytes 98312 | tf_op jit(solution)/shard_map/ppermute | solution.py:406
  31.1 0.0 collective-permute-start.1
  31.1 0.1 pad_add_fusion.edge_ref
  31.2 3.7 %all-to-all-done = f32[128,4,128]{2,1,0:T(4,128)S(1)} async-done(((f32[128,4,128]{2,1,0:T(4,128)}), f32[128,4,128]{2,1,0:T(4,128)S(1)}, u32[]{:S(2)}, u32[]{:S(2)}) %all-to-all-start) | async-done | bytes 262176 | tf_op jit(solution)/shard_map/all_to_all | solution.py:419
  34.9 2.7 %shard_map.123 = (f32[4,32,512]{2,1,0:T(8,128)S(1)}, s32[2,40,256]{2,1,0:T(8,128)S(1)}) custom-call(f32[512,128]{1,0:T(8,128)S(1)} %bitcast.17), custom_call_target="tpu_custom_call" | custom-call | bytes 12000000 | tf_op jit(solution)/shard_map/pallas_call | solution.py:456
  37.6 0.0 collective-permute-done.2.yl
  37.6 0.0 collective-permute-done.3.yh
  37.6 0.0 collective-permute-done.1.xh
  37.7 2.3 %shard_map.125 = (f32[256,128]{1,0:T(8,128)S(1)}, f32[32,512]{1,0:T(8,128)S(1)}, f32[4,32,512]{2,1,0:T(8,128)S(1)}, f32[6,32,512]{2,1,0:T(8,128)S(1)}, f32[8,512...) custom-call(s32[4]{0:T(128)S(1)} %pad_add_fusion.edge_ref, ...), custom_call_target="tpu_custom_call" | custom-call | bytes 12000000 | tf_op jit(solution)/shard_map/pallas_call | solution.py:464
  40.0 0.0 copy-start.3
  40.0 14.2 %all_to_all.44 = f32[128,2,128]{2,1,0:T(2,128)S(1)} all-to-all(f32[128,2,128]{2,1,0:T(2,128)S(1)} %bitcast.25), channel_id=1, replica_groups=mesh['flow'=8,'cross'=16] {'flow','cross'}, dimensions={0} | all-to-all | bytes 262144 | tf_op jit(solution)/shard_map/all_to_all | solution.py:419
  54.2 2.6 %shard_map.126 = (f32[256,128]{1,0:T(8,128)}, f32[24,256]{1,0:T(8,128)S(1)}) custom-call(f32[256,128]{1,0:T(8,128)S(1)} %bitcast.19, f32[24,256]{1,0:T(8,128)S(1)} %copy-done.3, f32[5,24,256]{2,1,0:T(8,128)S(1)} %get-tuple-element.41.coef_ref, s32[2,24,256]{2,1,0:T(8,128)S(1)} %get-tuple-element.42.slot_ref), custom_call_target="tpu_custom_call" | custom-call | bytes 15000000 | tf_op jit(solution)/shard_map/pallas_call | solution.py:475
  56.8 4.2 %all-to-all-start.2 = ((f32[128,2,128]{2,1,0:T(2,128)}), f32[128,2,128]{2,1,0:T(2,128)S(1)}, u32[]{:S(2)}, u32[]{:S(2)}) async-start(f32[128,2,128]{2,1,0:T(2,128)} %bitcast.12), calls=%async_computation.2 | async-start | bytes 262144 | tf_op jit(solution)/shard_map/all_to_all | solution.py:419
  61.0 1.6 %collective-permute-start.4 = (f32[8,512]{1,0:T(8,128)S(1)}, f32[8,512]{1,0:T(8,128)S(1)}, u32[]{:S(2)}, u32[]{:S(2)}) collective-permute-start(f32[8,512]{1,0:T(8,128)S(1)} %get-tuple-element.47), channel_id=1, source_target_pairs={{0,16},{16,32},{32,48},{48,64},{64,80},{80,96},{96,112},{112,0},{1... | collective-permute-start | bytes 49160 | tf_op jit(solution)/shard_map/ppermute | solution.py:406
  62.6 0.0 collective-permute-start.5
  62.6 1.4 %collective-permute-start.6 = (f32[4,512]{1,0:T(4,128)S(1)}, f32[4,512]{1,0:T(4,128)S(1)}, u32[]{:S(2)}, u32[]{:S(2)}) collective-permute-start(f32[4,512]{1,0:T(4,128)S(1)} %get-tuple-element.49), channel_id=1, source_target_pairs={{0,1},{1,2},{2,3},{3,4},{4,5},{5,6},{6,7},{7,8},{8,9},{9,10},{10,1... | collective-permute-start | bytes 24584 | tf_op jit(solution)/shard_map/ppermute | solution.py:406
  64.0 4.1 %collective-permute-start.7 = (f32[4,512]{1,0:T(4,128)S(1)}, f32[4,512]{1,0:T(4,128)S(1)}, u32[]{:S(2)}, u32[]{:S(2)}) collective-permute-start(f32[4,512]{1,0:T(4,128)S(1)} %get-tuple-element.50), channel_id=1, source_target_pairs={{0,15},{1,0},{2,1},{3,2},{4,3},{5,4},{6,5},{7,6},{8,7},{9,8},{10,9... | collective-permute-start | bytes 24584 | tf_op jit(solution)/shard_map/ppermute | solution.py:406
  68.1 1.4 %collective-permute-done.6.yl = f32[4,512]{1,0:T(4,128)S(1)} collective-permute-done((f32[4,512]{1,0:T(4,128)S(1)}, f32[4,512]{1,0:T(4,128)S(1)}, u32[]{:S(2)}, u32[]{:S(2)}) %collective-permute-start.6) | collective-permute-done | bytes 8224 | tf_op jit(solution)/shard_map/ppermute | solution.py:406
  69.5 0.1 shard_map.128
  69.6 2.3 %collective-permute-start.8 = (f32[8,512]{1,0:T(8,128)S(1)}, f32[8,512]{1,0:T(8,128)S(1)}, u32[]{:S(2)}, u32[]{:S(2)}) collective-permute-start(f32[8,512]{1,0:T(8,128)S(1)} %get-tuple-element.53), channel_id=1, source_target_pairs={{0,16},{16,32},{32,48},{48,64},{64,80},{80,96},{96,112},{112,0},{1... | collective-permute-start | bytes 49160 | tf_op jit(solution)/shard_map/ppermute | solution.py:406
  71.9 0.3 collective-permute-start.9
  72.2 0.0 collective-permute-start.10
  72.2 5.1 %collective-permute-start.11 = (f32[4,512]{1,0:T(4,128)S(1)}, f32[4,512]{1,0:T(4,128)S(1)}, u32[]{:S(2)}, u32[]{:S(2)}) collective-permute-start(f32[4,512]{1,0:T(4,128)S(1)} %get-tuple-element.56), channel_id=1, source_target_pairs={{0,15},{1,0},{2,1},{3,2},{4,3},{5,4},{6,5},{7,6},{8,7},{9,8},{10,9... | collective-permute-start | bytes 24584 | tf_op jit(solution)/shard_map/ppermute | solution.py:406
  77.3 1.4 %shard_map.127.hits_ref = f32[2,32,512]{2,1,0:T(8,128)S(1)} custom-call(f32[256,128]{1,0:T(8,128)S(1)} %bitcast.18, s32[2,40,256]{2,1,0:T(8,128)S(1)} %get-tuple-element.35.cells_ref), custom_call_target="tpu_custom_call" | custom-call | bytes 9000000 | tf_op jit(solution)/shard_map/pallas_call | solution.py:492
  78.8 2.3 %shard_map.129 = (f32[256,128]{1,0:T(8,128)}, f32[32,512]{1,0:T(8,128)S(1)}, f32[32,512]{1,0:T(8,128)S(1)}, f32[8,512]{1,0:T(8,128)S(1)}, f32[8,512]{1,0:T(8,128...) custom-call(f32[2,32,512]{2,1,0:T(8,128)S(1)} %shard_map.127.hits_ref, f32[32,512]{1,0:T(8,128)S(1)} %get-tuple-element.52.now_ref, ...), custom_call_target="tpu_custom_call" | custom-call | bytes 12000000 | tf_op jit(solution)/shard_map/pallas_call | solution.py:499
  81.0 9.6 %all-to-all-start.3 = ((f32[128,2,128]{2,1,0:T(2,128)}), f32[128,2,128]{2,1,0:T(2,128)S(1)}, u32[]{:S(2)}, u32[]{:S(2)}) async-start(f32[128,2,128]{2,1,0:T(2,128)} %bitcast.14), calls=%async_computation.3 | async-start | bytes 262144 | tf_op jit(solution)/shard_map/all_to_all | solution.py:419
  90.6 1.6 %collective-permute-start.12 = (f32[8,512]{1,0:T(8,128)S(1)}, f32[8,512]{1,0:T(8,128)S(1)}, u32[]{:S(2)}, u32[]{:S(2)}) collective-permute-start(f32[8,512]{1,0:T(8,128)S(1)} %get-tuple-element.59), channel_id=1, source_target_pairs={{0,16},{16,32},{32,48},{48,64},{64,80},{80,96},{96,112},{112,0},{1... | collective-permute-start | bytes 49160 | tf_op jit(solution)/shard_map/ppermute | solution.py:406
  92.2 1.3 %collective-permute-start.14 = (f32[4,512]{1,0:T(4,128)S(1)}, f32[4,512]{1,0:T(4,128)S(1)}, u32[]{:S(2)}, u32[]{:S(2)}) collective-permute-start(f32[4,512]{1,0:T(4,128)S(1)} %get-tuple-element.61), channel_id=1, source_target_pairs={{0,1},{1,2},{2,3},{3,4},{4,5},{5,6},{6,7},{7,8},{8,9},{9,10},{10,1... | collective-permute-start | bytes 24584 | tf_op jit(solution)/shard_map/ppermute | solution.py:406
  93.6 4.1 %collective-permute-start.15 = (f32[4,512]{1,0:T(4,128)S(1)}, f32[4,512]{1,0:T(4,128)S(1)}, u32[]{:S(2)}, u32[]{:S(2)}) collective-permute-start(f32[4,512]{1,0:T(4,128)S(1)} %get-tuple-element.62), channel_id=1, source_target_pairs={{0,15},{1,0},{2,1},{3,2},{4,3},{5,4},{6,5},{7,6},{8,7},{9,8},{10,9... | collective-permute-start | bytes 24584 | tf_op jit(solution)/shard_map/ppermute | solution.py:406
  97.6 3.0 %all-to-all-done.3 = f32[128,2,128]{2,1,0:T(2,128)S(1)} async-done(((f32[128,2,128]{2,1,0:T(2,128)}), f32[128,2,128]{2,1,0:T(2,128)S(1)}, u32[]{:S(2)}, u32[]{:S(2)}) %all-to-all-start.3) | async-done | bytes 131104 | tf_op jit(solution)/shard_map/all_to_all | solution.py:419
  100.6 1.5 %shard_map.130.after = f32[24,256]{1,0:T(8,128)} custom-call(f32[256,128]{1,0:T(8,128)S(1)} %bitcast.20, f32[5,24,256]{2,1,0:T(8,128)S(1)} %get-tuple-element.41.coef_ref, s32[2,24,256]{2,1,0:T(8,128)S(1)} %get-tuple-element.42.slot_ref, f32[24,256]{1,0:T(8,128)S(1)} %get-tuple-element.51.after.partial_ref), custom_call_target="tpu_custom_call" | custom-call | bytes 12000000 | tf_op jit(solution)/shard_map/pallas_call | solution.py:508
  102.1 0.0 copy-start.4
  102.1 0.7 copy-done.4
  102.8 0.7 shard_map.131
  (26 shorter events, 0.1 us)
Async XLA Ops:
  1.3 0.7 copy-start.2
  2.0 0.7 copy-start.6
  2.8 0.7 copy-start.7
  3.5 0.7 copy-start.8
  4.2 0.7 copy-start.9
  5.0 0.7 copy-start.10
  5.7 0.7 copy-start.11
  12.1 11.5 %copy-start = (f32[4,8,512]{2,1,0:T(8,128)S(1)}, f32[4,8,512]{2,1,0:T(8,128)}, u32[]{:S(2)}) copy-start(f32[4,8,512]{2,1,0:T(8,128)} %param.13) | copy-start | bytes 196612
  12.1 11.5 %copy-start.1 = (f32[4,8,512]{2,1,0:T(8,128)S(1)}, f32[4,8,512]{2,1,0:T(8,128)}, u32[]{:S(2)}) copy-start(f32[4,8,512]{2,1,0:T(8,128)} %param.11) | copy-start | bytes 196612
  12.1 22.8 %all-to-all-start = ((f32[128,4,128]{2,1,0:T(4,128)}), f32[128,4,128]{2,1,0:T(4,128)S(1)}, u32[]{:S(2)}, u32[]{:S(2)}) async-start(f32[128,4,128]{2,1,0:T(4,128)} %bitcast.5), calls=%async_computation | async-start | bytes 524288 | tf_op jit(solution)/shard_map/all_to_all | solution.py:419
  23.7 13.9 %collective-permute-start.2 = (f32[8,512]{1,0:T(8,128)S(1)}, f32[8,512]{1,0:T(8,128)S(1)}, u32[]{:S(2)}, u32[]{:S(2)}) collective-permute-start(f32[8,512]{1,0:T(8,128)S(1)} %get-tuple-element.38), channel_id=1, source_target_pairs={{0,1},{1,2},{2,3},{3,4},{4,5},{5,6},{6,7},{7,8},{8,9},{9,10},{10,1... | collective-permute-start | bytes 49160 | tf_op jit(solution)/shard_map/ppermute | solution.py:406
  25.3 12.4 %collective-permute-start.3 = (f32[8,512]{1,0:T(8,128)S(1)}, f32[8,512]{1,0:T(8,128)S(1)}, u32[]{:S(2)}, u32[]{:S(2)}) collective-permute-start(f32[8,512]{1,0:T(8,128)S(1)} %get-tuple-element.39), channel_id=1, source_target_pairs={{0,15},{1,0},{2,1},{3,2},{4,3},{5,4},{6,5},{7,6},{8,7},{9,8},{10,9... | collective-permute-start | bytes 49160 | tf_op jit(solution)/shard_map/ppermute | solution.py:406
  29.4 8.2 %collective-permute-start = (f32[16,512]{1,0:T(8,128)S(1)}, f32[16,512]{1,0:T(8,128)S(1)}, u32[]{:S(2)}, u32[]{:S(2)}) collective-permute-start(f32[16,512]{1,0:T(8,128)S(1)} %get-tuple-element.36), channel_id=1, source_target_pairs={{0,16},{16,32},{32,48},{48,64},{64,80},{80,96},{96,112},{112,0},{1... | collective-permute-start | bytes 98312 | tf_op jit(solution)/shard_map/ppermute | solution.py:406
  31.1 6.5 %collective-permute-start.1 = (f32[16,512]{1,0:T(8,128)S(1)}, f32[16,512]{1,0:T(8,128)S(1)}, u32[]{:S(2)}, u32[]{:S(2)}) collective-permute-start(f32[16,512]{1,0:T(8,128)S(1)} %get-tuple-element.37), channel_id=1, source_target_pairs={{0,112},{16,0},{32,16},{48,32},{64,48},{80,64},{96,80},{112,96},{1... | collective-permute-start | bytes 98312 | tf_op jit(solution)/shard_map/ppermute | solution.py:406
  34.9 2.8 %copy-start.5 = (f32[4,8,512]{2,1,0:T(8,128)S(1)}, f32[4,8,512]{2,1,0:T(8,128)}, u32[]{:S(2)}) copy-start(f32[4,8,512]{2,1,0:T(8,128)} %param.12) | copy-start | bytes 196612
  40.0 14.2 %copy-start.3 = (f32[24,256]{1,0:T(8,128)S(1)}, f32[24,256]{1,0:T(8,128)}, u32[]{:S(2)}) copy-start(f32[24,256]{1,0:T(8,128)} %start_ref.1) | copy-start | bytes 73732
  56.8 20.5 %all-to-all-start.2 = ((f32[128,2,128]{2,1,0:T(2,128)}), f32[128,2,128]{2,1,0:T(2,128)S(1)}, u32[]{:S(2)}, u32[]{:S(2)}) async-start(f32[128,2,128]{2,1,0:T(2,128)} %bitcast.12), calls=%async_computation.2 | async-start | bytes 262144 | tf_op jit(solution)/shard_map/all_to_all | solution.py:419
  61.0 8.5 %collective-permute-start.4 = (f32[8,512]{1,0:T(8,128)S(1)}, f32[8,512]{1,0:T(8,128)S(1)}, u32[]{:S(2)}, u32[]{:S(2)}) collective-permute-start(f32[8,512]{1,0:T(8,128)S(1)} %get-tuple-element.47), channel_id=1, source_target_pairs={{0,16},{16,32},{32,48},{48,64},{64,80},{80,96},{96,112},{112,0},{1... | collective-permute-start | bytes 49160 | tf_op jit(solution)/shard_map/ppermute | solution.py:406
  62.6 6.8 %collective-permute-start.5 = (f32[8,512]{1,0:T(8,128)S(1)}, f32[8,512]{1,0:T(8,128)S(1)}, u32[]{:S(2)}, u32[]{:S(2)}) collective-permute-start(f32[8,512]{1,0:T(8,128)S(1)} %get-tuple-element.48), channel_id=1, source_target_pairs={{0,112},{16,0},{32,16},{48,32},{64,48},{80,64},{96,80},{112,96},{1... | collective-permute-start | bytes 49160 | tf_op jit(solution)/shard_map/ppermute | solution.py:406
  62.6 6.8 %collective-permute-start.6 = (f32[4,512]{1,0:T(4,128)S(1)}, f32[4,512]{1,0:T(4,128)S(1)}, u32[]{:S(2)}, u32[]{:S(2)}) collective-permute-start(f32[4,512]{1,0:T(4,128)S(1)} %get-tuple-element.49), channel_id=1, source_target_pairs={{0,1},{1,2},{2,3},{3,4},{4,5},{5,6},{6,7},{7,8},{8,9},{9,10},{10,1... | collective-permute-start | bytes 24584 | tf_op jit(solution)/shard_map/ppermute | solution.py:406
  64.0 5.4 %collective-permute-start.7 = (f32[4,512]{1,0:T(4,128)S(1)}, f32[4,512]{1,0:T(4,128)S(1)}, u32[]{:S(2)}, u32[]{:S(2)}) collective-permute-start(f32[4,512]{1,0:T(4,128)S(1)} %get-tuple-element.50), channel_id=1, source_target_pairs={{0,15},{1,0},{2,1},{3,2},{4,3},{5,4},{6,5},{7,6},{8,7},{9,8},{10,9... | collective-permute-start | bytes 24584 | tf_op jit(solution)/shard_map/ppermute | solution.py:406
  69.6 9.2 %collective-permute-start.8 = (f32[8,512]{1,0:T(8,128)S(1)}, f32[8,512]{1,0:T(8,128)S(1)}, u32[]{:S(2)}, u32[]{:S(2)}) collective-permute-start(f32[8,512]{1,0:T(8,128)S(1)} %get-tuple-element.53), channel_id=1, source_target_pairs={{0,16},{16,32},{32,48},{48,64},{64,80},{80,96},{96,112},{112,0},{1... | collective-permute-start | bytes 49160 | tf_op jit(solution)/shard_map/ppermute | solution.py:406
  71.9 6.9 %collective-permute-start.9 = (f32[8,512]{1,0:T(8,128)S(1)}, f32[8,512]{1,0:T(8,128)S(1)}, u32[]{:S(2)}, u32[]{:S(2)}) collective-permute-start(f32[8,512]{1,0:T(8,128)S(1)} %get-tuple-element.54), channel_id=1, source_target_pairs={{0,112},{16,0},{32,16},{48,32},{64,48},{80,64},{96,80},{112,96},{1... | collective-permute-start | bytes 49160 | tf_op jit(solution)/shard_map/ppermute | solution.py:406
  72.2 6.5 %collective-permute-start.10 = (f32[4,512]{1,0:T(4,128)S(1)}, f32[4,512]{1,0:T(4,128)S(1)}, u32[]{:S(2)}, u32[]{:S(2)}) collective-permute-start(f32[4,512]{1,0:T(4,128)S(1)} %get-tuple-element.55), channel_id=1, source_target_pairs={{0,1},{1,2},{2,3},{3,4},{4,5},{5,6},{6,7},{7,8},{8,9},{9,10},{10,1... | collective-permute-start | bytes 24584 | tf_op jit(solution)/shard_map/ppermute | solution.py:406
  72.2 6.5 %collective-permute-start.11 = (f32[4,512]{1,0:T(4,128)S(1)}, f32[4,512]{1,0:T(4,128)S(1)}, u32[]{:S(2)}, u32[]{:S(2)}) collective-permute-start(f32[4,512]{1,0:T(4,128)S(1)} %get-tuple-element.56), channel_id=1, source_target_pairs={{0,15},{1,0},{2,1},{3,2},{4,3},{5,4},{6,5},{7,6},{8,7},{9,8},{10,9... | collective-permute-start | bytes 24584 | tf_op jit(solution)/shard_map/ppermute | solution.py:406
  81.0 19.6 %all-to-all-start.3 = ((f32[128,2,128]{2,1,0:T(2,128)}), f32[128,2,128]{2,1,0:T(2,128)S(1)}, u32[]{:S(2)}, u32[]{:S(2)}) async-start(f32[128,2,128]{2,1,0:T(2,128)} %bitcast.14), calls=%async_computation.3 | async-start | bytes 262144 | tf_op jit(solution)/shard_map/all_to_all | solution.py:419
  90.6 11.5 %collective-permute-start.12 = (f32[8,512]{1,0:T(8,128)S(1)}, f32[8,512]{1,0:T(8,128)S(1)}, u32[]{:S(2)}, u32[]{:S(2)}) collective-permute-start(f32[8,512]{1,0:T(8,128)S(1)} %get-tuple-element.59), channel_id=1, source_target_pairs={{0,16},{16,32},{32,48},{48,64},{64,80},{80,96},{96,112},{112,0},{1... | collective-permute-start | bytes 49160 | tf_op jit(solution)/shard_map/ppermute | solution.py:406
  92.2 9.9 %collective-permute-start.13 = (f32[8,512]{1,0:T(8,128)S(1)}, f32[8,512]{1,0:T(8,128)S(1)}, u32[]{:S(2)}, u32[]{:S(2)}) collective-permute-start(f32[8,512]{1,0:T(8,128)S(1)} %get-tuple-element.60), channel_id=1, source_target_pairs={{0,112},{16,0},{32,16},{48,32},{64,48},{80,64},{96,80},{112,96},{1... | collective-permute-start | bytes 49160 | tf_op jit(solution)/shard_map/ppermute | solution.py:406
  92.2 9.8 %collective-permute-start.14 = (f32[4,512]{1,0:T(4,128)S(1)}, f32[4,512]{1,0:T(4,128)S(1)}, u32[]{:S(2)}, u32[]{:S(2)}) collective-permute-start(f32[4,512]{1,0:T(4,128)S(1)} %get-tuple-element.61), channel_id=1, source_target_pairs={{0,1},{1,2},{2,3},{3,4},{4,5},{5,6},{6,7},{7,8},{8,9},{9,10},{10,1... | collective-permute-start | bytes 24584 | tf_op jit(solution)/shard_map/ppermute | solution.py:406
  93.6 8.5 %collective-permute-start.15 = (f32[4,512]{1,0:T(4,128)S(1)}, f32[4,512]{1,0:T(4,128)S(1)}, u32[]{:S(2)}, u32[]{:S(2)}) collective-permute-start(f32[4,512]{1,0:T(4,128)S(1)} %get-tuple-element.62), channel_id=1, source_target_pairs={{0,15},{1,0},{2,1},{3,2},{4,3},{5,4},{6,5},{7,6},{8,7},{9,8},{10,9... | collective-permute-start | bytes 24584 | tf_op jit(solution)/shard_map/ppermute | solution.py:406
  102.1 0.7 copy-start.4

commit v3 on v2

--- a/solution.py
+++ b/solution.py
@@ -20,11 +20,11 @@
 NT = (((1,), (1,)), ((), ()))
 
 
-def call(body, out_shape, n_in, scratch=(), smem=(), remote=(), microseconds=1):
+def call(body, out_shape, n_in, scratch=(), smem=(), remote=(), microseconds=1, vmem=VMEM_LIMIT):
     def place(i):
         if i in smem:
             return pltpu.SMEM
-        return pl.ANY if i in remote else pltpu.VMEM
+        return pltpu.HBM if i in remote else pltpu.VMEM
 
     out_specs = jax.tree.map(lambda _: pl.BlockSpec(memory_space=pltpu.VMEM), out_shape)
     return pl.pallas_call(
@@ -33,7 +33,7 @@
         in_specs=[pl.BlockSpec(memory_space=place(i)) for i in range(n_in)],
         out_specs=out_specs,
         scratch_shapes=list(scratch),
-        compiler_params=pltpu.CompilerParams(vmem_limit_bytes=VMEM_LIMIT),
+        compiler_params=pltpu.CompilerParams(vmem_limit_bytes=vmem),
         cost_estimate=pl.CostEstimate(
             flops=0, bytes_accessed=int(microseconds * 3_000_000), transcendentals=0
         ),
@@ -155,7 +155,6 @@
         1.0, 0.0,
     ).astype(BF16)
     before = jnp.zeros((128, LANES), F32)
-    total = jnp.zeros((10 * PAD_RANKS, LANES), F32)
     for b in range(blocks):
         target = slot_ref[0, b : b + 1, :]
         mine = same(target, 128)
@@ -164,13 +163,15 @@
         )
         rank = jnp.sum(jnp.where(mine, running + before, 0.0), axis=0, keepdims=True).astype(I32) - 1
         before += jnp.broadcast_to(running[:, LANES - 1 :], (128, LANES))
-        rank = jnp.maximum(rank, 0)
-        key = jnp.where(target >= 0, target + (rank & 1) * 128, -1)
-        rank_half = rank >> 1
-        slot_ref[0, b : b + 1, :] = key
-        slot_ref[1, b : b + 1, :] = rank_half
+        slot_ref[1, b : b + 1, :] = jnp.maximum(rank, 0)
+    target, rank = slot_ref[0], slot_ref[1]
+    slot_ref[0] = jnp.where(live, target + (rank & 1) * 128, -1)
+    slot_ref[1] = rank >> 1
+    total = jnp.zeros((10 * PAD_RANKS, LANES), F32)
+    for b in range(blocks):
         total += lax.dot_general(
-            spread_ranks(split, b, rank_half), hot_rows(key, LANES), NT, preferred_element_type=F32
+            spread_ranks(split, b, slot_ref[1, b : b + 1, :]),
+            hot_rows(slot_ref[0, b : b + 1, :], LANES), NT, preferred_element_type=F32,
         )
     sums = joined(total, PAD_RANKS, 5)
     store_slots(out_ref, jnp.concatenate(sums[:3], axis=0), 0, 2)
@@ -193,7 +194,7 @@
 
 
 def owner_middle(
-    recv_ref, start_ref, coef_ref, slot_ref, out_ref, partial_ref, key_hot, seen, split
+    recv_ref, start_ref, coef_ref, slot_ref, yh, xh, yl, xl, out_ref, partial_ref, key_hot, seen, split
 ):
     blocks = start_ref.shape[0]
     unpack(recv_ref, slot_ref, key_hot, seen, blocks)
@@ -214,7 +215,8 @@
     store_slots(out_ref, jnp.concatenate(joined(total, PAD_RANKS, 2), axis=0), 0, 1)
 
 
-def owner_last(recv_ref, coef_ref, slot_ref, partial_ref, out_ref, seen):
+def owner_last(recv_ref, coef_ref, slot_ref, partial_ref, out_ref, token_ref, seen):
+    token_ref[...] = jnp.zeros_like(token_ref)
     blocks = partial_ref.shape[0]
     unpack(recv_ref, slot_ref, None, seen, blocks)
     own, left, right, pull = [coef_ref[i] for i in range(4)]
@@ -265,26 +267,49 @@
         sums_ref[v] = unfold(both)
 
 
-def put_faces(field, refs):
+def pick(odd, yes, no):
+    return jnp.where(odd, yes, no)
+
+
+def parity():
+    return lax.axis_index("flow") % 2 == 1, lax.axis_index("cross") % 2 == 1
+
+
+def y_faces(field):
     rows = field.shape[0]
-    refs[0][...] = field[rows - 8 :]
-    refs[1][...] = field[:8]
-    refs[2][...] = jnp.concatenate([field[i + 7 : i + 8] for i in range(0, rows, 8)], axis=0)
-    refs[3][...] = jnp.concatenate([field[i : i + 1] for i in range(0, rows, 8)], axis=0)
-
-
-def rock_faces(perm_ref, start_ref, a, b, c, d):
-    perm, start = perm_ref[...], start_ref[...]
-    rows = perm.shape[0]
-    for i, field in enumerate((perm, start)):
-        a[i * 8 : i * 8 + 8, :] = field[rows - 8 :]
-        b[i * 8 : i * 8 + 8, :] = field[:8]
-    c[...] = jnp.concatenate(
-        [f[i + 7 : i + 8] for f in (perm, start) for i in range(0, rows, 8)], axis=0
-    )
-    d[...] = jnp.concatenate(
-        [f[i : i + 1] for f in (perm, start) for i in range(0, rows, 8)], axis=0
-    )
+    low = jnp.concatenate([field[i : i + 1] for i in range(0, rows, 8)], axis=0)
+    high = jnp.concatenate([field[i + 7 : i + 8] for i in range(0, rows, 8)], axis=0)
+    return low, high
+
+
+def put_faces(field, refs, place=0):
+    rows = field.shape[0]
+    odd_x, odd_y = parity()
+    x_low, x_high = field[:8], field[rows - 8 :]
+    y_low, y_high = y_faces(field)
+    at_x, at_y = pl.ds(place * 8, 8), pl.ds(place * (rows // 8), rows // 8)
+    refs[0][at_x, :] = pick(odd_x, x_low, x_high)
+    refs[1][at_x, :] = pick(odd_x, x_high, x_low)
+    refs[2][at_y, :] = pick(odd_y, y_low, y_high)
+    refs[3][at_y, :] = pick(odd_y, y_high, y_low)
+
+
+def sides_of(refs, place=0, rows=32):
+    odd_x, odd_y = parity()
+    at_x, at_y = pl.ds(place * 8, 8), pl.ds(place * (rows // 8), rows // 8)
+    x_first, x_second = refs[0][at_x, :], refs[1][at_x, :]
+    y_first, y_second = refs[2][at_y, :], refs[3][at_y, :]
+    return (
+        pick(odd_x, x_first, x_second),
+        pick(odd_x, x_second, x_first),
+        pick(odd_y, y_first, y_second),
+        pick(odd_y, y_second, y_first),
+    )
+
+
+def rock_faces(perm_ref, start_ref, *sides):
+    put_faces(perm_ref[...], sides, 0)
+    put_faces(start_ref[...], sides, 1)
 
 
 def neighbours(field, x_low, x_high, y_low, y_high, ny):
@@ -320,22 +345,22 @@
     scatter_cells(split, 4, cells_ref, sums_ref)
 
 
-def tile_first(edge_ref, hits_ref, cells_ref, perm_ref, start_ref, storage_ref, xl, xh, yl, yh,
+def tile_first(hits_ref, cells_ref, perm_ref, start_ref, storage_ref, yh, xh, yl, xl,
                out_ref, next_ref, sums_ref, faces_ref, a, b, c, d, found):
     rows, nz = perm_ref.shape
     ny = 8
     perm = perm_ref[...]
     start = start_ref[...]
-    nx = rows // ny
-    beside = neighbours(perm, xl[:8], xh[:8], yl[:nx], yh[:nx], ny)
-    around = neighbours(start, xl[8:], xh[8:], yl[nx:], yh[nx:], ny)
+    beside = neighbours(perm, *sides_of((xl, xh, yl, yh), 0), ny)
+    around = neighbours(start, *sides_of((xl, xh, yl, yh), 1), ny)
+    i_flow, i_cross = lax.axis_index("flow"), lax.axis_index("cross")
     row = lax.broadcasted_iota(I32, (rows, nz), 0)
     lane = lax.broadcasted_iota(I32, (rows, nz), 1)
     closed = [
-        (row < ny) & (edge_ref[0] == 0),
-        (row >= rows - ny) & (edge_ref[1] == 0),
-        (row % ny == 0) & (edge_ref[2] == 0),
-        (row % ny == ny - 1) & (edge_ref[3] == 0),
+        (row < ny) & (i_flow == 0),
+        (row >= rows - ny) & (i_flow == lax.axis_size("flow") - 1),
+        (row % ny == 0) & (i_cross == 0),
+        (row % ny == ny - 1) & (i_cross == lax.axis_size("cross") - 1),
         lane == 0,
         lane == nz - 1,
     ]
@@ -362,14 +387,14 @@
 
 
 def flow_in(field, faces_ref, xl, xh, yl, yh):
-    around = neighbours(field, xl[...], xh[...], yl[...], yh[...], 8)
+    around = neighbours(field, *sides_of((xl, xh, yl, yh)), 8)
     total = faces_ref[0] * around[0]
     for i in range(1, 6):
         total += faces_ref[i] * around[i]
     return total
 
 
-def tile_second(now_ref, sums_ref, faces_ref, xl, xh, yl, yh, after, next_ref, a, b, c, d):
+def tile_second(now_ref, sums_ref, faces_ref, yh, xh, yl, xl, after, next_ref, a, b, c, d):
     inflow = flow_in(now_ref[...], faces_ref, xl, xh, yl, yh)
     later = (sums_ref[2] + inflow) * sums_ref[0]
     next_ref[...] = later
@@ -383,7 +408,7 @@
     scatter_cells(split, 2, cells_ref, sums_ref)
 
 
-def tile_third(hits_ref, now_ref, sums_ref, faces_ref, cells_ref, xl, xh, yl, yh,
+def tile_third(hits_ref, now_ref, sums_ref, faces_ref, cells_ref, yh, xh, yl, xl,
                out_ref, next_ref, last_ref, a, b, c, d, found):
     now = now_ref[...]
     inflow = flow_in(now, faces_ref, xl, xh, yl, yh)
@@ -396,23 +421,25 @@
     store_slots(out_ref, found[...], 0, 1)
 
 
-def tile_last(now_ref, last_ref, sums_ref, faces_ref, xl, xh, yl, yh, after, out_ref):
+def tile_last(now_ref, last_ref, sums_ref, faces_ref, yh, xh, yl, xl, after, out_ref):
     inflow = flow_in(now_ref[...], faces_ref, xl, xh, yl, yh)
     out_ref[...] = (last_ref[...] + inflow) * sums_ref[0]
 
 
-def ring(block, axis, step):
+def trade(block, axis, first):
     count = lax.axis_size(axis)
-    return lax.ppermute(block, axis, [(i, (i + step) % count) for i in range(count)])
+    if count == 1:
+        return block
+    way = lambda i: 1 if (i % 2 == 0) == first else -1
+    return lax.ppermute(block, axis, [(i, (i + way(i)) % count) for i in range(count)])
 
 
 def swap(faces):
-    return (
-        ring(faces[0], "flow", 1),
-        ring(faces[1], "flow", -1),
-        ring(faces[2], "cross", 1),
-        ring(faces[3], "cross", -1),
-    )
+    y_first = trade(faces[2], "cross", True)
+    y_second = trade(faces[3], "cross", False)
+    x_first = trade(faces[0], "flow", True)
+    x_second = trade(faces[1], "flow", False)
+    return y_second, x_second, y_first, x_first
 
 
 def deliver(payload):
@@ -423,8 +450,6 @@
     matrix_start, storage, perm, frac_start, frac_store, frac_cond,
     segment_ids, block_counts, hit_tile, hit_cell, hit_weight,
 ):
-    n_flow, n_cross = lax.axis_size("flow"), lax.axis_size("cross")
-    i_flow, i_cross = lax.axis_index("flow"), lax.axis_index("cross")
     blocks = frac_start.shape[0]
     nx, ny, nz = matrix_start.shape
     rows = nx * ny
@@ -432,7 +457,6 @@
     field = shape(rows, nz)
     faces_of = lambda n: (shape(n * ny, nz), shape(n * ny, nz), shape(n * nx, nz), shape(n * nx, nz))
     owned = lambda dtype: pltpu.VMEM((blocks, LANES), dtype)
-    edges = jnp.stack([i_flow, n_flow - 1 - i_flow, i_cross, n_cross - 1 - i_cross]).astype(I32)
 
     hits, coef, slots = call(
         owner_first,
@@ -447,6 +471,7 @@
         smem=(0,),
         remote=range(1, 8),
         microseconds=6,
+        vmem=64 * 1024 * 1024 - 4096,
     )(
         block_counts, frac_start, frac_store, frac_cond, segment_ids,
         hit_tile.reshape(2 * blocks, 128), hit_cell, hit_weight,
@@ -464,25 +489,25 @@
     seen, first, sums, faces, *sides = call(
         tile_first,
         (shape(256, 128), field, shape(4, rows, nz), shape(6, rows, nz)) + faces_of(1),
-        10,
+        9,
         scratch=[found],
-        smem=(0,),
         microseconds=4,
-    )(edges, sums, cells, perm, start, storage, *around)
+    )(sums, cells, perm, start, storage, *around)
     seen = deliver(seen)
     around = swap(sides)
 
     pushed, partial = call(
         owner_middle,
         (shape(256, 128), shape(blocks, LANES)),
-        4,
+        8,
+        remote=range(4, 8),
         scratch=[
             pltpu.VMEM((blocks, LANES, LANES), BF16),
             pltpu.VMEM((2, blocks, LANES), F32),
             pltpu.VMEM((4, blocks, LANES), F32),
         ],
         microseconds=5,
-    )(seen, frac_start, coef, slots)
+    )(seen, frac_start, coef, slots, *around)
     pushed = deliver(pushed)
     second, *sides = call(tile_second, (field,) + faces_of(1), 8, remote=(7,))(
         first, sums, faces, *around, partial
@@ -505,14 +530,14 @@
     )(hits, second, sums, faces, cells, *around)
     seen = deliver(seen)
     around = swap(sides)
-    frac = call(
+    frac, token = call(
         owner_last,
-        shape(blocks, LANES),
+        (shape(blocks, LANES), shape(8, 128)),
         4,
         scratch=[pltpu.VMEM((2, blocks, LANES), F32)],
         microseconds=4,
     )(seen, coef, slots, partial)
-    fourth = call(tile_last, field, 9, remote=(8,))(third, last, sums, faces, *around, frac)
+    fourth = call(tile_last, field, 9)(third, last, sums, faces, *around, token)
     return fourth.reshape(nx, ny, nz), frac
 
 

time: 104 us -> 91.6 us (0.88)
  blocking collectives: 14.2 us -> 0 us
  starting transfers between devices: 54.5 us -> 63.3 us
  local copies, waits for them, and re-layouts: 5.91 us -> 0.03 us
  Pallas kernels: 19.3 us -> 17.9 us
    all_to_all x1 -> x0, blocking collectives: 14.2 us -> none  [deliver(): lax.all_to_all(payload, ('flow', 'cross'), split_axis=0, concat_axis=0, t...]
    unnamed x24 -> x12, local copies, waits for them, and re-layouts: 5.91 us -> 0.03 us
    ppermute x16, starting transfers between devices: 29.2 us -> 34.1 us  [trade(): lax.ppermute(block, axis, [(i, (i + way(i)) % count) for i in range(count)])]
    all_to_all x3 -> x4, starting transfers between devices: 25.3 us -> 29.2 us  [deliver(): lax.all_to_all(payload, ('flow', 'cross'), split_axis=0, concat_axis=0, t...]
    pallas_call x1, Pallas kernels: 5.66 us -> 4.12 us  [on_device(): call(owner_first, (shape(512, 128), shape(5, blocks, LANES), shape(2, blo...]
    ppermute x16, waiting for transfers between devices: 1.41 us -> 2.53 us  [trade(): lax.ppermute(block, axis, [(i, (i + way(i)) % count) for i in range(count)])]
    all_to_all x3 -> x4, waiting for transfers between devices: 6.64 us -> 5.89 us  [deliver(): lax.all_to_all(payload, ('flow', 'cross'), split_axis=0, concat_axis=0, t...]
  transfers between devices with their start and end apart: 19 -> 20, of which waited for: 3 -> 5; matrix products, arithmetic and copies ran while one was open for 0% -> 0% of each run, Pallas kernels for 6% -> 6%
where the time goes in v3:
time: 91.6 us; the launch traced here: 91.2 us
  starting transfers between devices  63.3 us (69%)
  Pallas kernels  17.9 us (20%)
  waiting for transfers between devices  8.43 us (9%)
  between operations  1.5 us (2%)
    ppermute x16, starting transfers between devices, trade(): lax.ppermute(block, axis, [(i, (i + way(i)) % count) for i in range(count)])  34.1 us
    all_to_all x4, starting transfers between devices, deliver(): lax.all_to_all(payload, ('flow', 'cross'), split_axis=0, concat_axis=0, t...  29.2 us
    all_to_all x4, waiting for transfers between devices, deliver(): lax.all_to_all(payload, ('flow', 'cross'), split_axis=0, concat_axis=0, t...  5.89 us
    pallas_call x1, Pallas kernels, on_device(): call(owner_first, (shape(512, 128), shape(5, blocks, LANES), shape(2, blo...  4.12 us
    pallas_call x1, Pallas kernels, on_device(): call(tile_scatter, (shape(4, rows, nz), shape(2, PAD_RANKS, LANES, dtype=...  2.72 us
    pallas_call x1, Pallas kernels, on_device(): call(owner_middle, (shape(256, 128), shape(blocks, LANES)), 8, remote=ran...  2.62 us
    ppermute x16, waiting for transfers between devices, trade(): lax.ppermute(block, axis, [(i, (i + way(i)) % count) for i in range(count)])  2.53 us
    pallas_call x1, Pallas kernels, on_device(): call(tile_first, (shape(256, 128), field, shape(4, rows, nz), shape(6, ro...  2.42 us
  transfers between devices with their start and end apart: 20, of which 5 were waited for; matrix products, arithmetic and copies ran while one was open for 0% of the time, Pallas kernels for 6%

profile of v3, /device:TPU:1, one launch (start us, length us, event | category | flops | bytes accessed | tf_op | source)
XLA Modules:
  0.0 91.2 jit_solution(8159411864340277710)
XLA Ops:
  1.3 4.1 %shard_map.122 = (f32[512,128]{1,0:T(8,128)}, f32[5,24,256]{2,1,0:T(8,128)}, s32[2,24,256]{2,1,0:T(8,128)}) custom-call(s32[1]{0:T(128)S(6)} %copy.13.count_ref, f32[24,256]{1,0:T(8,128)} %start_ref.1, f32[24,256]{1,0:T(8,128)} %store_hbm.1, f32[24,256]{1,0:T(8,128)} %cond_hbm.1, s32[24,256]{1,0:T(8,128)} %seg_hbm.1, s32[48,128]{1,0:T(8,128)} %bitcast.24, ...), custom_call_target="tpu_custom_call" | custom-call | bytes 18000000 | tf_op jit(solution)/shard_map/pallas_call | solution.py:461
  5.4 0.0 copy-start.1
  5.4 0.0 copy-start.2
  5.4 11.5 %all-to-all-start = ((f32[128,4,128]{2,1,0:T(4,128)}), f32[128,4,128]{2,1,0:T(4,128)S(1)}, u32[]{:S(2)}, u32[]{:S(2)}) async-start(f32[128,4,128]{2,1,0:T(4,128)} %bitcast.22), calls=%async_computation | async-start | bytes 524288 | tf_op jit(solution)/shard_map/all_to_all | solution.py:446
  17.0 1.7 %collective-permute-start.1 = (f32[16,512]{1,0:T(8,128)S(1)}, f32[16,512]{1,0:T(8,128)S(1)}, u32[]{:S(2)}, u32[]{:S(2)}) collective-permute-start(f32[16,512]{1,0:T(8,128)S(1)} %get-tuple-element.39), channel_id=1, source_target_pairs={{0,112},{16,32},{32,16},{48,64},{64,48},{80,96},{96,80},{112,0},{1... | collective-permute-start | bytes 98312 | tf_op jit(solution)/shard_map/ppermute | solution.py:434
  18.7 1.4 %collective-permute-start.3 = (f32[16,512]{1,0:T(8,128)S(1)}, f32[16,512]{1,0:T(8,128)S(1)}, u32[]{:S(2)}, u32[]{:S(2)}) collective-permute-start(f32[16,512]{1,0:T(8,128)S(1)} %get-tuple-element.41), channel_id=1, source_target_pairs={{0,16},{16,0},{32,48},{48,32},{64,80},{80,64},{96,112},{112,96},{1... | collective-permute-start | bytes 98312 | tf_op jit(solution)/shard_map/ppermute | solution.py:434
  20.1 5.4 %collective-permute-start = (f32[8,512]{1,0:T(8,128)S(1)}, f32[8,512]{1,0:T(8,128)S(1)}, u32[]{:S(2)}, u32[]{:S(2)}) collective-permute-start(f32[8,512]{1,0:T(8,128)S(1)} %get-tuple-element.38), channel_id=1, source_target_pairs={{0,15},{1,2},{2,1},{3,4},{4,3},{5,6},{6,5},{7,8},{8,7},{9,10},{10,... | collective-permute-start | bytes 49160 | tf_op jit(solution)/shard_map/ppermute | solution.py:434
  25.5 0.0 collective-permute-start.2
  25.5 3.0 %all-to-all-done = f32[128,4,128]{2,1,0:T(4,128)S(1)} async-done(((f32[128,4,128]{2,1,0:T(4,128)}), f32[128,4,128]{2,1,0:T(4,128)S(1)}, u32[]{:S(2)}, u32[]{:S(2)}) %all-to-all-start) | async-done | bytes 262176 | tf_op jit(solution)/shard_map/all_to_all | solution.py:446
  28.5 2.7 %shard_map.123 = (f32[4,32,512]{2,1,0:T(8,128)S(1)}, s32[2,40,256]{2,1,0:T(8,128)S(1)}) custom-call(f32[512,128]{1,0:T(8,128)S(1)} %bitcast.13), custom_call_target="tpu_custom_call" | custom-call | bytes 12000000 | tf_op jit(solution)/shard_map/pallas_call | solution.py:481
  31.2 0.0 collective-permute-done.yh
  31.2 0.0 collective-permute-done.2.yl
  31.2 0.0 collective-permute-done.1.xh
  31.2 0.0 collective-permute-done.3.xl
  31.3 2.4 %shard_map.125 = (f32[256,128]{1,0:T(8,128)}, f32[32,512]{1,0:T(8,128)S(1)}, f32[4,32,512]{2,1,0:T(8,128)S(1)}, f32[6,32,512]{2,1,0:T(8,128)S(1)}, f32[8,512]{1,...) custom-call(f32[4,32,512]{2,1,0:T(8,128)S(1)} %get-tuple-element.36.hits_ref, ...), custom_call_target="tpu_custom_call" | custom-call | bytes 12000000 | tf_op jit(solution)/shard_map/pallas_call | solution.py:489
  33.7 4.3 %all-to-all-start.1 = ((f32[128,2,128]{2,1,0:T(2,128)}), f32[128,2,128]{2,1,0:T(2,128)S(1)}, u32[]{:S(2)}, u32[]{:S(2)}) async-start(f32[128,2,128]{2,1,0:T(2,128)} %bitcast.6), calls=%async_computation.1 | async-start | bytes 262144 | tf_op jit(solution)/shard_map/all_to_all | solution.py:446
  38.0 1.7 %collective-permute-start.5 = (f32[8,512]{1,0:T(8,128)S(1)}, f32[8,512]{1,0:T(8,128)S(1)}, u32[]{:S(2)}, u32[]{:S(2)}) collective-permute-start(f32[8,512]{1,0:T(8,128)S(1)} %get-tuple-element.46), channel_id=1, source_target_pairs={{0,112},{16,32},{32,16},{48,64},{64,48},{80,96},{96,80},{112,0},{1... | collective-permute-start | bytes 49160 | tf_op jit(solution)/shard_map/ppermute | solution.py:434
  39.7 1.4 %collective-permute-start.7 = (f32[8,512]{1,0:T(8,128)S(1)}, f32[8,512]{1,0:T(8,128)S(1)}, u32[]{:S(2)}, u32[]{:S(2)}) collective-permute-start(f32[8,512]{1,0:T(8,128)S(1)} %get-tuple-element.48), channel_id=1, source_target_pairs={{0,16},{16,0},{32,48},{48,32},{64,80},{80,64},{96,112},{112,96},{1... | collective-permute-start | bytes 49160 | tf_op jit(solution)/shard_map/ppermute | solution.py:434
  41.1 5.5 %collective-permute-start.4 = (f32[4,512]{1,0:T(4,128)S(1)}, f32[4,512]{1,0:T(4,128)S(1)}, u32[]{:S(2)}, u32[]{:S(2)}) collective-permute-start(f32[4,512]{1,0:T(4,128)S(1)} %get-tuple-element.45), channel_id=1, source_target_pairs={{0,15},{1,2},{2,1},{3,4},{4,3},{5,6},{6,5},{7,8},{8,7},{9,10},{10,... | collective-permute-start | bytes 24584 | tf_op jit(solution)/shard_map/ppermute | solution.py:434
  46.6 0.0 collective-permute-start.6
  46.6 1.4 %collective-permute-done.4.yh = f32[4,512]{1,0:T(4,128)S(1)} collective-permute-done((f32[4,512]{1,0:T(4,128)S(1)}, f32[4,512]{1,0:T(4,128)S(1)}, u32[]{:S(2)}, u32[]{:S(2)}) %collective-permute-start.4) | collective-permute-done | bytes 8224 | tf_op jit(solution)/shard_map/ppermute | solution.py:434
  48.0 1.1 %collective-permute-done.6.yl = f32[4,512]{1,0:T(4,128)S(1)} collective-permute-done((f32[4,512]{1,0:T(4,128)S(1)}, f32[4,512]{1,0:T(4,128)S(1)}, u32[]{:S(2)}, u32[]{:S(2)}) %collective-permute-start.6) | collective-permute-done | bytes 8224 | tf_op jit(solution)/shard_map/ppermute | solution.py:434
  49.1 0.0 collective-permute-done.5.xh
  49.1 0.0 collective-permute-done.7.xl
  49.1 0.0 all-to-all-done.1
  49.2 2.6 %shard_map.126 = (f32[256,128]{1,0:T(8,128)}, f32[24,256]{1,0:T(8,128)S(1)}) custom-call(f32[256,128]{1,0:T(8,128)S(1)} %bitcast.14, f32[24,256]{1,0:T(8,128)S(1)} %copy-done.4, f32[5,24,256]{2,1,0:T(8,128)S(1)} %copy-done, s32[2,24,256]{2,1,0:T(8,128)S(1)} %copy-done.3, f32[4,512]{1,0:T(4,128)S(1)} %collective-permute-done.4.yh, ...), custom_call_target="tpu_custom_call" | custom-call | bytes 15000000 | tf_op jit(solution)/shard_map/pallas_call | solution.py:499
  51.8 6.9 %all-to-all-start.2 = ((f32[128,2,128]{2,1,0:T(2,128)}), f32[128,2,128]{2,1,0:T(2,128)S(1)}, u32[]{:S(2)}, u32[]{:S(2)}) async-start(f32[128,2,128]{2,1,0:T(2,128)} %bitcast.8), calls=%async_computation.2 | async-start | bytes 262144 | tf_op jit(solution)/shard_map/all_to_all | solution.py:446
  58.7 0.1 shard_map.128
  58.8 1.7 %collective-permute-start.9 = (f32[8,512]{1,0:T(8,128)S(1)}, f32[8,512]{1,0:T(8,128)S(1)}, u32[]{:S(2)}, u32[]{:S(2)}) collective-permute-start(f32[8,512]{1,0:T(8,128)S(1)} %get-tuple-element.56), channel_id=1, source_target_pairs={{0,112},{16,32},{32,16},{48,64},{64,48},{80,96},{96,80},{112,0},{1... | collective-permute-start | bytes 49160 | tf_op jit(solution)/shard_map/ppermute | solution.py:434
  60.5 1.4 %collective-permute-start.11 = (f32[8,512]{1,0:T(8,128)S(1)}, f32[8,512]{1,0:T(8,128)S(1)}, u32[]{:S(2)}, u32[]{:S(2)}) collective-permute-start(f32[8,512]{1,0:T(8,128)S(1)} %get-tuple-element.58), channel_id=1, source_target_pairs={{0,16},{16,0},{32,48},{48,32},{64,80},{80,64},{96,112},{112,96},{1... | collective-permute-start | bytes 49160 | tf_op jit(solution)/shard_map/ppermute | solution.py:434
  61.9 5.4 %collective-permute-start.8 = (f32[4,512]{1,0:T(4,128)S(1)}, f32[4,512]{1,0:T(4,128)S(1)}, u32[]{:S(2)}, u32[]{:S(2)}) collective-permute-start(f32[4,512]{1,0:T(4,128)S(1)} %get-tuple-element.55), channel_id=1, source_target_pairs={{0,15},{1,2},{2,1},{3,4},{4,3},{5,6},{6,5},{7,8},{8,7},{9,10},{10,... | collective-permute-start | bytes 24584 | tf_op jit(solution)/shard_map/ppermute | solution.py:434
  67.3 0.0 collective-permute-start.10
  67.3 1.4 %all-to-all-done.2 = f32[128,2,128]{2,1,0:T(2,128)S(1)} async-done(((f32[128,2,128]{2,1,0:T(2,128)}), f32[128,2,128]{2,1,0:T(2,128)S(1)}, u32[]{:S(2)}, u32[]{:S(2)}) %all-to-all-start.2) | async-done | bytes 131104 | tf_op jit(solution)/shard_map/all_to_all | solution.py:446
  68.7 1.4 %shard_map.127.hits_ref = f32[2,32,512]{2,1,0:T(8,128)S(1)} custom-call(f32[256,128]{1,0:T(8,128)S(1)} %bitcast.15, s32[2,40,256]{2,1,0:T(8,128)S(1)} %get-tuple-element.37.cells_ref), custom_call_target="tpu_custom_call" | custom-call | bytes 9000000 | tf_op jit(solution)/shard_map/pallas_call | solution.py:517
  70.1 0.0 collective-permute-done.8.yh
  70.1 0.0 collective-permute-done.10.yl
  70.1 0.0 collective-permute-done.9.xh
  70.1 0.0 collective-permute-done.11.xl
  70.2 2.3 %shard_map.129 = (f32[256,128]{1,0:T(8,128)}, f32[32,512]{1,0:T(8,128)S(1)}, f32[32,512]{1,0:T(8,128)S(1)}, f32[8,512]{1,0:T(8,128)S(1)}, f32[8,512]{1,0:T(8,128...) custom-call(f32[2,32,512]{2,1,0:T(8,128)S(1)} %shard_map.127.hits_ref, f32[32,512]{1,0:T(8,128)S(1)} %get-tuple-element.54.now_ref, ...), custom_call_target="tpu_custom_call" | custom-call | bytes 12000000 | tf_op jit(solution)/shard_map/pallas_call | solution.py:524
  72.4 6.5 %all-to-all-start.3 = ((f32[128,2,128]{2,1,0:T(2,128)}), f32[128,2,128]{2,1,0:T(2,128)S(1)}, u32[]{:S(2)}, u32[]{:S(2)}) async-start(f32[128,2,128]{2,1,0:T(2,128)} %bitcast.10), calls=%async_computation.3 | async-start | bytes 262144 | tf_op jit(solution)/shard_map/all_to_all | solution.py:446
  78.9 1.7 %collective-permute-start.13 = (f32[8,512]{1,0:T(8,128)S(1)}, f32[8,512]{1,0:T(8,128)S(1)}, u32[]{:S(2)}, u32[]{:S(2)}) collective-permute-start(f32[8,512]{1,0:T(8,128)S(1)} %get-tuple-element.62), channel_id=1, source_target_pairs={{0,112},{16,32},{32,16},{48,64},{64,48},{80,96},{96,80},{112,0},{1... | collective-permute-start | bytes 49160 | tf_op jit(solution)/shard_map/ppermute | solution.py:434
  80.7 1.4 %collective-permute-start.15 = (f32[8,512]{1,0:T(8,128)S(1)}, f32[8,512]{1,0:T(8,128)S(1)}, u32[]{:S(2)}, u32[]{:S(2)}) collective-permute-start(f32[8,512]{1,0:T(8,128)S(1)} %get-tuple-element.64), channel_id=1, source_target_pairs={{0,16},{16,0},{32,48},{48,32},{64,80},{80,64},{96,112},{112,96},{1... | collective-permute-start | bytes 49160 | tf_op jit(solution)/shard_map/ppermute | solution.py:434
  82.0 5.4 %collective-permute-start.12 = (f32[4,512]{1,0:T(4,128)S(1)}, f32[4,512]{1,0:T(4,128)S(1)}, u32[]{:S(2)}, u32[]{:S(2)}) collective-permute-start(f32[4,512]{1,0:T(4,128)S(1)} %get-tuple-element.61), channel_id=1, source_target_pairs={{0,15},{1,2},{2,1},{3,4},{4,3},{5,6},{6,5},{7,8},{8,7},{9,10},{10,... | collective-permute-start | bytes 24584 | tf_op jit(solution)/shard_map/ppermute | solution.py:434
  87.4 1.5 %all-to-all-done.3 = f32[128,2,128]{2,1,0:T(2,128)S(1)} async-done(((f32[128,2,128]{2,1,0:T(2,128)}), f32[128,2,128]{2,1,0:T(2,128)S(1)}, u32[]{:S(2)}, u32[]{:S(2)}) %all-to-all-start.3) | async-done | bytes 131104 | tf_op jit(solution)/shard_map/all_to_all | solution.py:446
  88.9 1.5 %shard_map.130 = (f32[24,256]{1,0:T(8,128)}, f32[8,128]{1,0:T(8,128)S(1)}) custom-call(f32[256,128]{1,0:T(8,128)S(1)} %bitcast.16, f32[5,24,256]{2,1,0:T(8,128)S(1)} %copy-done, s32[2,24,256]{2,1,0:T(8,128)S(1)} %copy-done.3, f32[24,256]{1,0:T(8,128)S(1)} %get-tuple-element.53.after.partial_ref), custom_call_target="tpu_custom_call" | custom-call | bytes 12000000 | tf_op jit(solution)/shard_map/pallas_call | solution.py:533
  90.4 0.0 collective-permute-done.14.yl
  90.4 0.0 collective-permute-done.13.xh
  90.4 0.7 shard_map.131
  (14 shorter events, 0.1 us)
Async XLA Ops:
  5.4 11.5 %copy-start.1 = (f32[4,8,512]{2,1,0:T(8,128)S(1)}, f32[4,8,512]{2,1,0:T(8,128)}, u32[]{:S(2)}) copy-start(f32[4,8,512]{2,1,0:T(8,128)} %param.13) | copy-start | bytes 196612
  5.4 11.5 %copy-start.2 = (f32[4,8,512]{2,1,0:T(8,128)S(1)}, f32[4,8,512]{2,1,0:T(8,128)}, u32[]{:S(2)}) copy-start(f32[4,8,512]{2,1,0:T(8,128)} %param.11) | copy-start | bytes 196612
  5.4 23.1 %all-to-all-start = ((f32[128,4,128]{2,1,0:T(4,128)}), f32[128,4,128]{2,1,0:T(4,128)S(1)}, u32[]{:S(2)}, u32[]{:S(2)}) async-start(f32[128,4,128]{2,1,0:T(4,128)} %bitcast.22), calls=%async_computation | async-start | bytes 524288 | tf_op jit(solution)/shard_map/all_to_all | solution.py:446
  17.0 14.2 %collective-permute-start.1 = (f32[16,512]{1,0:T(8,128)S(1)}, f32[16,512]{1,0:T(8,128)S(1)}, u32[]{:S(2)}, u32[]{:S(2)}) collective-permute-start(f32[16,512]{1,0:T(8,128)S(1)} %get-tuple-element.39), channel_id=1, source_target_pairs={{0,112},{16,32},{32,16},{48,64},{64,48},{80,96},{96,80},{112,0},{1... | collective-permute-start | bytes 98312 | tf_op jit(solution)/shard_map/ppermute | solution.py:434
  18.7 12.5 %collective-permute-start.3 = (f32[16,512]{1,0:T(8,128)S(1)}, f32[16,512]{1,0:T(8,128)S(1)}, u32[]{:S(2)}, u32[]{:S(2)}) collective-permute-start(f32[16,512]{1,0:T(8,128)S(1)} %get-tuple-element.41), channel_id=1, source_target_pairs={{0,16},{16,0},{32,48},{48,32},{64,80},{80,64},{96,112},{112,96},{1... | collective-permute-start | bytes 98312 | tf_op jit(solution)/shard_map/ppermute | solution.py:434
  20.1 11.1 %collective-permute-start = (f32[8,512]{1,0:T(8,128)S(1)}, f32[8,512]{1,0:T(8,128)S(1)}, u32[]{:S(2)}, u32[]{:S(2)}) collective-permute-start(f32[8,512]{1,0:T(8,128)S(1)} %get-tuple-element.38), channel_id=1, source_target_pairs={{0,15},{1,2},{2,1},{3,4},{4,3},{5,6},{6,5},{7,8},{8,7},{9,10},{10,... | collective-permute-start | bytes 49160 | tf_op jit(solution)/shard_map/ppermute | solution.py:434
  25.5 5.7 %collective-permute-start.2 = (f32[8,512]{1,0:T(8,128)S(1)}, f32[8,512]{1,0:T(8,128)S(1)}, u32[]{:S(2)}, u32[]{:S(2)}) collective-permute-start(f32[8,512]{1,0:T(8,128)S(1)} %get-tuple-element.40), channel_id=1, source_target_pairs={{0,1},{1,0},{2,3},{3,2},{4,5},{5,4},{6,7},{7,6},{8,9},{9,8},{10,11... | collective-permute-start | bytes 49160 | tf_op jit(solution)/shard_map/ppermute | solution.py:434
  28.5 2.8 %copy-start.5 = (f32[4,8,512]{2,1,0:T(8,128)S(1)}, f32[4,8,512]{2,1,0:T(8,128)}, u32[]{:S(2)}) copy-start(f32[4,8,512]{2,1,0:T(8,128)} %param.12) | copy-start | bytes 196612
  33.7 15.4 %copy-start = (f32[5,24,256]{2,1,0:T(8,128)S(1)}, f32[5,24,256]{2,1,0:T(8,128)}, u32[]{:S(2)}) copy-start(f32[5,24,256]{2,1,0:T(8,128)} %get-tuple-element.43.coef_ref) | copy-start | bytes 368644
  33.7 15.5 %copy-start.3 = (s32[2,24,256]{2,1,0:T(8,128)S(1)}, s32[2,24,256]{2,1,0:T(8,128)}, u32[]{:S(2)}) copy-start(s32[2,24,256]{2,1,0:T(8,128)} %get-tuple-element.44.slot_ref) | copy-start | bytes 147460
  33.7 15.5 %copy-start.4 = (f32[24,256]{1,0:T(8,128)S(1)}, f32[24,256]{1,0:T(8,128)}, u32[]{:S(2)}) copy-start(f32[24,256]{1,0:T(8,128)} %start_ref.1) | copy-start | bytes 73732
  33.7 15.4 %all-to-all-start.1 = ((f32[128,2,128]{2,1,0:T(2,128)}), f32[128,2,128]{2,1,0:T(2,128)S(1)}, u32[]{:S(2)}, u32[]{:S(2)}) async-start(f32[128,2,128]{2,1,0:T(2,128)} %bitcast.6), calls=%async_computation.1 | async-start | bytes 262144 | tf_op jit(solution)/shard_map/all_to_all | solution.py:446
  38.0 11.1 %collective-permute-start.5 = (f32[8,512]{1,0:T(8,128)S(1)}, f32[8,512]{1,0:T(8,128)S(1)}, u32[]{:S(2)}, u32[]{:S(2)}) collective-permute-start(f32[8,512]{1,0:T(8,128)S(1)} %get-tuple-element.46), channel_id=1, source_target_pairs={{0,112},{16,32},{32,16},{48,64},{64,48},{80,96},{96,80},{112,0},{1... | collective-permute-start | bytes 49160 | tf_op jit(solution)/shard_map/ppermute | solution.py:434
  39.7 9.4 %collective-permute-start.7 = (f32[8,512]{1,0:T(8,128)S(1)}, f32[8,512]{1,0:T(8,128)S(1)}, u32[]{:S(2)}, u32[]{:S(2)}) collective-permute-start(f32[8,512]{1,0:T(8,128)S(1)} %get-tuple-element.48), channel_id=1, source_target_pairs={{0,16},{16,0},{32,48},{48,32},{64,80},{80,64},{96,112},{112,96},{1... | collective-permute-start | bytes 49160 | tf_op jit(solution)/shard_map/ppermute | solution.py:434
  41.1 6.9 %collective-permute-start.4 = (f32[4,512]{1,0:T(4,128)S(1)}, f32[4,512]{1,0:T(4,128)S(1)}, u32[]{:S(2)}, u32[]{:S(2)}) collective-permute-start(f32[4,512]{1,0:T(4,128)S(1)} %get-tuple-element.45), channel_id=1, source_target_pairs={{0,15},{1,2},{2,1},{3,4},{4,3},{5,6},{6,5},{7,8},{8,7},{9,10},{10,... | collective-permute-start | bytes 24584 | tf_op jit(solution)/shard_map/ppermute | solution.py:434
  46.6 2.5 %collective-permute-start.6 = (f32[4,512]{1,0:T(4,128)S(1)}, f32[4,512]{1,0:T(4,128)S(1)}, u32[]{:S(2)}, u32[]{:S(2)}) collective-permute-start(f32[4,512]{1,0:T(4,128)S(1)} %get-tuple-element.47), channel_id=1, source_target_pairs={{0,1},{1,0},{2,3},{3,2},{4,5},{5,4},{6,7},{7,6},{8,9},{9,8},{10,11... | collective-permute-start | bytes 24584 | tf_op jit(solution)/shard_map/ppermute | solution.py:434
  51.8 16.9 %all-to-all-start.2 = ((f32[128,2,128]{2,1,0:T(2,128)}), f32[128,2,128]{2,1,0:T(2,128)S(1)}, u32[]{:S(2)}, u32[]{:S(2)}) async-start(f32[128,2,128]{2,1,0:T(2,128)} %bitcast.8), calls=%async_computation.2 | async-start | bytes 262144 | tf_op jit(solution)/shard_map/all_to_all | solution.py:446
  58.8 11.3 %collective-permute-start.9 = (f32[8,512]{1,0:T(8,128)S(1)}, f32[8,512]{1,0:T(8,128)S(1)}, u32[]{:S(2)}, u32[]{:S(2)}) collective-permute-start(f32[8,512]{1,0:T(8,128)S(1)} %get-tuple-element.56), channel_id=1, source_target_pairs={{0,112},{16,32},{32,16},{48,64},{64,48},{80,96},{96,80},{112,0},{1... | collective-permute-start | bytes 49160 | tf_op jit(solution)/shard_map/ppermute | solution.py:434
  60.5 9.6 %collective-permute-start.11 = (f32[8,512]{1,0:T(8,128)S(1)}, f32[8,512]{1,0:T(8,128)S(1)}, u32[]{:S(2)}, u32[]{:S(2)}) collective-permute-start(f32[8,512]{1,0:T(8,128)S(1)} %get-tuple-element.58), channel_id=1, source_target_pairs={{0,16},{16,0},{32,48},{48,32},{64,80},{80,64},{96,112},{112,96},{1... | collective-permute-start | bytes 49160 | tf_op jit(solution)/shard_map/ppermute | solution.py:434
  61.9 8.2 %collective-permute-start.8 = (f32[4,512]{1,0:T(4,128)S(1)}, f32[4,512]{1,0:T(4,128)S(1)}, u32[]{:S(2)}, u32[]{:S(2)}) collective-permute-start(f32[4,512]{1,0:T(4,128)S(1)} %get-tuple-element.55), channel_id=1, source_target_pairs={{0,15},{1,2},{2,1},{3,4},{4,3},{5,6},{6,5},{7,8},{8,7},{9,10},{10,... | collective-permute-start | bytes 24584 | tf_op jit(solution)/shard_map/ppermute | solution.py:434
  67.3 2.8 %collective-permute-start.10 = (f32[4,512]{1,0:T(4,128)S(1)}, f32[4,512]{1,0:T(4,128)S(1)}, u32[]{:S(2)}, u32[]{:S(2)}) collective-permute-start(f32[4,512]{1,0:T(4,128)S(1)} %get-tuple-element.57), channel_id=1, source_target_pairs={{0,1},{1,0},{2,3},{3,2},{4,5},{5,4},{6,7},{7,6},{8,9},{9,8},{10,11... | collective-permute-start | bytes 24584 | tf_op jit(solution)/shard_map/ppermute | solution.py:434
  72.4 16.5 %all-to-all-start.3 = ((f32[128,2,128]{2,1,0:T(2,128)}), f32[128,2,128]{2,1,0:T(2,128)S(1)}, u32[]{:S(2)}, u32[]{:S(2)}) async-start(f32[128,2,128]{2,1,0:T(2,128)} %bitcast.10), calls=%async_computation.3 | async-start | bytes 262144 | tf_op jit(solution)/shard_map/all_to_all | solution.py:446
  78.9 11.5 %collective-permute-start.13 = (f32[8,512]{1,0:T(8,128)S(1)}, f32[8,512]{1,0:T(8,128)S(1)}, u32[]{:S(2)}, u32[]{:S(2)}) collective-permute-start(f32[8,512]{1,0:T(8,128)S(1)} %get-tuple-element.62), channel_id=1, source_target_pairs={{0,112},{16,32},{32,16},{48,64},{64,48},{80,96},{96,80},{112,0},{1... | collective-permute-start | bytes 49160 | tf_op jit(solution)/shard_map/ppermute | solution.py:434
  80.7 9.8 %collective-permute-start.15 = (f32[8,512]{1,0:T(8,128)S(1)}, f32[8,512]{1,0:T(8,128)S(1)}, u32[]{:S(2)}, u32[]{:S(2)}) collective-permute-start(f32[8,512]{1,0:T(8,128)S(1)} %get-tuple-element.64), channel_id=1, source_target_pairs={{0,16},{16,0},{32,48},{48,32},{64,80},{80,64},{96,112},{112,96},{1... | collective-permute-start | bytes 49160 | tf_op jit(solution)/shard_map/ppermute | solution.py:434
  82.0 8.4 %collective-permute-start.12 = (f32[4,512]{1,0:T(4,128)S(1)}, f32[4,512]{1,0:T(4,128)S(1)}, u32[]{:S(2)}, u32[]{:S(2)}) collective-permute-start(f32[4,512]{1,0:T(4,128)S(1)} %get-tuple-element.61), channel_id=1, source_target_pairs={{0,15},{1,2},{2,1},{3,4},{4,3},{5,6},{6,5},{7,8},{8,7},{9,10},{10,... | collective-permute-start | bytes 24584 | tf_op jit(solution)/shard_map/ppermute | solution.py:434
  87.4 3.0 %collective-permute-start.14 = (f32[4,512]{1,0:T(4,128)S(1)}, f32[4,512]{1,0:T(4,128)S(1)}, u32[]{:S(2)}, u32[]{:S(2)}) collective-permute-start(f32[4,512]{1,0:T(4,128)S(1)} %get-tuple-element.63), channel_id=1, source_target_pairs={{0,1},{1,0},{2,3},{3,2},{4,5},{5,4},{6,7},{7,6},{8,9},{9,8},{10,11... | collective-permute-start | bytes 24584 | tf_op jit(solution)/shard_map/ppermute | solution.py:434

commit v4 on v3

--- a/solution.py
+++ b/solution.py
@@ -194,7 +194,7 @@
 
 
 def owner_middle(
-    recv_ref, start_ref, coef_ref, slot_ref, yh, xh, yl, xl, out_ref, partial_ref, key_hot, seen, split
+    recv_ref, start_ref, coef_ref, slot_ref, x_b, x_a, out_ref, partial_ref, key_hot, seen, split
 ):
     blocks = start_ref.shape[0]
     unpack(recv_ref, slot_ref, key_hot, seen, blocks)
@@ -275,18 +275,22 @@
     return lax.axis_index("flow") % 2 == 1, lax.axis_index("cross") % 2 == 1
 
 
-def y_faces(field):
-    rows = field.shape[0]
-    low = jnp.concatenate([field[i : i + 1] for i in range(0, rows, 8)], axis=0)
-    high = jnp.concatenate([field[i + 7 : i + 8] for i in range(0, rows, 8)], axis=0)
-    return low, high
+def y_layer(field, y):
+    return jnp.concatenate([field[i + y : i + y + 1] for i in range(0, field.shape[0], 8)], axis=0)
+
+
+def widen(layer):
+    rows, nz = layer.shape
+    return jnp.concatenate(
+        [jnp.broadcast_to(layer[i : i + 1], (8, nz)) for i in range(rows)], axis=0
+    )
 
 
 def put_faces(field, refs, place=0):
     rows = field.shape[0]
     odd_x, odd_y = parity()
     x_low, x_high = field[:8], field[rows - 8 :]
-    y_low, y_high = y_faces(field)
+    y_low, y_high = y_layer(field, 0), y_layer(field, 7)
     at_x, at_y = pl.ds(place * 8, 8), pl.ds(place * (rows // 8), rows // 8)
     refs[0][at_x, :] = pick(odd_x, x_low, x_high)
     refs[1][at_x, :] = pick(odd_x, x_high, x_low)
@@ -346,7 +350,7 @@
 
 
 def tile_first(hits_ref, cells_ref, perm_ref, start_ref, storage_ref, yh, xh, yl, xl,
-               out_ref, next_ref, sums_ref, faces_ref, a, b, c, d, found):
+               out_ref, next_ref, sums_ref, faces_ref, known_ref, x_a, x_b, found):
     rows, nz = perm_ref.shape
     ny = 8
     perm = perm_ref[...]
@@ -376,11 +380,28 @@
     inverse = 1.0 / total
     now = (base + inflow + hits_ref[1]) * inverse
     next_ref[...] = now
-    put_faces(now, (a, b, c, d))
     sums_ref[0] = inverse
     sums_ref[1] = base
-    sums_ref[2] = base + hits_ref[2] + start * hits_ref[3]
-    sums_ref[3] = hits_ref[3]
+    sums_ref[2] = hits_ref[3]
+    far, near = jnp.zeros((ny, nz), F32), jnp.zeros((rows // ny, nz), F32)
+    within = neighbours(now, far, far, near, near, ny)
+    inflow = base + hits_ref[2] + start * hits_ref[3]
+    for i in range(6):
+        inflow += faces_ref[i] * within[i]
+    known = inflow * inverse
+    known_ref[...] = known
+    south, north = faces_ref[2] * inverse, faces_ref[3] * inverse
+    spare = jnp.zeros((6, nz), F32)
+    odd_x, _ = parity()
+    sides = []
+    for x, face in ((0, 0), (rows // ny - 1, 1)):
+        at, end = x * ny, x * ny + ny
+        layers = [a[at:end] for a in (now, known, faces_ref[face] * inverse)]
+        sides.append(
+            jnp.concatenate(layers + [south[at : at + 1], north[end - 1 : end], spare], axis=0)
+        )
+    x_a[...] = pick(odd_x, sides[0], sides[1])
+    x_b[...] = pick(odd_x, sides[1], sides[0])
     found[...] = jnp.zeros_like(found)
     gather_cells([start, now], cells_ref, found)
     store_slots(out_ref, found[...], 0, 1)
@@ -394,11 +415,25 @@
     return total
 
 
-def tile_second(now_ref, sums_ref, faces_ref, yh, xh, yl, xl, after, next_ref, a, b, c, d):
-    inflow = flow_in(now_ref[...], faces_ref, xl, xh, yl, yh)
-    later = (sums_ref[2] + inflow) * sums_ref[0]
+def tile_second(known_ref, now_ref, sums_ref, faces_ref, x_b, x_a, after, next_ref, y_a, y_b):
+    odd_x, odd_y = parity()
+    x_low, x_high = pick(odd_x, x_a[...], x_b[...]), pick(odd_x, x_b[...], x_a[...])
+    now, inverse = now_ref[...], sums_ref[0]
+    rows, nz = now.shape
+    idle = jnp.zeros((rows - 16, nz), F32)
+    west, east = faces_ref[0] * inverse, faces_ref[1] * inverse
+    later = known_ref[...] + jnp.concatenate(
+        [west[:8] * x_low[:8], idle, east[rows - 8 :] * x_high[:8]], axis=0
+    )
     next_ref[...] = later
-    put_faces(later, (a, b, c, d))
+    spare = jnp.zeros((2, nz), F32)
+    sides = []
+    for y, face in ((0, 2), (7, 3)):
+        layers = [y_layer(a, y) for a in (now, later, faces_ref[face] * inverse)]
+        corners = [x_low[y : y + 1], x_high[y : y + 1]]
+        sides.append(jnp.concatenate(layers + corners + [spare], axis=0))
+    y_a[...] = pick(odd_y, sides[0], sides[1])
+    y_b[...] = pick(odd_y, sides[1], sides[0])
 
 
 def tile_scatter_again(recv_ref, cells_ref, sums_ref, split):
@@ -408,14 +443,36 @@
     scatter_cells(split, 2, cells_ref, sums_ref)
 
 
-def tile_third(hits_ref, now_ref, sums_ref, faces_ref, cells_ref, yh, xh, yl, xl,
+def tile_third(hits_ref, part_ref, before_ref, sums_ref, faces_ref, cells_ref, y_b, y_a, x_b, x_a,
                out_ref, next_ref, last_ref, a, b, c, d, found):
-    now = now_ref[...]
-    inflow = flow_in(now, faces_ref, xl, xh, yl, yh)
-    later = (sums_ref[1] + inflow + hits_ref[0]) * sums_ref[0]
+    odd_x, odd_y = parity()
+    x_low, x_high = pick(odd_x, x_a[...], x_b[...]), pick(odd_x, x_b[...], x_a[...])
+    y_low, y_high = pick(odd_y, y_a[...], y_b[...]), pick(odd_y, y_b[...], y_a[...])
+    before, inverse = before_ref[...], sums_ref[0]
+    rows, nz = before.shape
+    nx = rows // 8
+    y = lax.broadcasted_iota(I32, (rows, nz), 0) % 8
+    inflow = jnp.where(y == 0, faces_ref[2] * widen(y_low[:nx]), 0.0)
+    inflow += jnp.where(y == 7, faces_ref[3] * widen(y_high[:nx]), 0.0)
+    now = part_ref[...] + inflow * inverse
+    sides = []
+    still = jnp.zeros((6, nz), F32)
+    for i, (side, at) in enumerate(((x_low, 0), (x_high, rows - 8))):
+        corner = slice(3 * nx + i, 3 * nx + i + 1)
+        corners = [side[24:25] * y_low[corner], still, side[25:26] * y_high[corner]]
+        sides.append(
+            side[8:16] + side[16:24] * before[at : at + 8] + jnp.concatenate(corners, axis=0)
+        )
+    for side, at in ((y_low, 0), (y_high, 7)):
+        sides.append(side[nx : 2 * nx] + side[2 * nx : 3 * nx] * y_layer(before, at))
+    around = neighbours(now, *sides, 8)
+    inflow = sums_ref[1] + hits_ref[0]
+    for i in range(6):
+        inflow += faces_ref[i] * around[i]
+    later = inflow * inverse
     next_ref[...] = later
     put_faces(later, (a, b, c, d))
-    last_ref[...] = sums_ref[1] + hits_ref[1] + now * sums_ref[3]
+    last_ref[...] = sums_ref[1] + hits_ref[1] + now * sums_ref[2]
     found[...] = jnp.zeros_like(found)
     gather_cells([now, later], cells_ref, found)
     store_slots(out_ref, found[...], 0, 1)
@@ -486,33 +543,34 @@
         microseconds=4,
     )(hits)
     found = pltpu.VMEM((2 * PAD_RANKS, LANES), F32)
-    seen, first, sums, faces, *sides = call(
+    y_side, x_side = shape(4 * nx, nz), shape(4 * ny, nz)
+    seen, first, sums, faces, known, x_a, x_b = call(
         tile_first,
-        (shape(256, 128), field, shape(4, rows, nz), shape(6, rows, nz)) + faces_of(1),
+        (shape(256, 128), field, shape(3, rows, nz), shape(6, rows, nz), field, x_side, x_side),
         9,
         scratch=[found],
         microseconds=4,
     )(sums, cells, perm, start, storage, *around)
     seen = deliver(seen)
-    around = swap(sides)
+    beside_x = trade(x_b, "flow", False), trade(x_a, "flow", True)
 
     pushed, partial = call(
         owner_middle,
         (shape(256, 128), shape(blocks, LANES)),
-        8,
-        remote=range(4, 8),
+        6,
+        remote=(4, 5),
         scratch=[
             pltpu.VMEM((blocks, LANES, LANES), BF16),
             pltpu.VMEM((2, blocks, LANES), F32),
             pltpu.VMEM((4, blocks, LANES), F32),
         ],
         microseconds=5,
-    )(seen, frac_start, coef, slots, *around)
+    )(seen, frac_start, coef, slots, *beside_x)
     pushed = deliver(pushed)
-    second, *sides = call(tile_second, (field,) + faces_of(1), 8, remote=(7,))(
-        first, sums, faces, *around, partial
-    )
-    around = swap(sides)
+    second, y_a, y_b = call(tile_second, (field, y_side, y_side), 7, remote=(6,))(
+        known, first, sums, faces, *beside_x, partial
+    )
+    beside_y = trade(y_b, "cross", False), trade(y_a, "cross", True)
 
     hits = call(
         tile_scatter_again,
@@ -524,10 +582,10 @@
     seen, third, last, *sides = call(
         tile_third,
         (shape(256, 128), field, field) + faces_of(1),
-        9,
+        10,
         scratch=[found],
         microseconds=4,
-    )(hits, second, sums, faces, cells, *around)
+    )(hits, second, first, sums, faces, cells, *beside_y, *beside_x)
     seen = deliver(seen)
     around = swap(sides)
     frac, token = call(

time: 91.6 us -> 86.9 us (0.949)
  starting transfers between devices: 63.3 us -> 51.2 us
  waiting for transfers between devices: 8.43 us -> 15.8 us
    all_to_all x4, waiting for transfers between devices: 5.89 us -> 14.8 us  [deliver(): lax.all_to_all(payload, ('flow', 'cross'), split_axis=0, concat_axis=0, t...]
    ppermute x16 -> x12, starting transfers between devices: 34.1 us -> 25.7 us  [trade(): lax.ppermute(block, axis, [(i, (i + way(i)) % count) for i in range(count)])]
    all_to_all x4, starting transfers between devices: 29.2 us -> 25.5 us  [deliver(): lax.all_to_all(payload, ('flow', 'cross'), split_axis=0, concat_axis=0, t...]
    ppermute x16 -> x12, waiting for transfers between devices: 2.53 us -> 1.06 us  [trade(): lax.ppermute(block, axis, [(i, (i + way(i)) % count) for i in range(count)])]
  transfers between devices with their start and end apart: 20 -> 16, of which waited for: 5 -> 5; matrix products, arithmetic and copies ran while one was open for 0% -> 0% of each run, Pallas kernels for 6% -> 7%
where the time goes in v4:
time: 86.9 us; the launch traced here: 86.5 us
  starting transfers between devices  51.2 us (59%)
  Pallas kernels  18 us (21%)
  waiting for transfers between devices  15.8 us (18%)
  between operations  1.46 us (2%)
    ppermute x12, starting transfers between devices, trade(): lax.ppermute(block, axis, [(i, (i + way(i)) % count) for i in range(count)])  25.7 us
    all_to_all x4, starting transfers between devices, deliver(): lax.all_to_all(payload, ('flow', 'cross'), split_axis=0, concat_axis=0, t...  25.5 us
    all_to_all x4, waiting for transfers between devices, deliver(): lax.all_to_all(payload, ('flow', 'cross'), split_axis=0, concat_axis=0, t...  14.8 us
    pallas_call x1, Pallas kernels, on_device(): call(owner_first, (shape(512, 128), shape(5, blocks, LANES), shape(2, blo...  4.12 us
    pallas_call x1, Pallas kernels, on_device(): call(tile_scatter, (shape(4, rows, nz), shape(2, PAD_RANKS, LANES, dtype=...  2.72 us
    pallas_call x1, Pallas kernels, on_device(): call(owner_middle, (shape(256, 128), shape(blocks, LANES)), 6, remote=(4,...  2.63 us
    pallas_call x1, Pallas kernels, on_device(): call(tile_first, (shape(256, 128), field, shape(3, rows, nz), shape(6, ro...  2.43 us
    pallas_call x1, Pallas kernels, on_device(): call(tile_third, (shape(256, 128), field, field) + faces_of(1), 10, scrat...  2.34 us
  transfers between devices with their start and end apart: 16, of which 5 were waited for; matrix products, arithmetic and copies ran while one was open for 0% of the time, Pallas kernels for 7%

profile of v4, /device:TPU:1, one launch (start us, length us, event | category | flops | bytes accessed | tf_op | source)
XLA Modules:
  0.0 86.5 jit_solution(359306559281550625)
XLA Ops:
  1.3 4.1 %shard_map.122 = (f32[512,128]{1,0:T(8,128)}, f32[5,24,256]{2,1,0:T(8,128)}, s32[2,24,256]{2,1,0:T(8,128)}) custom-call(s32[1]{0:T(128)S(6)} %copy.13.count_ref, f32[24,256]{1,0:T(8,128)} %start_ref.1, f32[24,256]{1,0:T(8,128)} %store_hbm.1, f32[24,256]{1,0:T(8,128)} %cond_hbm.1, s32[24,256]{1,0:T(8,128)} %seg_hbm.1, s32[48,128]{1,0:T(8,128)} %bitcast.24, ...), custom_call_target="tpu_custom_call" | custom-call | bytes 18000000 | tf_op jit(solution)/shard_map/pallas_call | solution.py:518
  5.4 0.0 copy-start.1
  5.4 0.0 copy-start.2
  5.4 11.5 %all-to-all-start = ((f32[128,4,128]{2,1,0:T(4,128)}), f32[128,4,128]{2,1,0:T(4,128)S(1)}, u32[]{:S(2)}, u32[]{:S(2)}) async-start(f32[128,4,128]{2,1,0:T(4,128)} %bitcast.22), calls=%async_computation | async-start | bytes 524288 | tf_op jit(solution)/shard_map/all_to_all | solution.py:503
  16.9 0.0 copy-done.1
  17.0 0.0 copy-done.2
  17.0 1.7 %collective-permute-start.1 = (f32[16,512]{1,0:T(8,128)S(1)}, f32[16,512]{1,0:T(8,128)S(1)}, u32[]{:S(2)}, u32[]{:S(2)}) collective-permute-start(f32[16,512]{1,0:T(8,128)S(1)} %get-tuple-element.36), channel_id=1, source_target_pairs={{0,112},{16,32},{32,16},{48,64},{64,48},{80,96},{96,80},{112,0},{1... | collective-permute-start | bytes 98312 | tf_op jit(solution)/shard_map/ppermute | solution.py:491
  18.7 1.4 %collective-permute-start.3 = (f32[16,512]{1,0:T(8,128)S(1)}, f32[16,512]{1,0:T(8,128)S(1)}, u32[]{:S(2)}, u32[]{:S(2)}) collective-permute-start(f32[16,512]{1,0:T(8,128)S(1)} %get-tuple-element.38), channel_id=1, source_target_pairs={{0,16},{16,0},{32,48},{48,32},{64,80},{80,64},{96,112},{112,96},{1... | collective-permute-start | bytes 98312 | tf_op jit(solution)/shard_map/ppermute | solution.py:491
  20.1 5.4 %collective-permute-start = (f32[8,512]{1,0:T(8,128)S(1)}, f32[8,512]{1,0:T(8,128)S(1)}, u32[]{:S(2)}, u32[]{:S(2)}) collective-permute-start(f32[8,512]{1,0:T(8,128)S(1)} %get-tuple-element.35), channel_id=1, source_target_pairs={{0,15},{1,2},{2,1},{3,4},{4,3},{5,6},{6,5},{7,8},{8,7},{9,10},{10,... | collective-permute-start | bytes 49160 | tf_op jit(solution)/shard_map/ppermute | solution.py:491
  25.5 0.0 collective-permute-start.2
  25.5 3.0 %all-to-all-done = f32[128,4,128]{2,1,0:T(4,128)S(1)} async-done(((f32[128,4,128]{2,1,0:T(4,128)}), f32[128,4,128]{2,1,0:T(4,128)S(1)}, u32[]{:S(2)}, u32[]{:S(2)}) %all-to-all-start) | async-done | bytes 262176 | tf_op jit(solution)/shard_map/all_to_all | solution.py:503
  28.5 2.7 %shard_map.123 = (f32[4,32,512]{2,1,0:T(8,128)S(1)}, s32[2,40,256]{2,1,0:T(8,128)S(1)}) custom-call(f32[512,128]{1,0:T(8,128)S(1)} %bitcast.13), custom_call_target="tpu_custom_call" | custom-call | bytes 12000000 | tf_op jit(solution)/shard_map/pallas_call | solution.py:538
  31.2 0.0 collective-permute-done.yh
  31.2 0.0 collective-permute-done.2.yl
  31.2 0.0 collective-permute-done.1.xh
  31.2 0.0 collective-permute-done.3.xl
  31.3 0.0 copy-done.5
  31.3 2.4 %shard_map.125 = (f32[256,128]{1,0:T(8,128)}, f32[32,512]{1,0:T(8,128)S(1)}, f32[3,32,512]{2,1,0:T(8,128)S(1)}, f32[6,32,512]{2,1,0:T(8,128)S(1)}, f32[32,512]{1...) custom-call(f32[4,32,512]{2,1,0:T(8,128)S(1)} %get-tuple-element.33.hits_ref, ...), custom_call_target="tpu_custom_call" | custom-call | bytes 12000000 | tf_op jit(solution)/shard_map/pallas_call | solution.py:547
  33.7 4.3 %all-to-all-start.1 = ((f32[128,2,128]{2,1,0:T(2,128)}), f32[128,2,128]{2,1,0:T(2,128)S(1)}, u32[]{:S(2)}, u32[]{:S(2)}) async-start(f32[128,2,128]{2,1,0:T(2,128)} %bitcast.6), calls=%async_computation.1 | async-start | bytes 262144 | tf_op jit(solution)/shard_map/all_to_all | solution.py:503
  38.0 1.7 %collective-permute-start.4 = (f32[32,512]{1,0:T(8,128)S(1)}, f32[32,512]{1,0:T(8,128)S(1)}, u32[]{:S(2)}, u32[]{:S(2)}) collective-permute-start(f32[32,512]{1,0:T(8,128)S(1)} %get-tuple-element.42), channel_id=1, source_target_pairs={{0,112},{16,32},{32,16},{48,64},{64,48},{80,96},{96,80},{112,0},{1... | collective-permute-start | bytes 196616 | tf_op jit(solution)/shard_map/ppermute | solution.py:491
  39.7 1.4 %collective-permute-start.5 = (f32[32,512]{1,0:T(8,128)S(1)}, f32[32,512]{1,0:T(8,128)S(1)}, u32[]{:S(2)}, u32[]{:S(2)}) collective-permute-start(f32[32,512]{1,0:T(8,128)S(1)} %get-tuple-element.43), channel_id=1, source_target_pairs={{0,16},{16,0},{32,48},{48,32},{64,80},{80,64},{96,112},{112,96},{1... | collective-permute-start | bytes 196616 | tf_op jit(solution)/shard_map/ppermute | solution.py:491
  41.1 1.0 %collective-permute-done.4.x_b = f32[32,512]{1,0:T(8,128)S(1)} collective-permute-done((f32[32,512]{1,0:T(8,128)S(1)}, f32[32,512]{1,0:T(8,128)S(1)}, u32[]{:S(2)}, u32[]{:S(2)}) %collective-permute-start.4) | collective-permute-done | bytes 65568 | tf_op jit(solution)/shard_map/ppermute | solution.py:491
  42.1 0.0 collective-permute-done.5.x_a
  42.1 6.0 %all-to-all-done.1 = f32[128,2,128]{2,1,0:T(2,128)S(1)} async-done(((f32[128,2,128]{2,1,0:T(2,128)}), f32[128,2,128]{2,1,0:T(2,128)S(1)}, u32[]{:S(2)}, u32[]{:S(2)}) %all-to-all-start.1) | async-done | bytes 131104 | tf_op jit(solution)/shard_map/all_to_all | solution.py:503
  48.1 0.0 copy-done
  48.1 0.0 copy-done.4
  48.1 2.6 %shard_map.126 = (f32[256,128]{1,0:T(8,128)}, f32[24,256]{1,0:T(8,128)S(1)}) custom-call(f32[256,128]{1,0:T(8,128)S(1)} %bitcast.14, f32[24,256]{1,0:T(8,128)S(1)} %copy-done.4, f32[5,24,256]{2,1,0:T(8,128)S(1)} %copy-done, s32[2,24,256]{2,1,0:T(8,128)S(1)} %copy-done.3, f32[32,512]{1,0:T(8,128)S(1)} %collective-permute-done.4.x_b, ...), custom_call_target="tpu_custom_call" | custom-call | bytes 15000000 | tf_op jit(solution)/shard_map/pallas_call | solution.py:557
  50.8 4.2 %all-to-all-start.2 = ((f32[128,2,128]{2,1,0:T(2,128)}), f32[128,2,128]{2,1,0:T(2,128)S(1)}, u32[]{:S(2)}, u32[]{:S(2)}) async-start(f32[128,2,128]{2,1,0:T(2,128)} %bitcast.8), calls=%async_computation.2 | async-start | bytes 262144 | tf_op jit(solution)/shard_map/all_to_all | solution.py:503
  55.0 0.1 shard_map.128
  55.1 5.6 %collective-permute-start.6 = (f32[16,512]{1,0:T(8,128)S(1)}, f32[16,512]{1,0:T(8,128)S(1)}, u32[]{:S(2)}, u32[]{:S(2)}) collective-permute-start(f32[16,512]{1,0:T(8,128)S(1)} %get-tuple-element.51), channel_id=1, source_target_pairs={{0,15},{1,2},{2,1},{3,4},{4,3},{5,6},{6,5},{7,8},{8,7},{9,10},{10,... | collective-permute-start | bytes 98312 | tf_op jit(solution)/shard_map/ppermute | solution.py:491
  60.7 0.0 collective-permute-start.7
  60.7 4.3 %all-to-all-done.2 = f32[128,2,128]{2,1,0:T(2,128)S(1)} async-done(((f32[128,2,128]{2,1,0:T(2,128)}), f32[128,2,128]{2,1,0:T(2,128)S(1)}, u32[]{:S(2)}, u32[]{:S(2)}) %all-to-all-start.2) | async-done | bytes 131104 | tf_op jit(solution)/shard_map/all_to_all | solution.py:503
  65.0 1.4 %shard_map.127.hits_ref = f32[2,32,512]{2,1,0:T(8,128)S(1)} custom-call(f32[256,128]{1,0:T(8,128)S(1)} %bitcast.16, s32[2,40,256]{2,1,0:T(8,128)S(1)} %get-tuple-element.34.cells_ref), custom_call_target="tpu_custom_call" | custom-call | bytes 9000000 | tf_op jit(solution)/shard_map/pallas_call | solution.py:575
  66.5 0.0 collective-permute-done.6.y_b
  66.5 0.0 collective-permute-done.7.y_a
  66.5 2.3 %shard_map.129 = (f32[256,128]{1,0:T(8,128)}, f32[32,512]{1,0:T(8,128)S(1)}, f32[32,512]{1,0:T(8,128)S(1)}, f32[8,512]{1,0:T(8,128)S(1)}, f32[8,512]{1,0:T(8,128...) custom-call(f32[2,32,512]{2,1,0:T(8,128)S(1)} %shard_map.127.hits_ref, f32[32,512]{1,0:T(8,128)S(1)} %get-tuple-element.50.part_ref, ...), custom_call_target="tpu_custom_call" | custom-call | bytes 12000000 | tf_op jit(solution)/shard_map/pallas_call | solution.py:582
  68.8 5.4 %all-to-all-start.3 = ((f32[128,2,128]{2,1,0:T(2,128)}), f32[128,2,128]{2,1,0:T(2,128)S(1)}, u32[]{:S(2)}, u32[]{:S(2)}) async-start(f32[128,2,128]{2,1,0:T(2,128)} %bitcast.10), calls=%async_computation.3 | async-start | bytes 262144 | tf_op jit(solution)/shard_map/all_to_all | solution.py:503
  74.3 1.7 %collective-permute-start.9 = (f32[8,512]{1,0:T(8,128)S(1)}, f32[8,512]{1,0:T(8,128)S(1)}, u32[]{:S(2)}, u32[]{:S(2)}) collective-permute-start(f32[8,512]{1,0:T(8,128)S(1)} %get-tuple-element.56), channel_id=1, source_target_pairs={{0,112},{16,32},{32,16},{48,64},{64,48},{80,96},{96,80},{112,0},{1... | collective-permute-start | bytes 49160 | tf_op jit(solution)/shard_map/ppermute | solution.py:491
  76.0 1.4 %collective-permute-start.11 = (f32[8,512]{1,0:T(8,128)S(1)}, f32[8,512]{1,0:T(8,128)S(1)}, u32[]{:S(2)}, u32[]{:S(2)}) collective-permute-start(f32[8,512]{1,0:T(8,128)S(1)} %get-tuple-element.58), channel_id=1, source_target_pairs={{0,16},{16,0},{32,48},{48,32},{64,80},{80,64},{96,112},{112,96},{1... | collective-permute-start | bytes 49160 | tf_op jit(solution)/shard_map/ppermute | solution.py:491
  77.3 5.4 %collective-permute-start.8 = (f32[4,512]{1,0:T(4,128)S(1)}, f32[4,512]{1,0:T(4,128)S(1)}, u32[]{:S(2)}, u32[]{:S(2)}) collective-permute-start(f32[4,512]{1,0:T(4,128)S(1)} %get-tuple-element.55), channel_id=1, source_target_pairs={{0,15},{1,2},{2,1},{3,4},{4,3},{5,6},{6,5},{7,8},{8,7},{9,10},{10,... | collective-permute-start | bytes 24584 | tf_op jit(solution)/shard_map/ppermute | solution.py:491
  82.7 0.0 collective-permute-start.10
  82.7 1.5 %all-to-all-done.3 = f32[128,2,128]{2,1,0:T(2,128)S(1)} async-done(((f32[128,2,128]{2,1,0:T(2,128)}), f32[128,2,128]{2,1,0:T(2,128)S(1)}, u32[]{:S(2)}, u32[]{:S(2)}) %all-to-all-start.3) | async-done | bytes 131104 | tf_op jit(solution)/shard_map/all_to_all | solution.py:503
  84.3 1.5 %shard_map.130 = (f32[24,256]{1,0:T(8,128)}, f32[8,128]{1,0:T(8,128)S(1)}) custom-call(f32[256,128]{1,0:T(8,128)S(1)} %bitcast.15, f32[5,24,256]{2,1,0:T(8,128)S(1)} %copy-done, s32[2,24,256]{2,1,0:T(8,128)S(1)} %copy-done.3, f32[24,256]{1,0:T(8,128)S(1)} %get-tuple-element.49.after.partial_ref), custom_call_target="tpu_custom_call" | custom-call | bytes 12000000 | tf_op jit(solution)/shard_map/pallas_call | solution.py:591
  85.7 0.0 collective-permute-done.8.yh
  85.7 0.0 collective-permute-done.10.yl
  85.7 0.0 collective-permute-done.9.xh
  85.7 0.0 collective-permute-done.11.xl
  85.8 0.7 shard_map.131
  (6 shorter events, 0.0 us)
Async XLA Ops:
  5.4 11.5 %copy-start.1 = (f32[4,8,512]{2,1,0:T(8,128)S(1)}, f32[4,8,512]{2,1,0:T(8,128)}, u32[]{:S(2)}) copy-start(f32[4,8,512]{2,1,0:T(8,128)} %param.13) | copy-start | bytes 196612
  5.4 11.5 %copy-start.2 = (f32[4,8,512]{2,1,0:T(8,128)S(1)}, f32[4,8,512]{2,1,0:T(8,128)}, u32[]{:S(2)}) copy-start(f32[4,8,512]{2,1,0:T(8,128)} %param.11) | copy-start | bytes 196612
  5.4 23.1 %all-to-all-start = ((f32[128,4,128]{2,1,0:T(4,128)}), f32[128,4,128]{2,1,0:T(4,128)S(1)}, u32[]{:S(2)}, u32[]{:S(2)}) async-start(f32[128,4,128]{2,1,0:T(4,128)} %bitcast.22), calls=%async_computation | async-start | bytes 524288 | tf_op jit(solution)/shard_map/all_to_all | solution.py:503
  17.0 14.2 %collective-permute-start.1 = (f32[16,512]{1,0:T(8,128)S(1)}, f32[16,512]{1,0:T(8,128)S(1)}, u32[]{:S(2)}, u32[]{:S(2)}) collective-permute-start(f32[16,512]{1,0:T(8,128)S(1)} %get-tuple-element.36), channel_id=1, source_target_pairs={{0,112},{16,32},{32,16},{48,64},{64,48},{80,96},{96,80},{112,0},{1... | collective-permute-start | bytes 98312 | tf_op jit(solution)/shard_map/ppermute | solution.py:491
  18.7 12.5 %collective-permute-start.3 = (f32[16,512]{1,0:T(8,128)S(1)}, f32[16,512]{1,0:T(8,128)S(1)}, u32[]{:S(2)}, u32[]{:S(2)}) collective-permute-start(f32[16,512]{1,0:T(8,128)S(1)} %get-tuple-element.38), channel_id=1, source_target_pairs={{0,16},{16,0},{32,48},{48,32},{64,80},{80,64},{96,112},{112,96},{1... | collective-permute-start | bytes 98312 | tf_op jit(solution)/shard_map/ppermute | solution.py:491
  20.1 11.1 %collective-permute-start = (f32[8,512]{1,0:T(8,128)S(1)}, f32[8,512]{1,0:T(8,128)S(1)}, u32[]{:S(2)}, u32[]{:S(2)}) collective-permute-start(f32[8,512]{1,0:T(8,128)S(1)} %get-tuple-element.35), channel_id=1, source_target_pairs={{0,15},{1,2},{2,1},{3,4},{4,3},{5,6},{6,5},{7,8},{8,7},{9,10},{10,... | collective-permute-start | bytes 49160 | tf_op jit(solution)/shard_map/ppermute | solution.py:491
  25.5 5.7 %collective-permute-start.2 = (f32[8,512]{1,0:T(8,128)S(1)}, f32[8,512]{1,0:T(8,128)S(1)}, u32[]{:S(2)}, u32[]{:S(2)}) collective-permute-start(f32[8,512]{1,0:T(8,128)S(1)} %get-tuple-element.37), channel_id=1, source_target_pairs={{0,1},{1,0},{2,3},{3,2},{4,5},{5,4},{6,7},{7,6},{8,9},{9,8},{10,11... | collective-permute-start | bytes 49160 | tf_op jit(solution)/shard_map/ppermute | solution.py:491
  28.5 2.8 %copy-start.5 = (f32[4,8,512]{2,1,0:T(8,128)S(1)}, f32[4,8,512]{2,1,0:T(8,128)}, u32[]{:S(2)}) copy-start(f32[4,8,512]{2,1,0:T(8,128)} %param.12) | copy-start | bytes 196612
  33.7 14.4 %copy-start = (f32[5,24,256]{2,1,0:T(8,128)S(1)}, f32[5,24,256]{2,1,0:T(8,128)}, u32[]{:S(2)}) copy-start(f32[5,24,256]{2,1,0:T(8,128)} %get-tuple-element.40.coef_ref) | copy-start | bytes 368644
  33.7 14.4 %copy-start.3 = (s32[2,24,256]{2,1,0:T(8,128)S(1)}, s32[2,24,256]{2,1,0:T(8,128)}, u32[]{:S(2)}) copy-start(s32[2,24,256]{2,1,0:T(8,128)} %get-tuple-element.41.slot_ref) | copy-start | bytes 147460
  33.7 14.4 %copy-start.4 = (f32[24,256]{1,0:T(8,128)S(1)}, f32[24,256]{1,0:T(8,128)}, u32[]{:S(2)}) copy-start(f32[24,256]{1,0:T(8,128)} %start_ref.1) | copy-start | bytes 73732
  33.7 14.4 %all-to-all-start.1 = ((f32[128,2,128]{2,1,0:T(2,128)}), f32[128,2,128]{2,1,0:T(2,128)S(1)}, u32[]{:S(2)}, u32[]{:S(2)}) async-start(f32[128,2,128]{2,1,0:T(2,128)} %bitcast.6), calls=%async_computation.1 | async-start | bytes 262144 | tf_op jit(solution)/shard_map/all_to_all | solution.py:503
  38.0 4.1 %collective-permute-start.4 = (f32[32,512]{1,0:T(8,128)S(1)}, f32[32,512]{1,0:T(8,128)S(1)}, u32[]{:S(2)}, u32[]{:S(2)}) collective-permute-start(f32[32,512]{1,0:T(8,128)S(1)} %get-tuple-element.42), channel_id=1, source_target_pairs={{0,112},{16,32},{32,16},{48,64},{64,48},{80,96},{96,80},{112,0},{1... | collective-permute-start | bytes 196616 | tf_op jit(solution)/shard_map/ppermute | solution.py:491
  39.7 2.4 %collective-permute-start.5 = (f32[32,512]{1,0:T(8,128)S(1)}, f32[32,512]{1,0:T(8,128)S(1)}, u32[]{:S(2)}, u32[]{:S(2)}) collective-permute-start(f32[32,512]{1,0:T(8,128)S(1)} %get-tuple-element.43), channel_id=1, source_target_pairs={{0,16},{16,0},{32,48},{48,32},{64,80},{80,64},{96,112},{112,96},{1... | collective-permute-start | bytes 196616 | tf_op jit(solution)/shard_map/ppermute | solution.py:491
  50.8 14.2 %all-to-all-start.2 = ((f32[128,2,128]{2,1,0:T(2,128)}), f32[128,2,128]{2,1,0:T(2,128)S(1)}, u32[]{:S(2)}, u32[]{:S(2)}) async-start(f32[128,2,128]{2,1,0:T(2,128)} %bitcast.8), calls=%async_computation.2 | async-start | bytes 262144 | tf_op jit(solution)/shard_map/all_to_all | solution.py:503
  55.1 11.4 %collective-permute-start.6 = (f32[16,512]{1,0:T(8,128)S(1)}, f32[16,512]{1,0:T(8,128)S(1)}, u32[]{:S(2)}, u32[]{:S(2)}) collective-permute-start(f32[16,512]{1,0:T(8,128)S(1)} %get-tuple-element.51), channel_id=1, source_target_pairs={{0,15},{1,2},{2,1},{3,4},{4,3},{5,6},{6,5},{7,8},{8,7},{9,10},{10,... | collective-permute-start | bytes 98312 | tf_op jit(solution)/shard_map/ppermute | solution.py:491
  60.7 5.7 %collective-permute-start.7 = (f32[16,512]{1,0:T(8,128)S(1)}, f32[16,512]{1,0:T(8,128)S(1)}, u32[]{:S(2)}, u32[]{:S(2)}) collective-permute-start(f32[16,512]{1,0:T(8,128)S(1)} %get-tuple-element.52), channel_id=1, source_target_pairs={{0,1},{1,0},{2,3},{3,2},{4,5},{5,4},{6,7},{7,6},{8,9},{9,8},{10,11... | collective-permute-start | bytes 98312 | tf_op jit(solution)/shard_map/ppermute | solution.py:491
  68.8 15.4 %all-to-all-start.3 = ((f32[128,2,128]{2,1,0:T(2,128)}), f32[128,2,128]{2,1,0:T(2,128)S(1)}, u32[]{:S(2)}, u32[]{:S(2)}) async-start(f32[128,2,128]{2,1,0:T(2,128)} %bitcast.10), calls=%async_computation.3 | async-start | bytes 262144 | tf_op jit(solution)/shard_map/all_to_all | solution.py:503
  74.3 11.5 %collective-permute-start.9 = (f32[8,512]{1,0:T(8,128)S(1)}, f32[8,512]{1,0:T(8,128)S(1)}, u32[]{:S(2)}, u32[]{:S(2)}) collective-permute-start(f32[8,512]{1,0:T(8,128)S(1)} %get-tuple-element.56), channel_id=1, source_target_pairs={{0,112},{16,32},{32,16},{48,64},{64,48},{80,96},{96,80},{112,0},{1... | collective-permute-start | bytes 49160 | tf_op jit(solution)/shard_map/ppermute | solution.py:491
  76.0 9.8 %collective-permute-start.11 = (f32[8,512]{1,0:T(8,128)S(1)}, f32[8,512]{1,0:T(8,128)S(1)}, u32[]{:S(2)}, u32[]{:S(2)}) collective-permute-start(f32[8,512]{1,0:T(8,128)S(1)} %get-tuple-element.58), channel_id=1, source_target_pairs={{0,16},{16,0},{32,48},{48,32},{64,80},{80,64},{96,112},{112,96},{1... | collective-permute-start | bytes 49160 | tf_op jit(solution)/shard_map/ppermute | solution.py:491
  77.3 8.4 %collective-permute-start.8 = (f32[4,512]{1,0:T(4,128)S(1)}, f32[4,512]{1,0:T(4,128)S(1)}, u32[]{:S(2)}, u32[]{:S(2)}) collective-permute-start(f32[4,512]{1,0:T(4,128)S(1)} %get-tuple-element.55), channel_id=1, source_target_pairs={{0,15},{1,2},{2,1},{3,4},{4,3},{5,6},{6,5},{7,8},{8,7},{9,10},{10,... | collective-permute-start | bytes 24584 | tf_op jit(solution)/shard_map/ppermute | solution.py:491
  82.7 3.0 %collective-permute-start.10 = (f32[4,512]{1,0:T(4,128)S(1)}, f32[4,512]{1,0:T(4,128)S(1)}, u32[]{:S(2)}, u32[]{:S(2)}) collective-permute-start(f32[4,512]{1,0:T(4,128)S(1)} %get-tuple-element.57), channel_id=1, source_target_pairs={{0,1},{1,0},{2,3},{3,2},{4,5},{5,4},{6,7},{7,6},{8,9},{9,8},{10,11... | collective-permute-start | bytes 24584 | tf_op jit(solution)/shard_map/ppermute | solution.py:491

commit v5 on v4

--- a/solution.py
+++ b/solution.py
@@ -215,15 +215,6 @@
     store_slots(out_ref, jnp.concatenate(joined(total, PAD_RANKS, 2), axis=0), 0, 1)
 
 
-def owner_last(recv_ref, coef_ref, slot_ref, partial_ref, out_ref, token_ref, seen):
-    token_ref[...] = jnp.zeros_like(token_ref)
-    blocks = partial_ref.shape[0]
-    unpack(recv_ref, slot_ref, None, seen, blocks)
-    own, left, right, pull = [coef_ref[i] for i in range(4)]
-    now = partial_ref[...] + pull * seen[0]
-    out_ref[...] = own + left * shift_right(now) + right * shift_left(now) + pull * seen[1]
-
-
 def fold(field):
     return jnp.concatenate([field[:, :LANES], field[:, LANES:]], axis=0)
 
@@ -296,6 +287,8 @@
     refs[1][at_x, :] = pick(odd_x, x_high, x_low)
     refs[2][at_y, :] = pick(odd_y, y_low, y_high)
     refs[3][at_y, :] = pick(odd_y, y_high, y_low)
+    for ref in refs[2:]:
+        ref[ref.shape[0] - 8 :, :] = jnp.zeros((8, field.shape[1]), F32)
 
 
 def sides_of(refs, place=0, rows=32):
@@ -478,9 +471,15 @@
     store_slots(out_ref, found[...], 0, 1)
 
 
-def tile_last(now_ref, last_ref, sums_ref, faces_ref, yh, xh, yl, xl, after, out_ref):
+def last_pair(recv_ref, coef_ref, slot_ref, partial_ref, now_ref, last_ref, sums_ref, faces_ref,
+              yh, xh, yl, xl, frac_ref, matrix_ref, seen):
     inflow = flow_in(now_ref[...], faces_ref, xl, xh, yl, yh)
-    out_ref[...] = (last_ref[...] + inflow) * sums_ref[0]
+    matrix_ref[...] = (last_ref[...] + inflow) * sums_ref[0]
+    blocks = partial_ref.shape[0]
+    unpack(recv_ref, slot_ref, None, seen, blocks)
+    own, left, right, pull = [coef_ref[i] for i in range(4)]
+    now = partial_ref[...] + pull * seen[0]
+    frac_ref[...] = own + left * shift_right(now) + right * shift_left(now) + pull * seen[1]
 
 
 def trade(block, axis, first):
@@ -512,7 +511,7 @@
     rows = nx * ny
     start, storage, perm = [a.reshape(rows, nz) for a in (matrix_start, storage, perm)]
     field = shape(rows, nz)
-    faces_of = lambda n: (shape(n * ny, nz), shape(n * ny, nz), shape(n * nx, nz), shape(n * nx, nz))
+    faces_of = lambda n: (shape(n * ny, nz),) * 2 + (shape(n * nx + 8, nz),) * 2
     owned = lambda dtype: pltpu.VMEM((blocks, LANES), dtype)
 
     hits, coef, slots = call(
@@ -588,14 +587,13 @@
     )(hits, second, first, sums, faces, cells, *beside_y, *beside_x)
     seen = deliver(seen)
     around = swap(sides)
-    frac, token = call(
-        owner_last,
-        (shape(blocks, LANES), shape(8, 128)),
-        4,
+    frac, fourth = call(
+        last_pair,
+        (shape(blocks, LANES), field),
+        12,
         scratch=[pltpu.VMEM((2, blocks, LANES), F32)],
         microseconds=4,
-    )(seen, coef, slots, partial)
-    fourth = call(tile_last, field, 9)(third, last, sums, faces, *around, token)
+    )(seen, coef, slots, partial, third, last, sums, faces, *around)
     return fourth.reshape(nx, ny, nz), frac
 
 

time: 86.9 us -> 86.2 us (level)
    pallas_call x2 -> x1, Pallas kernels: 2.21 us -> 1.57 us  [on_device(): call(last_pair, (shape(blocks, LANES), field), 12, scratch=[pltpu.VMEM((2...]
  transfers between devices with their start and end apart: 16 -> 16, of which waited for: 5 -> 7; matrix products, arithmetic and copies ran while one was open for 0% -> 0% of each run, Pallas kernels for 7% -> 5%
where the time goes in v5:
time: 86.2 us; the launch traced here: 85.8 us
  starting transfers between devices  51.2 us (59%)
  Pallas kernels  17.3 us (20%)
  waiting for transfers between devices  15.8 us (18%)
  between operations  1.45 us (2%)
    ppermute x12, starting transfers between devices, trade(): lax.ppermute(block, axis, [(i, (i + way(i)) % count) for i in range(count)])  25.7 us
    all_to_all x4, starting transfers between devices, deliver(): lax.all_to_all(payload, ('flow', 'cross'), split_axis=0, concat_axis=0, t...  25.4 us
    all_to_all x4, waiting for transfers between devices, deliver(): lax.all_to_all(payload, ('flow', 'cross'), split_axis=0, concat_axis=0, t...  13.9 us
    pallas_call x1, Pallas kernels, on_device(): call(owner_first, (shape(512, 128), shape(5, blocks, LANES), shape(2, blo...  4.12 us
    pallas_call x1, Pallas kernels, on_device(): call(tile_scatter, (shape(4, rows, nz), shape(2, PAD_RANKS, LANES, dtype=...  2.72 us
    pallas_call x1, Pallas kernels, on_device(): call(owner_middle, (shape(256, 128), shape(blocks, LANES)), 6, remote=(4,...  2.63 us
    pallas_call x1, Pallas kernels, on_device(): call(tile_first, (shape(256, 128), field, shape(3, rows, nz), shape(6, ro...  2.43 us
    pallas_call x1, Pallas kernels, on_device(): call(tile_third, (shape(256, 128), field, field) + faces_of(1), 10, scrat...  2.32 us
  transfers between devices with their start and end apart: 16, of which 7 were waited for; matrix products, arithmetic and copies ran while one was open for 0% of the time, Pallas kernels for 5%

profile of v5, /device:TPU:1, one launch (start us, length us, event | category | flops | bytes accessed | tf_op | source)
XLA Modules:
  0.0 85.8 jit_solution(16584376814895243823)
XLA Ops:
  1.3 4.1 %shard_map.122 = (f32[512,128]{1,0:T(8,128)}, f32[5,24,256]{2,1,0:T(8,128)}, s32[2,24,256]{2,1,0:T(8,128)}) custom-call(s32[1]{0:T(128)S(6)} %copy.13.count_ref, f32[24,256]{1,0:T(8,128)} %start_ref.1, f32[24,256]{1,0:T(8,128)} %store_hbm.1, f32[24,256]{1,0:T(8,128)} %cond_hbm.1, s32[24,256]{1,0:T(8,128)} %seg_hbm.1, s32[48,128]{1,0:T(8,128)} %bitcast.23, ...), custom_call_target="tpu_custom_call" | custom-call | bytes 18000000 | tf_op jit(solution)/shard_map/pallas_call | solution.py:517
  5.4 0.0 copy-start.1
  5.4 0.0 copy-start.2
  5.4 11.5 %all-to-all-start = ((f32[128,4,128]{2,1,0:T(4,128)}), f32[128,4,128]{2,1,0:T(4,128)S(1)}, u32[]{:S(2)}, u32[]{:S(2)}) async-start(f32[128,4,128]{2,1,0:T(4,128)} %bitcast.22), calls=%async_computation | async-start | bytes 524288 | tf_op jit(solution)/shard_map/all_to_all | solution.py:502
  16.9 0.0 copy-done.1
  17.0 0.0 copy-done.2
  17.0 5.6 %collective-permute-start = (f32[16,512]{1,0:T(8,128)S(1)}, f32[16,512]{1,0:T(8,128)S(1)}, u32[]{:S(2)}, u32[]{:S(2)}) collective-permute-start(f32[16,512]{1,0:T(8,128)S(1)} %get-tuple-element.35), channel_id=1, source_target_pairs={{0,15},{1,2},{2,1},{3,4},{4,3},{5,6},{6,5},{7,8},{8,7},{9,10},{10,... | collective-permute-start | bytes 98312 | tf_op jit(solution)/shard_map/ppermute | solution.py:490
  22.6 1.7 %collective-permute-start.1 = (f32[16,512]{1,0:T(8,128)S(1)}, f32[16,512]{1,0:T(8,128)S(1)}, u32[]{:S(2)}, u32[]{:S(2)}) collective-permute-start(f32[16,512]{1,0:T(8,128)S(1)} %get-tuple-element.36), channel_id=1, source_target_pairs={{0,112},{16,32},{32,16},{48,64},{64,48},{80,96},{96,80},{112,0},{1... | collective-permute-start | bytes 98312 | tf_op jit(solution)/shard_map/ppermute | solution.py:490
  24.4 0.0 collective-permute-start.2
  24.4 1.1 %collective-permute-start.3 = (f32[16,512]{1,0:T(8,128)S(1)}, f32[16,512]{1,0:T(8,128)S(1)}, u32[]{:S(2)}, u32[]{:S(2)}) collective-permute-start(f32[16,512]{1,0:T(8,128)S(1)} %get-tuple-element.38), channel_id=1, source_target_pairs={{0,16},{16,0},{32,48},{48,32},{64,80},{80,64},{96,112},{112,96},{1... | collective-permute-start | bytes 98312 | tf_op jit(solution)/shard_map/ppermute | solution.py:490
  25.5 3.0 %all-to-all-done = f32[128,4,128]{2,1,0:T(4,128)S(1)} async-done(((f32[128,4,128]{2,1,0:T(4,128)}), f32[128,4,128]{2,1,0:T(4,128)S(1)}, u32[]{:S(2)}, u32[]{:S(2)}) %all-to-all-start) | async-done | bytes 262176 | tf_op jit(solution)/shard_map/all_to_all | solution.py:502
  28.5 2.7 %shard_map.123 = (f32[4,32,512]{2,1,0:T(8,128)S(1)}, s32[2,40,256]{2,1,0:T(8,128)S(1)}) custom-call(f32[512,128]{1,0:T(8,128)S(1)} %bitcast.13), custom_call_target="tpu_custom_call" | custom-call | bytes 12000000 | tf_op jit(solution)/shard_map/pallas_call | solution.py:537
  31.2 0.0 collective-permute-done.yh
  31.2 0.0 collective-permute-done.1.xh
  31.2 0.0 collective-permute-done.2.yl
  31.2 0.0 collective-permute-done.3.xl
  31.3 0.0 copy-done.5
  31.3 2.4 %shard_map.125 = (f32[256,128]{1,0:T(8,128)}, f32[32,512]{1,0:T(8,128)S(1)}, f32[3,32,512]{2,1,0:T(8,128)S(1)}, f32[6,32,512]{2,1,0:T(8,128)S(1)}, f32[32,512]{1...) custom-call(f32[4,32,512]{2,1,0:T(8,128)S(1)} %get-tuple-element.33.hits_ref, ...), custom_call_target="tpu_custom_call" | custom-call | bytes 12000000 | tf_op jit(solution)/shard_map/pallas_call | solution.py:546
  33.7 4.3 %all-to-all-start.1 = ((f32[128,2,128]{2,1,0:T(2,128)}), f32[128,2,128]{2,1,0:T(2,128)S(1)}, u32[]{:S(2)}, u32[]{:S(2)}) async-start(f32[128,2,128]{2,1,0:T(2,128)} %bitcast.6), calls=%async_computation.1 | async-start | bytes 262144 | tf_op jit(solution)/shard_map/all_to_all | solution.py:502
  38.0 1.7 %collective-permute-start.4 = (f32[32,512]{1,0:T(8,128)S(1)}, f32[32,512]{1,0:T(8,128)S(1)}, u32[]{:S(2)}, u32[]{:S(2)}) collective-permute-start(f32[32,512]{1,0:T(8,128)S(1)} %get-tuple-element.42), channel_id=1, source_target_pairs={{0,112},{16,32},{32,16},{48,64},{64,48},{80,96},{96,80},{112,0},{1... | collective-permute-start | bytes 196616 | tf_op jit(solution)/shard_map/ppermute | solution.py:490
  39.7 1.4 %collective-permute-start.5 = (f32[32,512]{1,0:T(8,128)S(1)}, f32[32,512]{1,0:T(8,128)S(1)}, u32[]{:S(2)}, u32[]{:S(2)}) collective-permute-start(f32[32,512]{1,0:T(8,128)S(1)} %get-tuple-element.43), channel_id=1, source_target_pairs={{0,16},{16,0},{32,48},{48,32},{64,80},{80,64},{96,112},{112,96},{1... | collective-permute-start | bytes 196616 | tf_op jit(solution)/shard_map/ppermute | solution.py:490
  41.1 1.0 %collective-permute-done.4.x_b = f32[32,512]{1,0:T(8,128)S(1)} collective-permute-done((f32[32,512]{1,0:T(8,128)S(1)}, f32[32,512]{1,0:T(8,128)S(1)}, u32[]{:S(2)}, u32[]{:S(2)}) %collective-permute-start.4) | collective-permute-done | bytes 65568 | tf_op jit(solution)/shard_map/ppermute | solution.py:490
  42.1 0.0 collective-permute-done.5.x_a
  42.1 6.0 %all-to-all-done.1 = f32[128,2,128]{2,1,0:T(2,128)S(1)} async-done(((f32[128,2,128]{2,1,0:T(2,128)}), f32[128,2,128]{2,1,0:T(2,128)S(1)}, u32[]{:S(2)}, u32[]{:S(2)}) %all-to-all-start.1) | async-done | bytes 131104 | tf_op jit(solution)/shard_map/all_to_all | solution.py:502
  48.1 0.0 copy-done
  48.1 0.0 copy-done.3
  48.1 0.0 copy-done.4
  48.1 2.6 %shard_map.126 = (f32[256,128]{1,0:T(8,128)}, f32[24,256]{1,0:T(8,128)S(1)}) custom-call(f32[256,128]{1,0:T(8,128)S(1)} %bitcast.15, f32[24,256]{1,0:T(8,128)S(1)} %copy-done.4, f32[5,24,256]{2,1,0:T(8,128)S(1)} %copy-done, s32[2,24,256]{2,1,0:T(8,128)S(1)} %copy-done.3, f32[32,512]{1,0:T(8,128)S(1)} %collective-permute-done.4.x_b, ...), custom_call_target="tpu_custom_call" | custom-call | bytes 15000000 | tf_op jit(solution)/shard_map/pallas_call | solution.py:556
  50.8 4.2 %all-to-all-start.2 = ((f32[128,2,128]{2,1,0:T(2,128)}), f32[128,2,128]{2,1,0:T(2,128)S(1)}, u32[]{:S(2)}, u32[]{:S(2)}) async-start(f32[128,2,128]{2,1,0:T(2,128)} %bitcast.8), calls=%async_computation.2 | async-start | bytes 262144 | tf_op jit(solution)/shard_map/all_to_all | solution.py:502
  55.0 0.1 shard_map.128
  55.1 5.6 %collective-permute-start.6 = (f32[16,512]{1,0:T(8,128)S(1)}, f32[16,512]{1,0:T(8,128)S(1)}, u32[]{:S(2)}, u32[]{:S(2)}) collective-permute-start(f32[16,512]{1,0:T(8,128)S(1)} %get-tuple-element.51), channel_id=1, source_target_pairs={{0,15},{1,2},{2,1},{3,4},{4,3},{5,6},{6,5},{7,8},{8,7},{9,10},{10,... | collective-permute-start | bytes 98312 | tf_op jit(solution)/shard_map/ppermute | solution.py:490
  60.7 0.0 collective-permute-start.7
  60.7 4.3 %all-to-all-done.2 = f32[128,2,128]{2,1,0:T(2,128)S(1)} async-done(((f32[128,2,128]{2,1,0:T(2,128)}), f32[128,2,128]{2,1,0:T(2,128)S(1)}, u32[]{:S(2)}, u32[]{:S(2)}) %all-to-all-start.2) | async-done | bytes 131104 | tf_op jit(solution)/shard_map/all_to_all | solution.py:502
  65.0 1.4 %shard_map.127.hits_ref = f32[2,32,512]{2,1,0:T(8,128)S(1)} custom-call(f32[256,128]{1,0:T(8,128)S(1)} %bitcast.16, s32[2,40,256]{2,1,0:T(8,128)S(1)} %get-tuple-element.34.cells_ref), custom_call_target="tpu_custom_call" | custom-call | bytes 9000000 | tf_op jit(solution)/shard_map/pallas_call | solution.py:574
  66.5 0.0 collective-permute-done.6.y_b
  66.5 0.0 collective-permute-done.7.y_a
  66.5 2.3 %shard_map.129 = (f32[256,128]{1,0:T(8,128)}, f32[32,512]{1,0:T(8,128)S(1)}, f32[32,512]{1,0:T(8,128)S(1)}, f32[8,512]{1,0:T(8,128)S(1)}, f32[8,512]{1,0:T(8,128...) custom-call(f32[2,32,512]{2,1,0:T(8,128)S(1)} %shard_map.127.hits_ref, f32[32,512]{1,0:T(8,128)S(1)} %get-tuple-element.50.part_ref, ...), custom_call_target="tpu_custom_call" | custom-call | bytes 12000000 | tf_op jit(solution)/shard_map/pallas_call | solution.py:581
  68.8 5.4 %all-to-all-start.3 = ((f32[128,2,128]{2,1,0:T(2,128)}), f32[128,2,128]{2,1,0:T(2,128)S(1)}, u32[]{:S(2)}, u32[]{:S(2)}) async-start(f32[128,2,128]{2,1,0:T(2,128)} %bitcast.10), calls=%async_computation.3 | async-start | bytes 262144 | tf_op jit(solution)/shard_map/all_to_all | solution.py:502
  74.2 5.6 %collective-permute-start.8 = (f32[12,512]{1,0:T(8,128)S(1)}, f32[12,512]{1,0:T(8,128)S(1)}, u32[]{:S(2)}, u32[]{:S(2)}) collective-permute-start(f32[12,512]{1,0:T(8,128)S(1)} %get-tuple-element.56), channel_id=1, source_target_pairs={{0,15},{1,2},{2,1},{3,4},{4,3},{5,6},{6,5},{7,8},{8,7},{9,10},{10,... | collective-permute-start | bytes 73736 | tf_op jit(solution)/shard_map/ppermute | solution.py:490
  79.9 0.0 collective-permute-start.10
  79.9 1.7 %collective-permute-start.9 = (f32[8,512]{1,0:T(8,128)S(1)}, f32[8,512]{1,0:T(8,128)S(1)}, u32[]{:S(2)}, u32[]{:S(2)}) collective-permute-start(f32[8,512]{1,0:T(8,128)S(1)} %get-tuple-element.57), channel_id=1, source_target_pairs={{0,112},{16,32},{32,16},{48,64},{64,48},{80,96},{96,80},{112,0},{1... | collective-permute-start | bytes 49160 | tf_op jit(solution)/shard_map/ppermute | solution.py:490
  81.6 1.1 %collective-permute-start.11 = (f32[8,512]{1,0:T(8,128)S(1)}, f32[8,512]{1,0:T(8,128)S(1)}, u32[]{:S(2)}, u32[]{:S(2)}) collective-permute-start(f32[8,512]{1,0:T(8,128)S(1)} %get-tuple-element.59), channel_id=1, source_target_pairs={{0,16},{16,0},{32,48},{48,32},{64,80},{80,64},{96,112},{112,96},{1... | collective-permute-start | bytes 49160 | tf_op jit(solution)/shard_map/ppermute | solution.py:490
  82.7 0.6 collective-permute-done.9.xh
  83.3 0.2 collective-permute-done.11.xl
  83.6 0.0 collective-permute-done.8.yh
  83.6 0.0 collective-permute-done.10.yl
  83.6 0.7 all-to-all-done.3
  84.2 1.6 %shard_map.130 = (f32[24,256]{1,0:T(8,128)}, f32[32,512]{1,0:T(8,128)}) custom-call(f32[256,128]{1,0:T(8,128)S(1)} %bitcast.14, f32[5,24,256]{2,1,0:T(8,128)S(1)} %copy-done, s32[2,24,256]{2,1,0:T(8,128)S(1)} %copy-done.3, f32[24,256]{1,0:T(8,128)S(1)} %get-tuple-element.49.after.partial_ref, f32[32,512]{1,0:T(8,128)S(1)} %get-tuple-element.54.now_ref, ...), custom_call_target="tpu_custom_call" | custom-call | bytes 12000000 | tf_op jit(solution)/shard_map/pallas_call | solution.py:590
  (5 shorter events, 0.0 us)
Async XLA Ops:
  5.4 11.5 %copy-start.1 = (f32[4,8,512]{2,1,0:T(8,128)S(1)}, f32[4,8,512]{2,1,0:T(8,128)}, u32[]{:S(2)}) copy-start(f32[4,8,512]{2,1,0:T(8,128)} %param.13) | copy-start | bytes 196612
  5.4 11.5 %copy-start.2 = (f32[4,8,512]{2,1,0:T(8,128)S(1)}, f32[4,8,512]{2,1,0:T(8,128)}, u32[]{:S(2)}) copy-start(f32[4,8,512]{2,1,0:T(8,128)} %param.11) | copy-start | bytes 196612
  5.4 23.1 %all-to-all-start = ((f32[128,4,128]{2,1,0:T(4,128)}), f32[128,4,128]{2,1,0:T(4,128)S(1)}, u32[]{:S(2)}, u32[]{:S(2)}) async-start(f32[128,4,128]{2,1,0:T(4,128)} %bitcast.22), calls=%async_computation | async-start | bytes 524288 | tf_op jit(solution)/shard_map/all_to_all | solution.py:502
  17.0 14.2 %collective-permute-start = (f32[16,512]{1,0:T(8,128)S(1)}, f32[16,512]{1,0:T(8,128)S(1)}, u32[]{:S(2)}, u32[]{:S(2)}) collective-permute-start(f32[16,512]{1,0:T(8,128)S(1)} %get-tuple-element.35), channel_id=1, source_target_pairs={{0,15},{1,2},{2,1},{3,4},{4,3},{5,6},{6,5},{7,8},{8,7},{9,10},{10,... | collective-permute-start | bytes 98312 | tf_op jit(solution)/shard_map/ppermute | solution.py:490
  22.6 8.6 %collective-permute-start.1 = (f32[16,512]{1,0:T(8,128)S(1)}, f32[16,512]{1,0:T(8,128)S(1)}, u32[]{:S(2)}, u32[]{:S(2)}) collective-permute-start(f32[16,512]{1,0:T(8,128)S(1)} %get-tuple-element.36), channel_id=1, source_target_pairs={{0,112},{16,32},{32,16},{48,64},{64,48},{80,96},{96,80},{112,0},{1... | collective-permute-start | bytes 98312 | tf_op jit(solution)/shard_map/ppermute | solution.py:490
  24.4 6.9 %collective-permute-start.2 = (f32[16,512]{1,0:T(8,128)S(1)}, f32[16,512]{1,0:T(8,128)S(1)}, u32[]{:S(2)}, u32[]{:S(2)}) collective-permute-start(f32[16,512]{1,0:T(8,128)S(1)} %get-tuple-element.37), channel_id=1, source_target_pairs={{0,1},{1,0},{2,3},{3,2},{4,5},{5,4},{6,7},{7,6},{8,9},{9,8},{10,11... | collective-permute-start | bytes 98312 | tf_op jit(solution)/shard_map/ppermute | solution.py:490
  24.4 6.9 %collective-permute-start.3 = (f32[16,512]{1,0:T(8,128)S(1)}, f32[16,512]{1,0:T(8,128)S(1)}, u32[]{:S(2)}, u32[]{:S(2)}) collective-permute-start(f32[16,512]{1,0:T(8,128)S(1)} %get-tuple-element.38), channel_id=1, source_target_pairs={{0,16},{16,0},{32,48},{48,32},{64,80},{80,64},{96,112},{112,96},{1... | collective-permute-start | bytes 98312 | tf_op jit(solution)/shard_map/ppermute | solution.py:490
  28.5 2.8 %copy-start.5 = (f32[4,8,512]{2,1,0:T(8,128)S(1)}, f32[4,8,512]{2,1,0:T(8,128)}, u32[]{:S(2)}) copy-start(f32[4,8,512]{2,1,0:T(8,128)} %param.12) | copy-start | bytes 196612
  33.7 14.4 %copy-start = (f32[5,24,256]{2,1,0:T(8,128)S(1)}, f32[5,24,256]{2,1,0:T(8,128)}, u32[]{:S(2)}) copy-start(f32[5,24,256]{2,1,0:T(8,128)} %get-tuple-element.40.coef_ref) | copy-start | bytes 368644
  33.7 14.4 %copy-start.3 = (s32[2,24,256]{2,1,0:T(8,128)S(1)}, s32[2,24,256]{2,1,0:T(8,128)}, u32[]{:S(2)}) copy-start(s32[2,24,256]{2,1,0:T(8,128)} %get-tuple-element.41.slot_ref) | copy-start | bytes 147460
  33.7 14.4 %copy-start.4 = (f32[24,256]{1,0:T(8,128)S(1)}, f32[24,256]{1,0:T(8,128)}, u32[]{:S(2)}) copy-start(f32[24,256]{1,0:T(8,128)} %start_ref.1) | copy-start | bytes 73732
  33.7 14.4 %all-to-all-start.1 = ((f32[128,2,128]{2,1,0:T(2,128)}), f32[128,2,128]{2,1,0:T(2,128)S(1)}, u32[]{:S(2)}, u32[]{:S(2)}) async-start(f32[128,2,128]{2,1,0:T(2,128)} %bitcast.6), calls=%async_computation.1 | async-start | bytes 262144 | tf_op jit(solution)/shard_map/all_to_all | solution.py:502
  38.0 4.1 %collective-permute-start.4 = (f32[32,512]{1,0:T(8,128)S(1)}, f32[32,512]{1,0:T(8,128)S(1)}, u32[]{:S(2)}, u32[]{:S(2)}) collective-permute-start(f32[32,512]{1,0:T(8,128)S(1)} %get-tuple-element.42), channel_id=1, source_target_pairs={{0,112},{16,32},{32,16},{48,64},{64,48},{80,96},{96,80},{112,0},{1... | collective-permute-start | bytes 196616 | tf_op jit(solution)/shard_map/ppermute | solution.py:490
  39.7 2.4 %collective-permute-start.5 = (f32[32,512]{1,0:T(8,128)S(1)}, f32[32,512]{1,0:T(8,128)S(1)}, u32[]{:S(2)}, u32[]{:S(2)}) collective-permute-start(f32[32,512]{1,0:T(8,128)S(1)} %get-tuple-element.43), channel_id=1, source_target_pairs={{0,16},{16,0},{32,48},{48,32},{64,80},{80,64},{96,112},{112,96},{1... | collective-permute-start | bytes 196616 | tf_op jit(solution)/shard_map/ppermute | solution.py:490
  50.8 14.2 %all-to-all-start.2 = ((f32[128,2,128]{2,1,0:T(2,128)}), f32[128,2,128]{2,1,0:T(2,128)S(1)}, u32[]{:S(2)}, u32[]{:S(2)}) async-start(f32[128,2,128]{2,1,0:T(2,128)} %bitcast.8), calls=%async_computation.2 | async-start | bytes 262144 | tf_op jit(solution)/shard_map/all_to_all | solution.py:502
  55.1 11.4 %collective-permute-start.6 = (f32[16,512]{1,0:T(8,128)S(1)}, f32[16,512]{1,0:T(8,128)S(1)}, u32[]{:S(2)}, u32[]{:S(2)}) collective-permute-start(f32[16,512]{1,0:T(8,128)S(1)} %get-tuple-element.51), channel_id=1, source_target_pairs={{0,15},{1,2},{2,1},{3,4},{4,3},{5,6},{6,5},{7,8},{8,7},{9,10},{10,... | collective-permute-start | bytes 98312 | tf_op jit(solution)/shard_map/ppermute | solution.py:490
  60.7 5.7 %collective-permute-start.7 = (f32[16,512]{1,0:T(8,128)S(1)}, f32[16,512]{1,0:T(8,128)S(1)}, u32[]{:S(2)}, u32[]{:S(2)}) collective-permute-start(f32[16,512]{1,0:T(8,128)S(1)} %get-tuple-element.52), channel_id=1, source_target_pairs={{0,1},{1,0},{2,3},{3,2},{4,5},{5,4},{6,7},{7,6},{8,9},{9,8},{10,11... | collective-permute-start | bytes 98312 | tf_op jit(solution)/shard_map/ppermute | solution.py:490
  68.8 15.4 %all-to-all-start.3 = ((f32[128,2,128]{2,1,0:T(2,128)}), f32[128,2,128]{2,1,0:T(2,128)S(1)}, u32[]{:S(2)}, u32[]{:S(2)}) async-start(f32[128,2,128]{2,1,0:T(2,128)} %bitcast.10), calls=%async_computation.3 | async-start | bytes 262144 | tf_op jit(solution)/shard_map/all_to_all | solution.py:502
  74.2 9.3 %collective-permute-start.8 = (f32[12,512]{1,0:T(8,128)S(1)}, f32[12,512]{1,0:T(8,128)S(1)}, u32[]{:S(2)}, u32[]{:S(2)}) collective-permute-start(f32[12,512]{1,0:T(8,128)S(1)} %get-tuple-element.56), channel_id=1, source_target_pairs={{0,15},{1,2},{2,1},{3,4},{4,3},{5,6},{6,5},{7,8},{8,7},{9,10},{10,... | collective-permute-start | bytes 73736 | tf_op jit(solution)/shard_map/ppermute | solution.py:490
  79.9 3.7 %collective-permute-start.10 = (f32[12,512]{1,0:T(8,128)S(1)}, f32[12,512]{1,0:T(8,128)S(1)}, u32[]{:S(2)}, u32[]{:S(2)}) collective-permute-start(f32[12,512]{1,0:T(8,128)S(1)} %get-tuple-element.58), channel_id=1, source_target_pairs={{0,1},{1,0},{2,3},{3,2},{4,5},{5,4},{6,7},{7,6},{8,9},{9,8},{10,11... | collective-permute-start | bytes 73736 | tf_op jit(solution)/shard_map/ppermute | solution.py:490
  79.9 3.5 %collective-permute-start.9 = (f32[8,512]{1,0:T(8,128)S(1)}, f32[8,512]{1,0:T(8,128)S(1)}, u32[]{:S(2)}, u32[]{:S(2)}) collective-permute-start(f32[8,512]{1,0:T(8,128)S(1)} %get-tuple-element.57), channel_id=1, source_target_pairs={{0,112},{16,32},{32,16},{48,64},{64,48},{80,96},{96,80},{112,0},{1... | collective-permute-start | bytes 49160 | tf_op jit(solution)/shard_map/ppermute | solution.py:490
  81.6 2.0 %collective-permute-start.11 = (f32[8,512]{1,0:T(8,128)S(1)}, f32[8,512]{1,0:T(8,128)S(1)}, u32[]{:S(2)}, u32[]{:S(2)}) collective-permute-start(f32[8,512]{1,0:T(8,128)S(1)} %get-tuple-element.59), channel_id=1, source_target_pairs={{0,16},{16,0},{32,48},{48,32},{64,80},{80,64},{96,112},{112,96},{1... | collective-permute-start | bytes 49160 | tf_op jit(solution)/shard_map/ppermute | solution.py:490

commit v6 on v5

--- a/solution.py
+++ b/solution.py
@@ -483,11 +483,17 @@
 
 
 def trade(block, axis, first):
-    count = lax.axis_size(axis)
-    if count == 1:
+    flow, cross = lax.axis_size("flow"), lax.axis_size("cross")
+    if flow * cross == 1:
         return block
-    way = lambda i: 1 if (i % 2 == 0) == first else -1
-    return lax.ppermute(block, axis, [(i, (i + way(i)) % count) for i in range(count)])
+    step, count = (cross, flow) if axis == "flow" else (1, cross)
+    pairs = []
+    for i in range(flow * cross):
+        at = i // step % count
+        to = at + 1 if (at % 2 == 0) == first else at - 1
+        other = i ^ (1 if axis == "flow" else cross)
+        pairs.append((i, i + (to - at) * step if 0 <= to < count else other))
+    return lax.ppermute(block, ("flow", "cross"), pairs)
 
 
 def swap(faces):

time: 86.2 us -> 85.2 us (0.988)
  starting transfers between devices: 51.2 us -> 39.7 us
  waiting for transfers between devices: 15.8 us -> 26.3 us
    ppermute x12, starting transfers between devices: 25.7 us -> 15.2 us  [trade(): return lax.ppermute(block, ('flow', 'cross'), pairs)]
    all_to_all x4, waiting for transfers between devices: 13.9 us -> 22.8 us  [deliver(): lax.all_to_all(payload, ('flow', 'cross'), split_axis=0, concat_axis=0, t...]
    ppermute x12, waiting for transfers between devices: 1.89 us -> 3.51 us  [trade(): return lax.ppermute(block, ('flow', 'cross'), pairs)]
    all_to_all x4, starting transfers between devices: 25.4 us -> 24.4 us  [deliver(): lax.all_to_all(payload, ('flow', 'cross'), split_axis=0, concat_axis=0, t...]
  transfers between devices with their start and end apart: 16 -> 16, of which waited for: 7 -> 6; matrix products, arithmetic and copies ran while one was open for 0% -> 0% of each run, Pallas kernels for 5% -> 5%
where the time goes in v6:
time: 85.2 us; the launch traced here: 84.8 us
  starting transfers between devices  39.7 us (47%)
  waiting for transfers between devices  26.3 us (31%)
  Pallas kernels  17.3 us (20%)
  between operations  1.45 us (2%)
    all_to_all x4, starting transfers between devices, deliver(): lax.all_to_all(payload, ('flow', 'cross'), split_axis=0, concat_axis=0, t...  24.4 us
    all_to_all x4, waiting for transfers between devices, deliver(): lax.all_to_all(payload, ('flow', 'cross'), split_axis=0, concat_axis=0, t...  22.8 us
    ppermute x12, starting transfers between devices, trade(): return lax.ppermute(block, ('flow', 'cross'), pairs)  15.2 us
    pallas_call x1, Pallas kernels, on_device(): call(owner_first, (shape(512, 128), shape(5, blocks, LANES), shape(2, blo...  4.12 us
    ppermute x12, waiting for transfers between devices, trade(): return lax.ppermute(block, ('flow', 'cross'), pairs)  3.51 us
    pallas_call x1, Pallas kernels, on_device(): call(tile_scatter, (shape(4, rows, nz), shape(2, PAD_RANKS, LANES, dtype=...  2.72 us
    pallas_call x1, Pallas kernels, on_device(): call(owner_middle, (shape(256, 128), shape(blocks, LANES)), 6, remote=(4,...  2.63 us
    pallas_call x1, Pallas kernels, on_device(): call(tile_first, (shape(256, 128), field, shape(3, rows, nz), shape(6, ro...  2.43 us
  transfers between devices with their start and end apart: 16, of which 6 were waited for; matrix products, arithmetic and copies ran while one was open for 0% of the time, Pallas kernels for 5%

profile of v6, /device:TPU:1, one launch (start us, length us, event | category | flops | bytes accessed | tf_op | source)
XLA Modules:
  0.0 84.8 jit_solution(2878595089393126870)
XLA Ops:
  1.3 4.1 %shard_map.122 = (f32[512,128]{1,0:T(8,128)}, f32[5,24,256]{2,1,0:T(8,128)}, s32[2,24,256]{2,1,0:T(8,128)}) custom-call(s32[1]{0:T(128)S(6)} %copy.13.count_ref, f32[24,256]{1,0:T(8,128)} %start_ref.1, f32[24,256]{1,0:T(8,128)} %store_hbm.1, f32[24,256]{1,0:T(8,128)} %cond_hbm.1, s32[24,256]{1,0:T(8,128)} %seg_hbm.1, s32[48,128]{1,0:T(8,128)} %bitcast.23, ...), custom_call_target="tpu_custom_call" | custom-call | bytes 18000000 | tf_op jit(solution)/shard_map/pallas_call | solution.py:523
  5.4 0.0 copy-start.1
  5.4 0.0 copy-start.2
  5.4 11.5 %all-to-all-start = ((f32[128,4,128]{2,1,0:T(4,128)}), f32[128,4,128]{2,1,0:T(4,128)S(1)}, u32[]{:S(2)}, u32[]{:S(2)}) async-start(f32[128,4,128]{2,1,0:T(4,128)} %bitcast.22), calls=%async_computation | async-start | bytes 524288 | tf_op jit(solution)/shard_map/all_to_all | solution.py:508
  16.9 0.0 copy-done.1
  17.0 0.0 copy-done.2
  17.0 1.1 %collective-permute-start = (f32[16,512]{1,0:T(8,128)S(1)}, f32[16,512]{1,0:T(8,128)S(1)}, u32[]{:S(2)}, u32[]{:S(2)}) collective-permute-start(f32[16,512]{1,0:T(8,128)S(1)} %get-tuple-element.35), channel_id=1, source_target_pairs={{0,16},{1,2},{2,1},{3,4},{4,3},{5,6},{6,5},{7,8},{8,7},{9,10},{10,... | collective-permute-start | bytes 98312 | tf_op jit(solution)/shard_map/ppermute | solution.py:496
  18.1 0.7 collective-permute-start.1
  18.9 2.9 %collective-permute-start.2 = (f32[16,512]{1,0:T(8,128)S(1)}, f32[16,512]{1,0:T(8,128)S(1)}, u32[]{:S(2)}, u32[]{:S(2)}) collective-permute-start(f32[16,512]{1,0:T(8,128)S(1)} %get-tuple-element.37), channel_id=1, source_target_pairs={{0,1},{1,0},{2,3},{3,2},{4,5},{5,4},{6,7},{7,6},{8,9},{9,8},{10,11... | collective-permute-start | bytes 98312 | tf_op jit(solution)/shard_map/ppermute | solution.py:496
  21.8 0.0 collective-permute-start.3
  21.8 6.7 %all-to-all-done = f32[128,4,128]{2,1,0:T(4,128)S(1)} async-done(((f32[128,4,128]{2,1,0:T(4,128)}), f32[128,4,128]{2,1,0:T(4,128)S(1)}, u32[]{:S(2)}, u32[]{:S(2)}) %all-to-all-start) | async-done | bytes 262176 | tf_op jit(solution)/shard_map/all_to_all | solution.py:508
  28.5 2.7 %shard_map.123 = (f32[4,32,512]{2,1,0:T(8,128)S(1)}, s32[2,40,256]{2,1,0:T(8,128)S(1)}) custom-call(f32[512,128]{1,0:T(8,128)S(1)} %bitcast.13), custom_call_target="tpu_custom_call" | custom-call | bytes 12000000 | tf_op jit(solution)/shard_map/pallas_call | solution.py:543
  31.2 0.0 collective-permute-done.yh
  31.2 0.0 collective-permute-done.1.xh
  31.2 0.0 collective-permute-done.2.yl
  31.2 0.0 collective-permute-done.3.xl
  31.3 0.0 copy-done.5
  31.3 2.4 %shard_map.125 = (f32[256,128]{1,0:T(8,128)}, f32[32,512]{1,0:T(8,128)S(1)}, f32[3,32,512]{2,1,0:T(8,128)S(1)}, f32[6,32,512]{2,1,0:T(8,128)S(1)}, f32[32,512]{1...) custom-call(f32[4,32,512]{2,1,0:T(8,128)S(1)} %get-tuple-element.33.hits_ref, ...), custom_call_target="tpu_custom_call" | custom-call | bytes 12000000 | tf_op jit(solution)/shard_map/pallas_call | solution.py:552
  33.7 4.3 %all-to-all-start.1 = ((f32[128,2,128]{2,1,0:T(2,128)}), f32[128,2,128]{2,1,0:T(2,128)S(1)}, u32[]{:S(2)}, u32[]{:S(2)}) async-start(f32[128,2,128]{2,1,0:T(2,128)} %bitcast.6), calls=%async_computation.1 | async-start | bytes 262144 | tf_op jit(solution)/shard_map/all_to_all | solution.py:508
  38.0 1.7 %collective-permute-start.4 = (f32[32,512]{1,0:T(8,128)S(1)}, f32[32,512]{1,0:T(8,128)S(1)}, u32[]{:S(2)}, u32[]{:S(2)}) collective-permute-start(f32[32,512]{1,0:T(8,128)S(1)} %get-tuple-element.42), channel_id=1, source_target_pairs={{0,1},{1,0},{2,3},{3,2},{4,5},{5,4},{6,7},{7,6},{8,9},{9,8},{10,11... | collective-permute-start | bytes 196616 | tf_op jit(solution)/shard_map/ppermute | solution.py:496
  39.7 0.6 collective-permute-start.5
  40.4 1.8 %collective-permute-done.4.x_b = f32[32,512]{1,0:T(8,128)S(1)} collective-permute-done((f32[32,512]{1,0:T(8,128)S(1)}, f32[32,512]{1,0:T(8,128)S(1)}, u32[]{:S(2)}, u32[]{:S(2)}) %collective-permute-start.4) | collective-permute-done | bytes 65568 | tf_op jit(solution)/shard_map/ppermute | solution.py:496
  42.1 0.0 collective-permute-done.5.x_a
  42.1 6.0 %all-to-all-done.1 = f32[128,2,128]{2,1,0:T(2,128)S(1)} async-done(((f32[128,2,128]{2,1,0:T(2,128)}), f32[128,2,128]{2,1,0:T(2,128)S(1)}, u32[]{:S(2)}, u32[]{:S(2)}) %all-to-all-start.1) | async-done | bytes 131104 | tf_op jit(solution)/shard_map/all_to_all | solution.py:508
  48.1 0.0 copy-done
  48.1 0.0 copy-done.3
  48.1 0.0 copy-done.4
  48.1 2.6 %shard_map.126 = (f32[256,128]{1,0:T(8,128)}, f32[24,256]{1,0:T(8,128)S(1)}) custom-call(f32[256,128]{1,0:T(8,128)S(1)} %bitcast.15, f32[24,256]{1,0:T(8,128)S(1)} %copy-done.4, f32[5,24,256]{2,1,0:T(8,128)S(1)} %copy-done, s32[2,24,256]{2,1,0:T(8,128)S(1)} %copy-done.3, f32[32,512]{1,0:T(8,128)S(1)} %collective-permute-done.4.x_b, ...), custom_call_target="tpu_custom_call" | custom-call | bytes 15000000 | tf_op jit(solution)/shard_map/pallas_call | solution.py:562
  50.8 4.2 %all-to-all-start.2 = ((f32[128,2,128]{2,1,0:T(2,128)}), f32[128,2,128]{2,1,0:T(2,128)S(1)}, u32[]{:S(2)}, u32[]{:S(2)}) async-start(f32[128,2,128]{2,1,0:T(2,128)} %bitcast.8), calls=%async_computation.2 | async-start | bytes 262144 | tf_op jit(solution)/shard_map/all_to_all | solution.py:508
  55.0 0.1 shard_map.128
  55.0 1.2 %collective-permute-start.6 = (f32[16,512]{1,0:T(8,128)S(1)}, f32[16,512]{1,0:T(8,128)S(1)}, u32[]{:S(2)}, u32[]{:S(2)}) collective-permute-start(f32[16,512]{1,0:T(8,128)S(1)} %get-tuple-element.51), channel_id=1, source_target_pairs={{0,16},{1,2},{2,1},{3,4},{4,3},{5,6},{6,5},{7,8},{8,7},{9,10},{10,... | collective-permute-start | bytes 98312 | tf_op jit(solution)/shard_map/ppermute | solution.py:496
  56.2 1.9 %collective-permute-start.7 = (f32[16,512]{1,0:T(8,128)S(1)}, f32[16,512]{1,0:T(8,128)S(1)}, u32[]{:S(2)}, u32[]{:S(2)}) collective-permute-start(f32[16,512]{1,0:T(8,128)S(1)} %get-tuple-element.52), channel_id=1, source_target_pairs={{0,1},{1,0},{2,3},{3,2},{4,5},{5,4},{6,7},{7,6},{8,9},{9,8},{10,11... | collective-permute-start | bytes 98312 | tf_op jit(solution)/shard_map/ppermute | solution.py:496
  58.1 6.9 %all-to-all-done.2 = f32[128,2,128]{2,1,0:T(2,128)S(1)} async-done(((f32[128,2,128]{2,1,0:T(2,128)}), f32[128,2,128]{2,1,0:T(2,128)S(1)}, u32[]{:S(2)}, u32[]{:S(2)}) %all-to-all-start.2) | async-done | bytes 131104 | tf_op jit(solution)/shard_map/all_to_all | solution.py:508
  65.0 1.4 %shard_map.127.hits_ref = f32[2,32,512]{2,1,0:T(8,128)S(1)} custom-call(f32[256,128]{1,0:T(8,128)S(1)} %bitcast.16, s32[2,40,256]{2,1,0:T(8,128)S(1)} %get-tuple-element.34.cells_ref), custom_call_target="tpu_custom_call" | custom-call | bytes 9000000 | tf_op jit(solution)/shard_map/pallas_call | solution.py:580
  66.4 0.0 collective-permute-done.6.y_b
  66.4 0.0 collective-permute-done.7.y_a
  66.4 2.3 %shard_map.129 = (f32[256,128]{1,0:T(8,128)}, f32[32,512]{1,0:T(8,128)S(1)}, f32[32,512]{1,0:T(8,128)S(1)}, f32[8,512]{1,0:T(8,128)S(1)}, f32[8,512]{1,0:T(8,128...) custom-call(f32[2,32,512]{2,1,0:T(8,128)S(1)} %shard_map.127.hits_ref, f32[32,512]{1,0:T(8,128)S(1)} %get-tuple-element.50.part_ref, ...), custom_call_target="tpu_custom_call" | custom-call | bytes 12000000 | tf_op jit(solution)/shard_map/pallas_call | solution.py:587
  68.8 4.5 %all-to-all-start.3 = ((f32[128,2,128]{2,1,0:T(2,128)}), f32[128,2,128]{2,1,0:T(2,128)S(1)}, u32[]{:S(2)}, u32[]{:S(2)}) async-start(f32[128,2,128]{2,1,0:T(2,128)} %bitcast.10), calls=%async_computation.3 | async-start | bytes 262144 | tf_op jit(solution)/shard_map/all_to_all | solution.py:508
  73.2 1.1 %collective-permute-start.8 = (f32[12,512]{1,0:T(8,128)S(1)}, f32[12,512]{1,0:T(8,128)S(1)}, u32[]{:S(2)}, u32[]{:S(2)}) collective-permute-start(f32[12,512]{1,0:T(8,128)S(1)} %get-tuple-element.56), channel_id=1, source_target_pairs={{0,16},{1,2},{2,1},{3,4},{4,3},{5,6},{6,5},{7,8},{8,7},{9,10},{10,... | collective-permute-start | bytes 73736 | tf_op jit(solution)/shard_map/ppermute | solution.py:496
  74.4 1.9 %collective-permute-start.10 = (f32[12,512]{1,0:T(8,128)S(1)}, f32[12,512]{1,0:T(8,128)S(1)}, u32[]{:S(2)}, u32[]{:S(2)}) collective-permute-start(f32[12,512]{1,0:T(8,128)S(1)} %get-tuple-element.58), channel_id=1, source_target_pairs={{0,1},{1,0},{2,3},{3,2},{4,5},{5,4},{6,7},{7,6},{8,9},{9,8},{10,11... | collective-permute-start | bytes 73736 | tf_op jit(solution)/shard_map/ppermute | solution.py:496
  76.3 2.0 %collective-permute-start.9 = (f32[8,512]{1,0:T(8,128)S(1)}, f32[8,512]{1,0:T(8,128)S(1)}, u32[]{:S(2)}, u32[]{:S(2)}) collective-permute-start(f32[8,512]{1,0:T(8,128)S(1)} %get-tuple-element.57), channel_id=1, source_target_pairs={{0,1},{1,0},{2,3},{3,2},{4,5},{5,4},{6,7},{7,6},{8,9},{9,8},{10,11... | collective-permute-start | bytes 49160 | tf_op jit(solution)/shard_map/ppermute | solution.py:496
  78.3 0.0 collective-permute-start.11
  78.3 1.7 %collective-permute-done.9.xh = f32[8,512]{1,0:T(8,128)S(1)} collective-permute-done((f32[8,512]{1,0:T(8,128)S(1)}, f32[8,512]{1,0:T(8,128)S(1)}, u32[]{:S(2)}, u32[]{:S(2)}) %collective-permute-start.9) | collective-permute-done | bytes 16416 | tf_op jit(solution)/shard_map/ppermute | solution.py:496
  80.0 0.0 collective-permute-done.11.xl
  80.0 0.0 collective-permute-done.8.yh
  80.0 0.0 collective-permute-done.10.yl
  80.0 3.2 %all-to-all-done.3 = f32[128,2,128]{2,1,0:T(2,128)S(1)} async-done(((f32[128,2,128]{2,1,0:T(2,128)}), f32[128,2,128]{2,1,0:T(2,128)S(1)}, u32[]{:S(2)}, u32[]{:S(2)}) %all-to-all-start.3) | async-done | bytes 131104 | tf_op jit(solution)/shard_map/all_to_all | solution.py:508
  83.2 1.6 %shard_map.130 = (f32[24,256]{1,0:T(8,128)}, f32[32,512]{1,0:T(8,128)}) custom-call(f32[256,128]{1,0:T(8,128)S(1)} %bitcast.14, f32[5,24,256]{2,1,0:T(8,128)S(1)} %copy-done, s32[2,24,256]{2,1,0:T(8,128)S(1)} %copy-done.3, f32[24,256]{1,0:T(8,128)S(1)} %get-tuple-element.49.after.partial_ref, f32[32,512]{1,0:T(8,128)S(1)} %get-tuple-element.54.now_ref, ...), custom_call_target="tpu_custom_call" | custom-call | bytes 12000000 | tf_op jit(solution)/shard_map/pallas_call | solution.py:596
  (5 shorter events, 0.0 us)
Async XLA Ops:
  5.4 11.5 %copy-start.1 = (f32[4,8,512]{2,1,0:T(8,128)S(1)}, f32[4,8,512]{2,1,0:T(8,128)}, u32[]{:S(2)}) copy-start(f32[4,8,512]{2,1,0:T(8,128)} %param.13) | copy-start | bytes 196612
  5.4 11.5 %copy-start.2 = (f32[4,8,512]{2,1,0:T(8,128)S(1)}, f32[4,8,512]{2,1,0:T(8,128)}, u32[]{:S(2)}) copy-start(f32[4,8,512]{2,1,0:T(8,128)} %param.11) | copy-start | bytes 196612
  5.4 23.1 %all-to-all-start = ((f32[128,4,128]{2,1,0:T(4,128)}), f32[128,4,128]{2,1,0:T(4,128)S(1)}, u32[]{:S(2)}, u32[]{:S(2)}) async-start(f32[128,4,128]{2,1,0:T(4,128)} %bitcast.22), calls=%async_computation | async-start | bytes 524288 | tf_op jit(solution)/shard_map/all_to_all | solution.py:508
  17.0 14.2 %collective-permute-start = (f32[16,512]{1,0:T(8,128)S(1)}, f32[16,512]{1,0:T(8,128)S(1)}, u32[]{:S(2)}, u32[]{:S(2)}) collective-permute-start(f32[16,512]{1,0:T(8,128)S(1)} %get-tuple-element.35), channel_id=1, source_target_pairs={{0,16},{1,2},{2,1},{3,4},{4,3},{5,6},{6,5},{7,8},{8,7},{9,10},{10,... | collective-permute-start | bytes 98312 | tf_op jit(solution)/shard_map/ppermute | solution.py:496
  18.1 13.1 %collective-permute-start.1 = (f32[16,512]{1,0:T(8,128)S(1)}, f32[16,512]{1,0:T(8,128)S(1)}, u32[]{:S(2)}, u32[]{:S(2)}) collective-permute-start(f32[16,512]{1,0:T(8,128)S(1)} %get-tuple-element.36), channel_id=1, source_target_pairs={{0,1},{1,0},{2,3},{3,2},{4,5},{5,4},{6,7},{7,6},{8,9},{9,8},{10,11... | collective-permute-start | bytes 98312 | tf_op jit(solution)/shard_map/ppermute | solution.py:496
  18.9 12.4 %collective-permute-start.2 = (f32[16,512]{1,0:T(8,128)S(1)}, f32[16,512]{1,0:T(8,128)S(1)}, u32[]{:S(2)}, u32[]{:S(2)}) collective-permute-start(f32[16,512]{1,0:T(8,128)S(1)} %get-tuple-element.37), channel_id=1, source_target_pairs={{0,1},{1,0},{2,3},{3,2},{4,5},{5,4},{6,7},{7,6},{8,9},{9,8},{10,11... | collective-permute-start | bytes 98312 | tf_op jit(solution)/shard_map/ppermute | solution.py:496
  21.8 9.5 %collective-permute-start.3 = (f32[16,512]{1,0:T(8,128)S(1)}, f32[16,512]{1,0:T(8,128)S(1)}, u32[]{:S(2)}, u32[]{:S(2)}) collective-permute-start(f32[16,512]{1,0:T(8,128)S(1)} %get-tuple-element.38), channel_id=1, source_target_pairs={{0,16},{1,17},{2,18},{3,19},{4,20},{5,21},{6,22},{7,23},{8,24},{9,... | collective-permute-start | bytes 98312 | tf_op jit(solution)/shard_map/ppermute | solution.py:496
  28.5 2.8 %copy-start.5 = (f32[4,8,512]{2,1,0:T(8,128)S(1)}, f32[4,8,512]{2,1,0:T(8,128)}, u32[]{:S(2)}) copy-start(f32[4,8,512]{2,1,0:T(8,128)} %param.12) | copy-start | bytes 196612
  33.7 14.4 %copy-start = (f32[5,24,256]{2,1,0:T(8,128)S(1)}, f32[5,24,256]{2,1,0:T(8,128)}, u32[]{:S(2)}) copy-start(f32[5,24,256]{2,1,0:T(8,128)} %get-tuple-element.40.coef_ref) | copy-start | bytes 368644
  33.7 14.4 %copy-start.3 = (s32[2,24,256]{2,1,0:T(8,128)S(1)}, s32[2,24,256]{2,1,0:T(8,128)}, u32[]{:S(2)}) copy-start(s32[2,24,256]{2,1,0:T(8,128)} %get-tuple-element.41.slot_ref) | copy-start | bytes 147460
  33.7 14.4 %copy-start.4 = (f32[24,256]{1,0:T(8,128)S(1)}, f32[24,256]{1,0:T(8,128)}, u32[]{:S(2)}) copy-start(f32[24,256]{1,0:T(8,128)} %start_ref.1) | copy-start | bytes 73732
  33.7 14.4 %all-to-all-start.1 = ((f32[128,2,128]{2,1,0:T(2,128)}), f32[128,2,128]{2,1,0:T(2,128)S(1)}, u32[]{:S(2)}, u32[]{:S(2)}) async-start(f32[128,2,128]{2,1,0:T(2,128)} %bitcast.6), calls=%async_computation.1 | async-start | bytes 262144 | tf_op jit(solution)/shard_map/all_to_all | solution.py:508
  38.0 4.1 %collective-permute-start.4 = (f32[32,512]{1,0:T(8,128)S(1)}, f32[32,512]{1,0:T(8,128)S(1)}, u32[]{:S(2)}, u32[]{:S(2)}) collective-permute-start(f32[32,512]{1,0:T(8,128)S(1)} %get-tuple-element.42), channel_id=1, source_target_pairs={{0,1},{1,0},{2,3},{3,2},{4,5},{5,4},{6,7},{7,6},{8,9},{9,8},{10,11... | collective-permute-start | bytes 196616 | tf_op jit(solution)/shard_map/ppermute | solution.py:496
  39.7 2.4 %collective-permute-start.5 = (f32[32,512]{1,0:T(8,128)S(1)}, f32[32,512]{1,0:T(8,128)S(1)}, u32[]{:S(2)}, u32[]{:S(2)}) collective-permute-start(f32[32,512]{1,0:T(8,128)S(1)} %get-tuple-element.43), channel_id=1, source_target_pairs={{0,16},{1,17},{2,18},{3,19},{4,20},{5,21},{6,22},{7,23},{8,24},{9,... | collective-permute-start | bytes 196616 | tf_op jit(solution)/shard_map/ppermute | solution.py:496
  50.8 14.2 %all-to-all-start.2 = ((f32[128,2,128]{2,1,0:T(2,128)}), f32[128,2,128]{2,1,0:T(2,128)S(1)}, u32[]{:S(2)}, u32[]{:S(2)}) async-start(f32[128,2,128]{2,1,0:T(2,128)} %bitcast.8), calls=%async_computation.2 | async-start | bytes 262144 | tf_op jit(solution)/shard_map/all_to_all | solution.py:508
  55.0 11.4 %collective-permute-start.6 = (f32[16,512]{1,0:T(8,128)S(1)}, f32[16,512]{1,0:T(8,128)S(1)}, u32[]{:S(2)}, u32[]{:S(2)}) collective-permute-start(f32[16,512]{1,0:T(8,128)S(1)} %get-tuple-element.51), channel_id=1, source_target_pairs={{0,16},{1,2},{2,1},{3,4},{4,3},{5,6},{6,5},{7,8},{8,7},{9,10},{10,... | collective-permute-start | bytes 98312 | tf_op jit(solution)/shard_map/ppermute | solution.py:496
  56.2 10.2 %collective-permute-start.7 = (f32[16,512]{1,0:T(8,128)S(1)}, f32[16,512]{1,0:T(8,128)S(1)}, u32[]{:S(2)}, u32[]{:S(2)}) collective-permute-start(f32[16,512]{1,0:T(8,128)S(1)} %get-tuple-element.52), channel_id=1, source_target_pairs={{0,1},{1,0},{2,3},{3,2},{4,5},{5,4},{6,7},{7,6},{8,9},{9,8},{10,11... | collective-permute-start | bytes 98312 | tf_op jit(solution)/shard_map/ppermute | solution.py:496
  68.8 14.5 %all-to-all-start.3 = ((f32[128,2,128]{2,1,0:T(2,128)}), f32[128,2,128]{2,1,0:T(2,128)S(1)}, u32[]{:S(2)}, u32[]{:S(2)}) async-start(f32[128,2,128]{2,1,0:T(2,128)} %bitcast.10), calls=%async_computation.3 | async-start | bytes 262144 | tf_op jit(solution)/shard_map/all_to_all | solution.py:508
  73.2 6.8 %collective-permute-start.8 = (f32[12,512]{1,0:T(8,128)S(1)}, f32[12,512]{1,0:T(8,128)S(1)}, u32[]{:S(2)}, u32[]{:S(2)}) collective-permute-start(f32[12,512]{1,0:T(8,128)S(1)} %get-tuple-element.56), channel_id=1, source_target_pairs={{0,16},{1,2},{2,1},{3,4},{4,3},{5,6},{6,5},{7,8},{8,7},{9,10},{10,... | collective-permute-start | bytes 73736 | tf_op jit(solution)/shard_map/ppermute | solution.py:496
  74.4 5.6 %collective-permute-start.10 = (f32[12,512]{1,0:T(8,128)S(1)}, f32[12,512]{1,0:T(8,128)S(1)}, u32[]{:S(2)}, u32[]{:S(2)}) collective-permute-start(f32[12,512]{1,0:T(8,128)S(1)} %get-tuple-element.58), channel_id=1, source_target_pairs={{0,1},{1,0},{2,3},{3,2},{4,5},{5,4},{6,7},{7,6},{8,9},{9,8},{10,11... | collective-permute-start | bytes 73736 | tf_op jit(solution)/shard_map/ppermute | solution.py:496
  76.3 3.7 %collective-permute-start.9 = (f32[8,512]{1,0:T(8,128)S(1)}, f32[8,512]{1,0:T(8,128)S(1)}, u32[]{:S(2)}, u32[]{:S(2)}) collective-permute-start(f32[8,512]{1,0:T(8,128)S(1)} %get-tuple-element.57), channel_id=1, source_target_pairs={{0,1},{1,0},{2,3},{3,2},{4,5},{5,4},{6,7},{7,6},{8,9},{9,8},{10,11... | collective-permute-start | bytes 49160 | tf_op jit(solution)/shard_map/ppermute | solution.py:496
  78.3 1.7 %collective-permute-start.11 = (f32[8,512]{1,0:T(8,128)S(1)}, f32[8,512]{1,0:T(8,128)S(1)}, u32[]{:S(2)}, u32[]{:S(2)}) collective-permute-start(f32[8,512]{1,0:T(8,128)S(1)} %get-tuple-element.59), channel_id=1, source_target_pairs={{0,16},{1,17},{2,18},{3,19},{4,20},{5,21},{6,22},{7,23},{8,24},{9,... | collective-permute-start | bytes 49160 | tf_op jit(solution)/shard_map/ppermute | solution.py:496

commit v7 on v6

--- a/solution.py
+++ b/solution.py
@@ -20,13 +20,15 @@
 NT = (((1,), (1,)), ((), ()))
 
 
-def call(body, out_shape, n_in, scratch=(), smem=(), remote=(), microseconds=1, vmem=VMEM_LIMIT):
+def call(body, out_shape, n_in, scratch=(), smem=(), remote=(), microseconds=1, vmem=VMEM_LIMIT, early=False):
     def place(i):
         if i in smem:
             return pltpu.SMEM
         return pltpu.HBM if i in remote else pltpu.VMEM
 
     out_specs = jax.tree.map(lambda _: pl.BlockSpec(memory_space=pltpu.VMEM), out_shape)
+    if early:
+        out_specs = (pl.BlockSpec(memory_space=pltpu.HBM),) + tuple(out_specs[1:])
     return pl.pallas_call(
         body,
         out_shape=out_shape,
@@ -117,12 +119,32 @@
     copies = [pltpu.make_async_copy(a, b, arrived.at[i]) for i, (a, b) in enumerate(pairs)]
     for copy in copies:
         copy.start()
-    for copy in copies:
-        copy.wait()
     blocks = start_ref.shape[0]
     size = (blocks, LANES)
     live = lax.broadcasted_iota(I32, size, 0) < count_ref[0]
     lane = lax.broadcasted_iota(I32, size, 1)
+    copies[0].wait()
+    tile = jnp.concatenate(
+        [tile_ref[pl.ds(0, blocks, stride=2), :], tile_ref[pl.ds(1, blocks, stride=2), :]], axis=1
+    )
+    target = jnp.where(live, tile, -1)
+    slot_ref[0] = target
+    upper = jnp.where(
+        lax.broadcasted_iota(I32, (LANES, LANES), 0) <= lax.broadcasted_iota(I32, (LANES, LANES), 1),
+        1.0, 0.0,
+    ).astype(BF16)
+    before = jnp.zeros((128, LANES), F32)
+    for b in range(blocks):
+        mine = hot_rows(slot_ref[0, b : b + 1, :], 128)
+        running = lax.dot_general(mine, upper, NN, preferred_element_type=F32)
+        rank = jnp.sum(mine.astype(F32) * (running + before), axis=0, keepdims=True)
+        before += jnp.broadcast_to(running[:, LANES - 1 :], (128, LANES))
+        slot_ref[1, b : b + 1, :] = rank.astype(I32)
+    rank = jnp.maximum(slot_ref[1] - 1, 0)
+    slot_ref[0] = jnp.where(live, target + (rank & 1) * 128, -1)
+    slot_ref[1] = rank >> 1
+    for copy in copies[1:]:
+        copy.wait()
     start = start_ref[...]
     store = store_ref[...]
     weight = jnp.where(live, weight_ref[...], 0.0)
@@ -146,27 +168,6 @@
     put_split(split, 2, weight * start)
     put_split(split, 3, weight * partial)
     put_split(split, 4, weight * pull)
-    tile = jnp.concatenate(
-        [tile_ref[pl.ds(0, blocks, stride=2), :], tile_ref[pl.ds(1, blocks, stride=2), :]], axis=1
-    )
-    slot_ref[0] = jnp.where(live, tile, -1)
-    upper = jnp.where(
-        lax.broadcasted_iota(I32, (LANES, LANES), 0) <= lax.broadcasted_iota(I32, (LANES, LANES), 1),
-        1.0, 0.0,
-    ).astype(BF16)
-    before = jnp.zeros((128, LANES), F32)
-    for b in range(blocks):
-        target = slot_ref[0, b : b + 1, :]
-        mine = same(target, 128)
-        running = lax.dot_general(
-            jnp.where(mine, 1.0, 0.0).astype(BF16), upper, NN, preferred_element_type=F32
-        )
-        rank = jnp.sum(jnp.where(mine, running + before, 0.0), axis=0, keepdims=True).astype(I32) - 1
-        before += jnp.broadcast_to(running[:, LANES - 1 :], (128, LANES))
-        slot_ref[1, b : b + 1, :] = jnp.maximum(rank, 0)
-    target, rank = slot_ref[0], slot_ref[1]
-    slot_ref[0] = jnp.where(live, target + (rank & 1) * 128, -1)
-    slot_ref[1] = rank >> 1
     total = jnp.zeros((10 * PAD_RANKS, LANES), F32)
     for b in range(blocks):
         total += lax.dot_general(
@@ -343,7 +344,7 @@
 
 
 def tile_first(hits_ref, cells_ref, perm_ref, start_ref, storage_ref, yh, xh, yl, xl,
-               out_ref, next_ref, sums_ref, faces_ref, known_ref, x_a, x_b, found):
+               out_ref, next_ref, sums_ref, faces_ref, known_ref, x_a, x_b, found, stage, left):
     rows, nz = perm_ref.shape
     ny = 8
     perm = perm_ref[...]
@@ -376,6 +377,11 @@
     sums_ref[0] = inverse
     sums_ref[1] = base
     sums_ref[2] = hits_ref[3]
+    found[...] = jnp.zeros_like(found)
+    gather_cells([start, now], cells_ref, found)
+    store_slots(stage, found[...], 0, 1)
+    copy = pltpu.make_async_copy(stage, out_ref, left.at[0])
+    copy.start()
     far, near = jnp.zeros((ny, nz), F32), jnp.zeros((rows // ny, nz), F32)
     within = neighbours(now, far, far, near, near, ny)
     inflow = base + hits_ref[2] + start * hits_ref[3]
@@ -395,9 +401,7 @@
         )
     x_a[...] = pick(odd_x, sides[0], sides[1])
     x_b[...] = pick(odd_x, sides[1], sides[0])
-    found[...] = jnp.zeros_like(found)
-    gather_cells([start, now], cells_ref, found)
-    store_slots(out_ref, found[...], 0, 1)
+    copy.wait()
 
 
 def flow_in(field, faces_ref, xl, xh, yl, yh):
@@ -437,7 +441,7 @@
 
 
 def tile_third(hits_ref, part_ref, before_ref, sums_ref, faces_ref, cells_ref, y_b, y_a, x_b, x_a,
-               out_ref, next_ref, last_ref, a, b, c, d, found):
+               out_ref, next_ref, last_ref, a, b, c, d, found, stage, left):
     odd_x, odd_y = parity()
     x_low, x_high = pick(odd_x, x_a[...], x_b[...]), pick(odd_x, x_b[...], x_a[...])
     y_low, y_high = pick(odd_y, y_a[...], y_b[...]), pick(odd_y, y_b[...], y_a[...])
@@ -464,11 +468,14 @@
         inflow += faces_ref[i] * around[i]
     later = inflow * inverse
     next_ref[...] = later
+    found[...] = jnp.zeros_like(found)
+    gather_cells([now, later], cells_ref, found)
+    store_slots(stage, found[...], 0, 1)
+    copy = pltpu.make_async_copy(stage, out_ref, left.at[0])
+    copy.start()
     put_faces(later, (a, b, c, d))
     last_ref[...] = sums_ref[1] + hits_ref[1] + now * sums_ref[2]
-    found[...] = jnp.zeros_like(found)
-    gather_cells([now, later], cells_ref, found)
-    store_slots(out_ref, found[...], 0, 1)
+    copy.wait()
 
 
 def last_pair(recv_ref, coef_ref, slot_ref, partial_ref, now_ref, last_ref, sums_ref, faces_ref,
@@ -553,7 +560,8 @@
         tile_first,
         (shape(256, 128), field, shape(3, rows, nz), shape(6, rows, nz), field, x_side, x_side),
         9,
-        scratch=[found],
+        scratch=[found, pltpu.VMEM((256, 128), F32), pltpu.SemaphoreType.DMA((1,))],
+        early=True,
         microseconds=4,
     )(sums, cells, perm, start, storage, *around)
     seen = deliver(seen)
@@ -588,7 +596,8 @@
         tile_third,
         (shape(256, 128), field, field) + faces_of(1),
         10,
-        scratch=[found],
+        scratch=[found, pltpu.VMEM((256, 128), F32), pltpu.SemaphoreType.DMA((1,))],
+        early=True,
         microseconds=4,
     )(hits, second, first, sums, faces, cells, *beside_y, *beside_x)
     seen = deliver(seen)

time: 85.2 us -> 85.1 us (level)
  no operation moved by 1% of the time
where the time goes in v7:
time: 85.1 us; the launch traced here: 84.8 us
  starting transfers between devices  39.7 us (47%)
  waiting for transfers between devices  26.3 us (31%)
  Pallas kernels  17.2 us (20%)
  between operations  1.49 us (2%)
    all_to_all x4, starting transfers between devices, deliver(): lax.all_to_all(payload, ('flow', 'cross'), split_axis=0, concat_axis=0, t...  24.5 us
    all_to_all x4, waiting for transfers between devices, deliver(): lax.all_to_all(payload, ('flow', 'cross'), split_axis=0, concat_axis=0, t...  22.8 us
    ppermute x12, starting transfers between devices, trade(): return lax.ppermute(block, ('flow', 'cross'), pairs)  15.2 us
    pallas_call x1, Pallas kernels, on_device(): call(owner_first, (shape(512, 128), shape(5, blocks, LANES), shape(2, blo...  3.99 us
    ppermute x12, waiting for transfers between devices, trade(): return lax.ppermute(block, ('flow', 'cross'), pairs)  3.51 us
    pallas_call x1, Pallas kernels, on_device(): call(tile_scatter, (shape(4, rows, nz), shape(2, PAD_RANKS, LANES, dtype=...  2.72 us
    pallas_call x1, Pallas kernels, on_device(): call(owner_middle, (shape(256, 128), shape(blocks, LANES)), 6, remote=(4,...  2.63 us
    pallas_call x1, Pallas kernels, on_device(): call(tile_first, (shape(256, 128), field, shape(3, rows, nz), shape(6, ro...  2.43 us
  transfers between devices with their start and end apart: 16, of which 6 were waited for; matrix products, arithmetic and copies ran while one was open for 0% of the time, Pallas kernels for 5%

profile of v7, /device:TPU:1, one launch (start us, length us, event | category | flops | bytes accessed | tf_op | source)
XLA Modules:
  0.0 84.8 jit_solution(15010588808062603354)
XLA Ops:
  1.3 4.0 %shard_map.122 = (f32[512,128]{1,0:T(8,128)}, f32[5,24,256]{2,1,0:T(8,128)}, s32[2,24,256]{2,1,0:T(8,128)}) custom-call(s32[1]{0:T(128)S(6)} %copy.13.count_ref, f32[24,256]{1,0:T(8,128)} %start_ref.1, f32[24,256]{1,0:T(8,128)} %store_hbm.1, f32[24,256]{1,0:T(8,128)} %cond_hbm.1, s32[24,256]{1,0:T(8,128)} %seg_hbm.1, s32[48,128]{1,0:T(8,128)} %bitcast.23, ...), custom_call_target="tpu_custom_call" | custom-call | bytes 18000000 | tf_op jit(solution)/shard_map/pallas_call | solution.py:530
  5.3 0.0 copy-start.1
  5.3 0.0 copy-start.2
  5.3 11.5 %all-to-all-start = ((f32[128,4,128]{2,1,0:T(4,128)}), f32[128,4,128]{2,1,0:T(4,128)S(1)}, u32[]{:S(2)}, u32[]{:S(2)}) async-start(f32[128,4,128]{2,1,0:T(4,128)} %bitcast.22), calls=%async_computation | async-start | bytes 524288 | tf_op jit(solution)/shard_map/all_to_all | solution.py:515
  16.8 0.0 copy-done.1
  16.8 0.0 copy-done.2
  16.9 1.1 %collective-permute-start = (f32[16,512]{1,0:T(8,128)S(1)}, f32[16,512]{1,0:T(8,128)S(1)}, u32[]{:S(2)}, u32[]{:S(2)}) collective-permute-start(f32[16,512]{1,0:T(8,128)S(1)} %get-tuple-element.35), channel_id=1, source_target_pairs={{0,16},{1,2},{2,1},{3,4},{4,3},{5,6},{6,5},{7,8},{8,7},{9,10},{10,... | collective-permute-start | bytes 98312 | tf_op jit(solution)/shard_map/ppermute | solution.py:503
  18.0 0.7 collective-permute-start.1
  18.7 2.9 %collective-permute-start.2 = (f32[16,512]{1,0:T(8,128)S(1)}, f32[16,512]{1,0:T(8,128)S(1)}, u32[]{:S(2)}, u32[]{:S(2)}) collective-permute-start(f32[16,512]{1,0:T(8,128)S(1)} %get-tuple-element.37), channel_id=1, source_target_pairs={{0,1},{1,0},{2,3},{3,2},{4,5},{5,4},{6,7},{7,6},{8,9},{9,8},{10,11... | collective-permute-start | bytes 98312 | tf_op jit(solution)/shard_map/ppermute | solution.py:503
  21.6 0.0 collective-permute-start.3
  21.7 6.7 %all-to-all-done = f32[128,4,128]{2,1,0:T(4,128)S(1)} async-done(((f32[128,4,128]{2,1,0:T(4,128)}), f32[128,4,128]{2,1,0:T(4,128)S(1)}, u32[]{:S(2)}, u32[]{:S(2)}) %all-to-all-start) | async-done | bytes 262176 | tf_op jit(solution)/shard_map/all_to_all | solution.py:515
  28.4 2.7 %shard_map.123 = (f32[4,32,512]{2,1,0:T(8,128)S(1)}, s32[2,40,256]{2,1,0:T(8,128)S(1)}) custom-call(f32[512,128]{1,0:T(8,128)S(1)} %bitcast.13), custom_call_target="tpu_custom_call" | custom-call | bytes 12000000 | tf_op jit(solution)/shard_map/pallas_call | solution.py:550
  31.1 0.0 collective-permute-done.yh
  31.1 0.0 collective-permute-done.1.xh
  31.1 0.0 collective-permute-done.2.yl
  31.1 0.0 collective-permute-done.3.xl
  31.1 0.0 copy-done.5
  31.1 2.4 %shard_map.125 = (f32[256,128]{1,0:T(8,128)}, f32[32,512]{1,0:T(8,128)S(1)}, f32[3,32,512]{2,1,0:T(8,128)S(1)}, f32[6,32,512]{2,1,0:T(8,128)S(1)}, f32[32,512]{1...) custom-call(f32[4,32,512]{2,1,0:T(8,128)S(1)} %get-tuple-element.33.hits_ref, ...), custom_call_target="tpu_custom_call" | custom-call | bytes 12000000 | tf_op jit(solution)/shard_map/pallas_call | solution.py:559
  33.6 0.0 copy-start.3
  33.6 0.0 copy-start.4
  33.6 4.3 %all-to-all-start.1 = ((f32[128,2,128]{2,1,0:T(2,128)}), f32[128,2,128]{2,1,0:T(2,128)S(1)}, u32[]{:S(2)}, u32[]{:S(2)}) async-start(f32[128,2,128]{2,1,0:T(2,128)} %bitcast.6), calls=%async_computation.1 | async-start | bytes 262144 | tf_op jit(solution)/shard_map/all_to_all | solution.py:515
  37.9 1.7 %collective-permute-start.4 = (f32[32,512]{1,0:T(8,128)S(1)}, f32[32,512]{1,0:T(8,128)S(1)}, u32[]{:S(2)}, u32[]{:S(2)}) collective-permute-start(f32[32,512]{1,0:T(8,128)S(1)} %get-tuple-element.42), channel_id=1, source_target_pairs={{0,1},{1,0},{2,3},{3,2},{4,5},{5,4},{6,7},{7,6},{8,9},{9,8},{10,11... | collective-permute-start | bytes 196616 | tf_op jit(solution)/shard_map/ppermute | solution.py:503
  39.7 0.6 collective-permute-start.5
  40.3 1.8 %collective-permute-done.4.x_b = f32[32,512]{1,0:T(8,128)S(1)} collective-permute-done((f32[32,512]{1,0:T(8,128)S(1)}, f32[32,512]{1,0:T(8,128)S(1)}, u32[]{:S(2)}, u32[]{:S(2)}) %collective-permute-start.4) | collective-permute-done | bytes 65568 | tf_op jit(solution)/shard_map/ppermute | solution.py:503
  42.1 0.0 collective-permute-done.5.x_a
  42.1 6.0 %all-to-all-done.1 = f32[128,2,128]{2,1,0:T(2,128)S(1)} async-done(((f32[128,2,128]{2,1,0:T(2,128)}), f32[128,2,128]{2,1,0:T(2,128)S(1)}, u32[]{:S(2)}, u32[]{:S(2)}) %all-to-all-start.1) | async-done | bytes 131104 | tf_op jit(solution)/shard_map/all_to_all | solution.py:515
  48.1 0.0 copy-done.3
  48.1 2.6 %shard_map.126 = (f32[256,128]{1,0:T(8,128)}, f32[24,256]{1,0:T(8,128)S(1)}) custom-call(f32[256,128]{1,0:T(8,128)S(1)} %bitcast.15, f32[24,256]{1,0:T(8,128)S(1)} %copy-done.4, f32[5,24,256]{2,1,0:T(8,128)S(1)} %copy-done, s32[2,24,256]{2,1,0:T(8,128)S(1)} %copy-done.3, f32[32,512]{1,0:T(8,128)S(1)} %collective-permute-done.4.x_b, ...), custom_call_target="tpu_custom_call" | custom-call | bytes 15000000 | tf_op jit(solution)/shard_map/pallas_call | solution.py:570
  50.7 4.2 %all-to-all-start.2 = ((f32[128,2,128]{2,1,0:T(2,128)}), f32[128,2,128]{2,1,0:T(2,128)S(1)}, u32[]{:S(2)}, u32[]{:S(2)}) async-start(f32[128,2,128]{2,1,0:T(2,128)} %bitcast.8), calls=%async_computation.2 | async-start | bytes 262144 | tf_op jit(solution)/shard_map/all_to_all | solution.py:515
  54.9 0.1 shard_map.128
  55.0 1.2 %collective-permute-start.6 = (f32[16,512]{1,0:T(8,128)S(1)}, f32[16,512]{1,0:T(8,128)S(1)}, u32[]{:S(2)}, u32[]{:S(2)}) collective-permute-start(f32[16,512]{1,0:T(8,128)S(1)} %get-tuple-element.51), channel_id=1, source_target_pairs={{0,16},{1,2},{2,1},{3,4},{4,3},{5,6},{6,5},{7,8},{8,7},{9,10},{10,... | collective-permute-start | bytes 98312 | tf_op jit(solution)/shard_map/ppermute | solution.py:503
  56.1 1.9 %collective-permute-start.7 = (f32[16,512]{1,0:T(8,128)S(1)}, f32[16,512]{1,0:T(8,128)S(1)}, u32[]{:S(2)}, u32[]{:S(2)}) collective-permute-start(f32[16,512]{1,0:T(8,128)S(1)} %get-tuple-element.52), channel_id=1, source_target_pairs={{0,1},{1,0},{2,3},{3,2},{4,5},{5,4},{6,7},{7,6},{8,9},{9,8},{10,11... | collective-permute-start | bytes 98312 | tf_op jit(solution)/shard_map/ppermute | solution.py:503
  58.0 6.9 %all-to-all-done.2 = f32[128,2,128]{2,1,0:T(2,128)S(1)} async-done(((f32[128,2,128]{2,1,0:T(2,128)}), f32[128,2,128]{2,1,0:T(2,128)S(1)}, u32[]{:S(2)}, u32[]{:S(2)}) %all-to-all-start.2) | async-done | bytes 131104 | tf_op jit(solution)/shard_map/all_to_all | solution.py:515
  64.9 1.4 %shard_map.127.hits_ref = f32[2,32,512]{2,1,0:T(8,128)S(1)} custom-call(f32[256,128]{1,0:T(8,128)S(1)} %bitcast.16, s32[2,40,256]{2,1,0:T(8,128)S(1)} %get-tuple-element.34.cells_ref), custom_call_target="tpu_custom_call" | custom-call | bytes 9000000 | tf_op jit(solution)/shard_map/pallas_call | solution.py:588
  66.4 0.0 collective-permute-done.6.y_b
  66.4 0.0 collective-permute-done.7.y_a
  66.4 2.3 %shard_map.129 = (f32[256,128]{1,0:T(8,128)}, f32[32,512]{1,0:T(8,128)S(1)}, f32[32,512]{1,0:T(8,128)S(1)}, f32[8,512]{1,0:T(8,128)S(1)}, f32[8,512]{1,0:T(8,128...) custom-call(f32[2,32,512]{2,1,0:T(8,128)S(1)} %shard_map.127.hits_ref, f32[32,512]{1,0:T(8,128)S(1)} %get-tuple-element.50.part_ref, ...), custom_call_target="tpu_custom_call" | custom-call | bytes 12000000 | tf_op jit(solution)/shard_map/pallas_call | solution.py:595
  68.7 4.4 %all-to-all-start.3 = ((f32[128,2,128]{2,1,0:T(2,128)}), f32[128,2,128]{2,1,0:T(2,128)S(1)}, u32[]{:S(2)}, u32[]{:S(2)}) async-start(f32[128,2,128]{2,1,0:T(2,128)} %bitcast.10), calls=%async_computation.3 | async-start | bytes 262144 | tf_op jit(solution)/shard_map/all_to_all | solution.py:515
  73.2 1.1 %collective-permute-start.8 = (f32[12,512]{1,0:T(8,128)S(1)}, f32[12,512]{1,0:T(8,128)S(1)}, u32[]{:S(2)}, u32[]{:S(2)}) collective-permute-start(f32[12,512]{1,0:T(8,128)S(1)} %get-tuple-element.56), channel_id=1, source_target_pairs={{0,16},{1,2},{2,1},{3,4},{4,3},{5,6},{6,5},{7,8},{8,7},{9,10},{10,... | collective-permute-start | bytes 73736 | tf_op jit(solution)/shard_map/ppermute | solution.py:503
  74.3 1.9 %collective-permute-start.10 = (f32[12,512]{1,0:T(8,128)S(1)}, f32[12,512]{1,0:T(8,128)S(1)}, u32[]{:S(2)}, u32[]{:S(2)}) collective-permute-start(f32[12,512]{1,0:T(8,128)S(1)} %get-tuple-element.58), channel_id=1, source_target_pairs={{0,1},{1,0},{2,3},{3,2},{4,5},{5,4},{6,7},{7,6},{8,9},{9,8},{10,11... | collective-permute-start | bytes 73736 | tf_op jit(solution)/shard_map/ppermute | solution.py:503
  76.2 2.0 %collective-permute-start.9 = (f32[8,512]{1,0:T(8,128)S(1)}, f32[8,512]{1,0:T(8,128)S(1)}, u32[]{:S(2)}, u32[]{:S(2)}) collective-permute-start(f32[8,512]{1,0:T(8,128)S(1)} %get-tuple-element.57), channel_id=1, source_target_pairs={{0,1},{1,0},{2,3},{3,2},{4,5},{5,4},{6,7},{7,6},{8,9},{9,8},{10,11... | collective-permute-start | bytes 49160 | tf_op jit(solution)/shard_map/ppermute | solution.py:503
  78.2 0.0 collective-permute-start.11
  78.2 1.7 %collective-permute-done.9.xh = f32[8,512]{1,0:T(8,128)S(1)} collective-permute-done((f32[8,512]{1,0:T(8,128)S(1)}, f32[8,512]{1,0:T(8,128)S(1)}, u32[]{:S(2)}, u32[]{:S(2)}) %collective-permute-start.9) | collective-permute-done | bytes 16416 | tf_op jit(solution)/shard_map/ppermute | solution.py:503
  79.9 0.0 collective-permute-done.11.xl
  79.9 0.0 collective-permute-done.8.yh
  79.9 0.0 collective-permute-done.10.yl
  80.0 3.2 %all-to-all-done.3 = f32[128,2,128]{2,1,0:T(2,128)S(1)} async-done(((f32[128,2,128]{2,1,0:T(2,128)}), f32[128,2,128]{2,1,0:T(2,128)S(1)}, u32[]{:S(2)}, u32[]{:S(2)}) %all-to-all-start.3) | async-done | bytes 131104 | tf_op jit(solution)/shard_map/all_to_all | solution.py:515
  83.2 1.6 %shard_map.130 = (f32[24,256]{1,0:T(8,128)}, f32[32,512]{1,0:T(8,128)}) custom-call(f32[256,128]{1,0:T(8,128)S(1)} %bitcast.14, f32[5,24,256]{2,1,0:T(8,128)S(1)} %copy-done, s32[2,24,256]{2,1,0:T(8,128)S(1)} %copy-done.3, f32[24,256]{1,0:T(8,128)S(1)} %get-tuple-element.49.after.partial_ref, f32[32,512]{1,0:T(8,128)S(1)} %get-tuple-element.54.now_ref, ...), custom_call_target="tpu_custom_call" | custom-call | bytes 12000000 | tf_op jit(solution)/shard_map/pallas_call | solution.py:605
  (5 shorter events, 0.0 us)
Async XLA Ops:
  5.3 11.6 %copy-start.1 = (f32[4,8,512]{2,1,0:T(8,128)S(1)}, f32[4,8,512]{2,1,0:T(8,128)}, u32[]{:S(2)}) copy-start(f32[4,8,512]{2,1,0:T(8,128)} %param.13) | copy-start | bytes 196612
  5.3 11.5 %copy-start.2 = (f32[4,8,512]{2,1,0:T(8,128)S(1)}, f32[4,8,512]{2,1,0:T(8,128)}, u32[]{:S(2)}) copy-start(f32[4,8,512]{2,1,0:T(8,128)} %param.11) | copy-start | bytes 196612
  5.3 23.1 %all-to-all-start = ((f32[128,4,128]{2,1,0:T(4,128)}), f32[128,4,128]{2,1,0:T(4,128)S(1)}, u32[]{:S(2)}, u32[]{:S(2)}) async-start(f32[128,4,128]{2,1,0:T(4,128)} %bitcast.22), calls=%async_computation | async-start | bytes 524288 | tf_op jit(solution)/shard_map/all_to_all | solution.py:515
  16.9 14.2 %collective-permute-start = (f32[16,512]{1,0:T(8,128)S(1)}, f32[16,512]{1,0:T(8,128)S(1)}, u32[]{:S(2)}, u32[]{:S(2)}) collective-permute-start(f32[16,512]{1,0:T(8,128)S(1)} %get-tuple-element.35), channel_id=1, source_target_pairs={{0,16},{1,2},{2,1},{3,4},{4,3},{5,6},{6,5},{7,8},{8,7},{9,10},{10,... | collective-permute-start | bytes 98312 | tf_op jit(solution)/shard_map/ppermute | solution.py:503
  18.0 13.1 %collective-permute-start.1 = (f32[16,512]{1,0:T(8,128)S(1)}, f32[16,512]{1,0:T(8,128)S(1)}, u32[]{:S(2)}, u32[]{:S(2)}) collective-permute-start(f32[16,512]{1,0:T(8,128)S(1)} %get-tuple-element.36), channel_id=1, source_target_pairs={{0,1},{1,0},{2,3},{3,2},{4,5},{5,4},{6,7},{7,6},{8,9},{9,8},{10,11... | collective-permute-start | bytes 98312 | tf_op jit(solution)/shard_map/ppermute | solution.py:503
  18.7 12.4 %collective-permute-start.2 = (f32[16,512]{1,0:T(8,128)S(1)}, f32[16,512]{1,0:T(8,128)S(1)}, u32[]{:S(2)}, u32[]{:S(2)}) collective-permute-start(f32[16,512]{1,0:T(8,128)S(1)} %get-tuple-element.37), channel_id=1, source_target_pairs={{0,1},{1,0},{2,3},{3,2},{4,5},{5,4},{6,7},{7,6},{8,9},{9,8},{10,11... | collective-permute-start | bytes 98312 | tf_op jit(solution)/shard_map/ppermute | solution.py:503
  21.6 9.5 %collective-permute-start.3 = (f32[16,512]{1,0:T(8,128)S(1)}, f32[16,512]{1,0:T(8,128)S(1)}, u32[]{:S(2)}, u32[]{:S(2)}) collective-permute-start(f32[16,512]{1,0:T(8,128)S(1)} %get-tuple-element.38), channel_id=1, source_target_pairs={{0,16},{1,17},{2,18},{3,19},{4,20},{5,21},{6,22},{7,23},{8,24},{9,... | collective-permute-start | bytes 98312 | tf_op jit(solution)/shard_map/ppermute | solution.py:503
  28.4 2.8 %copy-start.5 = (f32[4,8,512]{2,1,0:T(8,128)S(1)}, f32[4,8,512]{2,1,0:T(8,128)}, u32[]{:S(2)}) copy-start(f32[4,8,512]{2,1,0:T(8,128)} %param.12) | copy-start | bytes 196612
  33.6 14.5 %copy-start = (f32[5,24,256]{2,1,0:T(8,128)S(1)}, f32[5,24,256]{2,1,0:T(8,128)}, u32[]{:S(2)}) copy-start(f32[5,24,256]{2,1,0:T(8,128)} %get-tuple-element.40.coef_ref) | copy-start | bytes 368644
  33.6 14.5 %copy-start.3 = (s32[2,24,256]{2,1,0:T(8,128)S(1)}, s32[2,24,256]{2,1,0:T(8,128)}, u32[]{:S(2)}) copy-start(s32[2,24,256]{2,1,0:T(8,128)} %get-tuple-element.41.slot_ref) | copy-start | bytes 147460
  33.6 14.5 %copy-start.4 = (f32[24,256]{1,0:T(8,128)S(1)}, f32[24,256]{1,0:T(8,128)}, u32[]{:S(2)}) copy-start(f32[24,256]{1,0:T(8,128)} %start_ref.1) | copy-start | bytes 73732
  33.6 14.5 %all-to-all-start.1 = ((f32[128,2,128]{2,1,0:T(2,128)}), f32[128,2,128]{2,1,0:T(2,128)S(1)}, u32[]{:S(2)}, u32[]{:S(2)}) async-start(f32[128,2,128]{2,1,0:T(2,128)} %bitcast.6), calls=%async_computation.1 | async-start | bytes 262144 | tf_op jit(solution)/shard_map/all_to_all | solution.py:515
  37.9 4.1 %collective-permute-start.4 = (f32[32,512]{1,0:T(8,128)S(1)}, f32[32,512]{1,0:T(8,128)S(1)}, u32[]{:S(2)}, u32[]{:S(2)}) collective-permute-start(f32[32,512]{1,0:T(8,128)S(1)} %get-tuple-element.42), channel_id=1, source_target_pairs={{0,1},{1,0},{2,3},{3,2},{4,5},{5,4},{6,7},{7,6},{8,9},{9,8},{10,11... | collective-permute-start | bytes 196616 | tf_op jit(solution)/shard_map/ppermute | solution.py:503
  39.7 2.4 %collective-permute-start.5 = (f32[32,512]{1,0:T(8,128)S(1)}, f32[32,512]{1,0:T(8,128)S(1)}, u32[]{:S(2)}, u32[]{:S(2)}) collective-permute-start(f32[32,512]{1,0:T(8,128)S(1)} %get-tuple-element.43), channel_id=1, source_target_pairs={{0,16},{1,17},{2,18},{3,19},{4,20},{5,21},{6,22},{7,23},{8,24},{9,... | collective-permute-start | bytes 196616 | tf_op jit(solution)/shard_map/ppermute | solution.py:503
  50.7 14.2 %all-to-all-start.2 = ((f32[128,2,128]{2,1,0:T(2,128)}), f32[128,2,128]{2,1,0:T(2,128)S(1)}, u32[]{:S(2)}, u32[]{:S(2)}) async-start(f32[128,2,128]{2,1,0:T(2,128)} %bitcast.8), calls=%async_computation.2 | async-start | bytes 262144 | tf_op jit(solution)/shard_map/all_to_all | solution.py:515
  55.0 11.4 %collective-permute-start.6 = (f32[16,512]{1,0:T(8,128)S(1)}, f32[16,512]{1,0:T(8,128)S(1)}, u32[]{:S(2)}, u32[]{:S(2)}) collective-permute-start(f32[16,512]{1,0:T(8,128)S(1)} %get-tuple-element.51), channel_id=1, source_target_pairs={{0,16},{1,2},{2,1},{3,4},{4,3},{5,6},{6,5},{7,8},{8,7},{9,10},{10,... | collective-permute-start | bytes 98312 | tf_op jit(solution)/shard_map/ppermute | solution.py:503
  56.1 10.2 %collective-permute-start.7 = (f32[16,512]{1,0:T(8,128)S(1)}, f32[16,512]{1,0:T(8,128)S(1)}, u32[]{:S(2)}, u32[]{:S(2)}) collective-permute-start(f32[16,512]{1,0:T(8,128)S(1)} %get-tuple-element.52), channel_id=1, source_target_pairs={{0,1},{1,0},{2,3},{3,2},{4,5},{5,4},{6,7},{7,6},{8,9},{9,8},{10,11... | collective-permute-start | bytes 98312 | tf_op jit(solution)/shard_map/ppermute | solution.py:503
  68.7 14.5 %all-to-all-start.3 = ((f32[128,2,128]{2,1,0:T(2,128)}), f32[128,2,128]{2,1,0:T(2,128)S(1)}, u32[]{:S(2)}, u32[]{:S(2)}) async-start(f32[128,2,128]{2,1,0:T(2,128)} %bitcast.10), calls=%async_computation.3 | async-start | bytes 262144 | tf_op jit(solution)/shard_map/all_to_all | solution.py:515
  73.2 6.8 %collective-permute-start.8 = (f32[12,512]{1,0:T(8,128)S(1)}, f32[12,512]{1,0:T(8,128)S(1)}, u32[]{:S(2)}, u32[]{:S(2)}) collective-permute-start(f32[12,512]{1,0:T(8,128)S(1)} %get-tuple-element.56), channel_id=1, source_target_pairs={{0,16},{1,2},{2,1},{3,4},{4,3},{5,6},{6,5},{7,8},{8,7},{9,10},{10,... | collective-permute-start | bytes 73736 | tf_op jit(solution)/shard_map/ppermute | solution.py:503
  74.3 5.6 %collective-permute-start.10 = (f32[12,512]{1,0:T(8,128)S(1)}, f32[12,512]{1,0:T(8,128)S(1)}, u32[]{:S(2)}, u32[]{:S(2)}) collective-permute-start(f32[12,512]{1,0:T(8,128)S(1)} %get-tuple-element.58), channel_id=1, source_target_pairs={{0,1},{1,0},{2,3},{3,2},{4,5},{5,4},{6,7},{7,6},{8,9},{9,8},{10,11... | collective-permute-start | bytes 73736 | tf_op jit(solution)/shard_map/ppermute | solution.py:503
  76.2 3.7 %collective-permute-start.9 = (f32[8,512]{1,0:T(8,128)S(1)}, f32[8,512]{1,0:T(8,128)S(1)}, u32[]{:S(2)}, u32[]{:S(2)}) collective-permute-start(f32[8,512]{1,0:T(8,128)S(1)} %get-tuple-element.57), channel_id=1, source_target_pairs={{0,1},{1,0},{2,3},{3,2},{4,5},{5,4},{6,7},{7,6},{8,9},{9,8},{10,11... | collective-permute-start | bytes 49160 | tf_op jit(solution)/shard_map/ppermute | solution.py:503
  78.2 1.7 %collective-permute-start.11 = (f32[8,512]{1,0:T(8,128)S(1)}, f32[8,512]{1,0:T(8,128)S(1)}, u32[]{:S(2)}, u32[]{:S(2)}) collective-permute-start(f32[8,512]{1,0:T(8,128)S(1)} %get-tuple-element.59), channel_id=1, source_target_pairs={{0,16},{1,17},{2,18},{3,19},{4,20},{5,21},{6,22},{7,23},{8,24},{9,... | collective-permute-start | bytes 49160 | tf_op jit(solution)/shard_map/ppermute | solution.py:503
